TPU v7x, 32 devices: a whole 2x2x4 slice. The times are simulated.
32 devices in a mesh: section: 2 (over core), dp: 8 (over z, y), tensor: 2 (over x).
Axes of the slice: x: 2, y: 2, z: 4, core: 2. Of those that a mesh axis runs over, the one named last changes fastest.
Arguments:
- tokens: bfloat16 [2, 4096, 1024], P(None, ('dp', 'tensor')), may hold values from -6 to 6
- lengths: int32 [8, 2, 25], P('dp'), may hold values from 1 to 60, 512 in all within a row
- w_qkv: bfloat16 [2, 1024, 3, 1024], P('section', None, None, 'tensor'), may hold values from -0.1875 to 0.1875
- w_out: bfloat16 [2, 1024, 1024], P('section', 'tensor'), may hold values from -0.5 to 0.5
- w_up: bfloat16 [2, 1024, 2048], P('section', None, 'tensor'), may hold values from -0.1875 to 0.1875
- w_down: bfloat16 [2, 2048, 1024], P('section', 'tensor'), may hold values from -0.1875 to 0.1875
- norm_gain: float32 [2, 2, 1024], P('section'), may hold values from 0.25 to 1.75
- norm_bias: float32 [2, 2, 1024], P('section'), may hold values from -1.5 to 1.5
- cotangent: bfloat16 [2, 4096, 1024], P(None, ('dp', 'tensor')), may hold values from -6 to 6
Outputs:
- layer_outputs: bfloat16 [2, 2, 4096, 1024], P('section', None, ('dp', 'tensor'))
- grad_inputs: bfloat16 [2, 2, 4096, 1024], P('section', None, ('dp', 'tensor'))
- grad_qkv: float32 [2, 1024, 3, 1024], P('section', None, None, 'tensor')
- grad_out: float32 [2, 1024, 1024], P('section', 'tensor')
- grad_up: float32 [2, 1024, 2048], P('section', None, 'tensor')
- grad_down: float32 [2, 2048, 1024], P('section', 'tensor')
- grad_gain: float32 [2, 2, 1024], P('section', None, 'tensor')
- grad_bias: float32 [2, 2, 1024], P('section', None, 'tensor')
Inputs may be any that keep to these rules, and one draw needn't show every extreme that they name: Each row along the last dimension lists in order the lengths of the 25 series packed into the 512 tokens of one micro-batch of one data rank; each row sums to 512 and its longest entry is exactly 60.
All inputs are finite; a program needn't handle non-finite values.
Results may differ from a plain program's by a relative error of at most 0.025.
Values may be sent and summed in bfloat16 or wider, within the bound.
No kernel may reach another device: no remote copies, remote signals or barrier semaphores. Data moves between devices by JAX's collectives and lax.ppermute only.
A program may use at most 128 MiB of HBM per device.

v0:
```python
import jax
import jax.numpy as jnp
from jax import lax
from jax.sharding import PartitionSpec as P

HEAD_DIM = 128


epsilon = 1e-05
masked_score = -1e30


def shifted(block, axis, distance):
    devices = range(lax.axis_size(axis))
    route = [(i - distance, i) for i in devices if i - distance in devices]
    return lax.ppermute(block, axis, route)


def segment_ids(series_lengths, row_count):
    series_ends = jnp.cumsum(series_lengths)
    places = jnp.arange(row_count, dtype=jnp.int32)
    return jnp.sum((places[:, None] >= series_ends[None, :]).astype(jnp.int32), axis=1)


def allowed_pairs(series_lengths, row_count):
    segment = segment_ids(series_lengths, row_count)
    places = jnp.arange(row_count, dtype=jnp.int32)
    return (segment[:, None] == segment[None, :]) & (places[None, :] <= places[:, None])


def normalize(values, gain_row, bias_row):
    centre = values - jnp.mean(values, axis=-1, keepdims=True)
    spread = jnp.mean(centre * centre, axis=-1, keepdims=True)
    scale_rows = lax.rsqrt(spread + epsilon)
    unit_rows = centre * scale_rows
    return (unit_rows * gain_row + bias_row, unit_rows, scale_rows)


def normalize_back(incoming, unit_rows, scale_rows, gain_row):
    scaled = incoming * gain_row
    inner_part = (
        scaled
        - jnp.mean(scaled, axis=-1, keepdims=True)
        - unit_rows * jnp.mean(scaled * unit_rows, axis=-1, keepdims=True)
    )
    return (
        scale_rows * inner_part,
        jnp.sum(incoming * unit_rows, axis=0),
        jnp.sum(incoming, axis=0),
    )


def gather_tokens(shard):
    return lax.all_gather(shard, "tensor", axis=0, tiled=True)


def gather_grads(shard):
    return lax.all_gather(shard, "tensor", axis=0, tiled=True)


def sum_partials(term_rows):
    return lax.psum_scatter(
        term_rows.astype(jnp.bfloat16), "tensor", scatter_dimension=0, tiled=True
    ).astype(jnp.float32)


def sum_grad_partials(term_rows):
    return lax.psum_scatter(
        term_rows.astype(jnp.bfloat16), "tensor", scatter_dimension=0, tiled=True
    ).astype(jnp.float32)


def score_rows(query_rows, key_rows, allowed):
    scores = jnp.einsum(
        "thd,shd->hts", query_rows, key_rows, preferred_element_type=jnp.float32
    ) * HEAD_DIM ** (-0.5)
    return jnp.where(allowed[None], scores, masked_score)


def layer_forward(layer_input, weights, allowed):
    w_qkv, w_out, w_up, w_down, norm_gain, norm_bias = weights
    model_width = w_qkv.shape[0]
    local_width = w_qkv.shape[2]
    local_heads = local_width // HEAD_DIM
    first_norm, unit_one, scale_one = normalize(layer_input, norm_gain[0], norm_bias[0])
    first_low = first_norm.astype(jnp.bfloat16)
    gathered_one = gather_tokens(first_low)
    row_count = gathered_one.shape[0]
    qkv_rows = jnp.dot(
        gathered_one,
        w_qkv.reshape(model_width, 3 * local_width),
        preferred_element_type=jnp.float32,
    )
    qkv_rows = qkv_rows.astype(jnp.bfloat16).reshape(row_count, 3, local_heads, HEAD_DIM)
    scores = score_rows(qkv_rows[:, 0], qkv_rows[:, 1], allowed)
    row_peak = jnp.max(scores, axis=-1, keepdims=True)
    expo_rows = jnp.exp(scores - row_peak)
    row_total = jnp.sum(expo_rows, axis=-1, keepdims=True)
    attention_probs = expo_rows / row_total
    log_total = row_peak + jnp.log(row_total)
    heads_out = jnp.einsum(
        "hts,shd->thd",
        attention_probs.astype(jnp.bfloat16),
        qkv_rows[:, 2],
        preferred_element_type=jnp.float32,
    )
    heads_out = heads_out.reshape(row_count, local_width).astype(jnp.bfloat16)
    mixed_rows = layer_input + sum_partials(
        jnp.dot(heads_out, w_out, preferred_element_type=jnp.float32)
    )
    second_norm, unit_two, scale_two = normalize(mixed_rows, norm_gain[1], norm_bias[1])
    second_low = second_norm.astype(jnp.bfloat16)
    gathered_two = gather_tokens(second_low)
    pre_act = jnp.dot(gathered_two, w_up, preferred_element_type=jnp.float32)
    hidden_rows = jax.nn.gelu(pre_act).astype(jnp.bfloat16)
    layer_output = mixed_rows + sum_partials(
        jnp.dot(hidden_rows, w_down, preferred_element_type=jnp.float32)
    )
    saved = (
        unit_one,
        scale_one,
        unit_two,
        scale_two,
        first_low,
        second_low,
        gathered_one,
        gathered_two,
        qkv_rows,
        log_total,
        heads_out,
        pre_act,
    )
    return (layer_output.astype(jnp.bfloat16), saved)


def layer_backward(incoming, saved, weights, allowed):
    w_qkv, w_out, w_up, w_down, norm_gain, norm_bias = weights
    (
        unit_one,
        scale_one,
        unit_two,
        scale_two,
        first_low,
        second_low,
        gathered_one,
        gathered_two,
        qkv_rows,
        log_total,
        heads_out,
        pre_act,
    ) = saved
    model_width = w_qkv.shape[0]
    local_width = w_qkv.shape[2]
    local_heads = local_width // HEAD_DIM
    row_count = qkv_rows.shape[0]
    gathered_grad = gather_grads(incoming.astype(jnp.bfloat16))
    hidden_grad = jnp.einsum("td,fd->tf", gathered_grad, w_down, preferred_element_type=jnp.float32)
    hidden_rows, gelu_pull = jax.vjp(jax.nn.gelu, pre_act)
    pre_grad = gelu_pull(hidden_grad)[0].astype(jnp.bfloat16)
    grad_down = jnp.einsum(
        "tf,td->fd",
        hidden_rows.astype(jnp.bfloat16),
        gathered_grad,
        preferred_element_type=jnp.float32,
    )
    grad_up = jnp.einsum("td,tf->df", gathered_two, pre_grad, preferred_element_type=jnp.float32)
    norm_grad_two = sum_grad_partials(
        jnp.einsum("tf,df->td", pre_grad, w_up, preferred_element_type=jnp.float32)
    )
    back_two, gain_two, bias_two = normalize_back(norm_grad_two, unit_two, scale_two, norm_gain[1])
    mixed_grad = incoming + back_two
    gathered_mixed = gather_grads(mixed_grad.astype(jnp.bfloat16))
    heads_grad = jnp.einsum(
        "td,kd->tk", gathered_mixed, w_out, preferred_element_type=jnp.float32
    ).astype(jnp.bfloat16)
    grad_out = jnp.einsum(
        "tk,td->kd", heads_out, gathered_mixed, preferred_element_type=jnp.float32
    )
    heads_grad = heads_grad.reshape(row_count, local_heads, HEAD_DIM)
    query_rows, key_rows, value_rows = (qkv_rows[:, 0], qkv_rows[:, 1], qkv_rows[:, 2])
    attention_probs = jnp.exp(score_rows(query_rows, key_rows, allowed) - log_total)
    prob_grad = jnp.einsum(
        "thd,shd->hts", heads_grad, value_rows, preferred_element_type=jnp.float32
    )
    value_grad = jnp.einsum(
        "hts,thd->shd",
        attention_probs.astype(jnp.bfloat16),
        heads_grad,
        preferred_element_type=jnp.float32,
    ).astype(jnp.bfloat16)
    row_inner = jnp.sum(attention_probs * prob_grad, axis=-1, keepdims=True)
    score_grad = (attention_probs * (prob_grad - row_inner) * HEAD_DIM ** (-0.5)).astype(
        jnp.bfloat16
    )
    query_grad = jnp.einsum(
        "hts,shd->thd", score_grad, key_rows, preferred_element_type=jnp.float32
    ).astype(jnp.bfloat16)
    key_grad = jnp.einsum(
        "hts,thd->shd", score_grad, query_rows, preferred_element_type=jnp.float32
    ).astype(jnp.bfloat16)
    qkv_grad = jnp.stack([query_grad, key_grad, value_grad], axis=1).reshape(
        row_count, 3 * local_width
    )
    grad_qkv = jnp.einsum("td,tk->dk", gathered_one, qkv_grad, preferred_element_type=jnp.float32)
    grad_qkv = grad_qkv.reshape(model_width, 3, local_width)
    norm_grad_one = sum_grad_partials(
        jnp.einsum(
            "tk,dk->td",
            qkv_grad,
            w_qkv.reshape(model_width, 3 * local_width),
            preferred_element_type=jnp.float32,
        )
    )
    back_one, gain_one, bias_one = normalize_back(norm_grad_one, unit_one, scale_one, norm_gain[0])
    input_grad = mixed_grad + back_one
    norm_part = jnp.stack([gain_one, gain_two, bias_one, bias_two])
    return (input_grad, (grad_qkv, grad_out, grad_up, grad_down, norm_part))


def per_device(tokens, lengths, w_qkv, w_out, w_up, w_down, norm_gain, norm_bias, cotangent):
    first_section = lax.axis_index("section") == 0
    micro_count = tokens.shape[0]
    row_count = tokens.shape[1] * lax.axis_size("tensor")
    weights = (w_qkv[0], w_out[0], w_up[0], w_down[0], norm_gain[0], norm_bias[0])
    mask_list = [allowed_pairs(lengths[0, micro], row_count) for micro in range(micro_count)]
    zero_rows = jnp.zeros_like(tokens[0])
    arriving = zero_rows
    forward_out = []
    kept = []
    for turn_index in range(micro_count + 1):
        fresh_rows = tokens[turn_index] if turn_index < micro_count else zero_rows
        layer_input = jnp.where(first_section, fresh_rows, arriving).astype(jnp.float32)
        allowed = jnp.where(
            first_section,
            mask_list[min(turn_index, micro_count - 1)],
            mask_list[max(turn_index - 1, 0)],
        )
        layer_output, saved = layer_forward(layer_input, weights, allowed)
        forward_out.append(layer_output)
        kept.append(saved)
        if turn_index < micro_count:
            arriving = shifted(layer_output, "section", 1)
    returning = zero_rows
    backward_out = []
    running = None
    for turn_index in range(micro_count + 1):
        early_turn = max(turn_index - 1, 0)
        late_turn = min(turn_index + 1, micro_count)
        saved = jax.tree.map(
            lambda early_leaf, late_leaf: jnp.where(first_section, early_leaf, late_leaf),
            kept[early_turn],
            kept[late_turn],
        )
        allowed = jnp.where(
            first_section, mask_list[early_turn], mask_list[min(turn_index, micro_count - 1)]
        )
        outer_grad = cotangent[turn_index] if turn_index < micro_count else zero_rows
        incoming = jnp.where(first_section, returning, outer_grad).astype(jnp.float32)
        valid_turn = jnp.where(first_section, turn_index >= 1, turn_index < micro_count)
        input_grad, pieces = layer_backward(incoming, saved, weights, allowed)
        low_grad = input_grad.astype(jnp.bfloat16)
        backward_out.append(low_grad)
        if turn_index < micro_count:
            returning = shifted(low_grad, "section", -1)
        pieces = jax.tree.map(lambda leaf: jnp.where(valid_turn, leaf, 0.0), pieces)
        running = pieces if running is None else jax.tree.map(jnp.add, running, pieces)
    part_qkv, part_out, part_up, part_down, part_norm = running
    norm_local = lax.psum_scatter(part_norm, "tensor", scatter_dimension=1, tiled=True)
    summed = lax.psum((part_qkv, part_out, part_up, part_down, norm_local), "dp")
    total_qkv, total_out, total_up, total_down, total_norm = summed
    layer_outputs = jnp.stack(
        [
            jnp.where(first_section, forward_out[micro], forward_out[micro + 1])
            for micro in range(micro_count)
        ]
    )[None]
    grad_inputs = jnp.stack(
        [
            jnp.where(first_section, backward_out[micro + 1], backward_out[micro])
            for micro in range(micro_count)
        ]
    )[None]
    return (
        layer_outputs,
        grad_inputs,
        total_qkv[None],
        total_out[None],
        total_up[None],
        total_down[None],
        total_norm[None, :2],
        total_norm[None, 2:],
    )


def solution(mesh):
    in_specs = (
        P(None, ("dp", "tensor"), None),
        P("dp", None, None),
        P("section", None, None, "tensor"),
        P("section", "tensor", None),
        P("section", None, "tensor"),
        P("section", "tensor", None),
        P("section", None, None),
        P("section", None, None),
        P(None, ("dp", "tensor"), None),
    )
    out_specs = (
        P("section", None, ("dp", "tensor"), None),
        P("section", None, ("dp", "tensor"), None),
        P("section", None, None, "tensor"),
        P("section", "tensor", None),
        P("section", None, "tensor"),
        P("section", "tensor", None),
        P("section", None, "tensor"),
        P("section", None, "tensor"),
    )
    return jax.shard_map(
        per_device, mesh=mesh, in_specs=in_specs, out_specs=out_specs, check_vma=False
    )
```

profile of v0, /device:TPU:0, one launch (start us, length us, event | category | flops | bytes accessed | tf_op | source)
XLA Modules:
  0.0 1298.6 jit_solution(14293131668818184564)
XLA Ops:
  14.2 4.6 copy.142
  20.3 17.5 %all-gather.14.cloned.1.call-done = bf16[512,1024]{1,0:T(8,128)(2,1)} async-done(((bf16[256,1024]{1,0:T(8,128)(2,1)}), bf16[512,1024]{1,0:T(8,128)(2,1)}) %all-gather.14.cloned.1.call-update) | async-done | bytes 1048592 | tf_op jit(solution)/shard_map/all_gather | solution.py:54
  37.7 5.2 convolution_convert_fusion.2
  58.1 20.4 %reduce-scatter.16.cloned.1.call-done = bf16[256,1024]{1,0:T(8,128)(2,1)} async-done(((bf16[512,1024]{1,0:T(8,128)(2,1)}), bf16[256,1024]{1,0:T(8,128)(2,1)}) %reduce-scatter.16.cloned.1.call-update) | async-done | bytes 524304 | tf_op jit(solution)/shard_map/reduce_scatter | solution.py:62
  82.4 21.4 %all-gather.16.cloned.1.call-done = bf16[512,1024]{1,0:T(8,128)(2,1)} async-done(((bf16[256,1024]{1,0:T(8,128)(2,1)}), bf16[512,1024]{1,0:T(8,128)(2,1)}) %all-gather.16.cloned.1.call-update) | async-done | bytes 1048592 | tf_op jit(solution)/shard_map/all_gather | solution.py:54
  110.5 20.2 %reduce-scatter.18.cloned.1.call-done = bf16[256,1024]{1,0:T(8,128)(2,1)} async-done(((bf16[512,1024]{1,0:T(8,128)(2,1)}), bf16[256,1024]{1,0:T(8,128)(2,1)}) %reduce-scatter.18.cloned.1.call-update) | async-done | bytes 524304 | tf_op jit(solution)/shard_map/reduce_scatter | solution.py:62
  137.2 21.4 %all-gather.18.cloned.1.call-done = bf16[512,1024]{1,0:T(8,128)(2,1)} async-done(((bf16[256,1024]{1,0:T(8,128)(2,1)}), bf16[512,1024]{1,0:T(8,128)(2,1)}) %all-gather.18.cloned.1.call-update) | async-done | bytes 1048592 | tf_op jit(solution)/shard_map/all_gather | solution.py:54
  158.7 5.2 convolution_convert_fusion.1
  163.9 4.0 reshape.524
  179.2 20.4 %reduce-scatter.20.cloned.1.call-done = bf16[256,1024]{1,0:T(8,128)(2,1)} async-done(((bf16[512,1024]{1,0:T(8,128)(2,1)}), bf16[256,1024]{1,0:T(8,128)(2,1)}) %reduce-scatter.20.cloned.1.call-update) | async-done | bytes 524304 | tf_op jit(solution)/shard_map/reduce_scatter | solution.py:62
  203.4 21.4 %all-gather.20.cloned.1.call-done = bf16[512,1024]{1,0:T(8,128)(2,1)} async-done(((bf16[256,1024]{1,0:T(8,128)(2,1)}), bf16[512,1024]{1,0:T(8,128)(2,1)}) %all-gather.20.cloned.1.call-update) | async-done | bytes 1048592 | tf_op jit(solution)/shard_map/all_gather | solution.py:54
  231.3 20.4 %reduce-scatter.22.cloned.1.call-done = bf16[256,1024]{1,0:T(8,128)(2,1)} async-done(((bf16[512,1024]{1,0:T(8,128)(2,1)}), bf16[256,1024]{1,0:T(8,128)(2,1)}) %reduce-scatter.22.cloned.1.call-update) | async-done | bytes 524304 | tf_op jit(solution)/shard_map/reduce_scatter | solution.py:62
  259.9 18.5 %all-gather.36.cloned.1.call-done = bf16[1,512,1024]{2,1,0:T(8,128)(2,1)} async-done(((bf16[1,256,1024]{2,1,0:T(8,128)(2,1)}), bf16[1,512,1024]{2,1,0:T(8,128)(2,1)}) %all-gather.36.cloned.1.call-update) | async-done | bytes 1048592 | tf_op jit(solution)/shard_map/all_gather | solution.py:58
  278.4 5.0 fusion.42
  286.7 15.0 %all-gather.22.cloned.1.call-done = bf16[512,1024]{1,0:T(8,128)(2,1)} async-done(((bf16[256,1024]{1,0:T(8,128)(2,1)}), bf16[512,1024]{1,0:T(8,128)(2,1)}) %all-gather.22.cloned.1.call-update) | async-done | bytes 1048592 | tf_op jit(solution)/shard_map/all_gather | solution.py:54
  301.7 5.2 convolution_convert_fusion
  310.8 5.5 broadcast_select_fusion
  331.9 17.2 %reduce-scatter.24.cloned.1.call-done = bf16[256,1024]{1,0:T(8,128)(2,1)} async-done(((bf16[512,1024]{1,0:T(8,128)(2,1)}), bf16[256,1024]{1,0:T(8,128)(2,1)}) %reduce-scatter.24.cloned.1.call-update) | async-done | bytes 524304 | tf_op jit(solution)/shard_map/reduce_scatter | solution.py:62
  355.3 4.5 subtract_exponential_fusion.2
  359.8 16.3 %all-gather.26.cloned.1.call-done = bf16[512,1024]{1,0:T(8,128)(2,1)} async-done(((bf16[256,1024]{1,0:T(8,128)(2,1)}), bf16[512,1024]{1,0:T(8,128)(2,1)}) %all-gather.26.cloned.1.call-update) | async-done | bytes 1048592 | tf_op jit(solution)/shard_map/all_gather | solution.py:58
  384.0 8.2 fusion.206
  392.2 8.5 fusion.209
  407.0 19.8 %reduce-scatter.30.cloned.1.call-done = bf16[256,1024]{1,0:T(8,128)(2,1)} async-done(((bf16[512,1024]{1,0:T(8,128)(2,1)}), bf16[256,1024]{1,0:T(8,128)(2,1)}) %reduce-scatter.30.cloned.1.call-update) | async-done | bytes 524304 | tf_op jit(solution)/shard_map/reduce_scatter | solution.py:68
  437.4 12.2 all-gather.24.cloned.1.call-done
  453.4 19.0 %all-gather.28.cloned.1.call-done = bf16[512,1024]{1,0:T(8,128)(2,1)} async-done(((bf16[256,1024]{1,0:T(8,128)(2,1)}), bf16[512,1024]{1,0:T(8,128)(2,1)}) %all-gather.28.cloned.1.call-update) | async-done | bytes 1048592 | tf_op jit(solution)/shard_map/all_gather | solution.py:58
  472.4 4.9 fusion.49
  480.7 20.4 %reduce-scatter.32.cloned.1.call-done = bf16[256,1024]{1,0:T(8,128)(2,1)} async-done(((bf16[512,1024]{1,0:T(8,128)(2,1)}), bf16[256,1024]{1,0:T(8,128)(2,1)}) %reduce-scatter.32.cloned.1.call-update) | async-done | bytes 524304 | tf_op jit(solution)/shard_map/reduce_scatter | solution.py:68
  505.9 4.5 subtract_exponential_fusion.1
  510.4 16.9 %all-gather.30.cloned.1.call-done = bf16[512,1024]{1,0:T(8,128)(2,1)} async-done(((bf16[256,1024]{1,0:T(8,128)(2,1)}), bf16[512,1024]{1,0:T(8,128)(2,1)}) %all-gather.30.cloned.1.call-update) | async-done | bytes 1048592 | tf_op jit(solution)/shard_map/all_gather | solution.py:58
  535.1 8.2 fusion.212
  543.3 8.5 fusion.215
  557.6 20.4 %reduce-scatter.34.cloned.1.call-done = bf16[256,1024]{1,0:T(8,128)(2,1)} async-done(((bf16[512,1024]{1,0:T(8,128)(2,1)}), bf16[256,1024]{1,0:T(8,128)(2,1)}) %reduce-scatter.34.cloned.1.call-update) | async-done | bytes 524304 | tf_op jit(solution)/shard_map/reduce_scatter | solution.py:68
  588.9 21.2 %all-gather.32.cloned.1.call-done = bf16[512,1024]{1,0:T(8,128)(2,1)} async-done(((bf16[256,1024]{1,0:T(8,128)(2,1)}), bf16[512,1024]{1,0:T(8,128)(2,1)}) %all-gather.32.cloned.1.call-update) | async-done | bytes 1048592 | tf_op jit(solution)/shard_map/all_gather | solution.py:58
  610.1 4.9 fusion.56
  618.5 20.4 %reduce-scatter.36.cloned.1.call-done = bf16[256,1024]{1,0:T(8,128)(2,1)} async-done(((bf16[512,1024]{1,0:T(8,128)(2,1)}), bf16[256,1024]{1,0:T(8,128)(2,1)}) %reduce-scatter.36.cloned.1.call-update) | async-done | bytes 524304 | tf_op jit(solution)/shard_map/reduce_scatter | solution.py:68
  643.5 4.4 subtract_exponential_fusion
  647.9 17.0 %all-gather.34.cloned.1.call-done = bf16[512,1024]{1,0:T(8,128)(2,1)} async-done(((bf16[256,1024]{1,0:T(8,128)(2,1)}), bf16[512,1024]{1,0:T(8,128)(2,1)}) %all-gather.34.cloned.1.call-update) | async-done | bytes 1048592 | tf_op jit(solution)/shard_map/all_gather | solution.py:58
  672.7 8.2 fusion.218
  680.9 8.5 fusion.221
  695.2 5.0 fusion.296
  722.8 7.1 add_bitcast_fusion.1
  730.0 5.2 add_bitcast_fusion.2
  735.1 5.0 add_bitcast_fusion
  743.1 4.2 add_bitcast_fusion.3
  753.6 4.2 reduce-scatter.40.cloned.1.call-done
  758.9 22.1 %psum.39 = f32[4,512]{1,0:T(4,128)S(1)} all-reduce(f32[4,512]{1,0:T(4,128)S(1)} %copy.212), channel_id=1, replica_groups=mesh['section'=2,'dp'=8,'tensor'=2] {'dp'}, use_global_device_ids=true, to_apply=%region_66.67 | all-reduce | flops 2048 | bytes 16384 | tf_op jit(solution)/shard_map/psum | solution.py:269
  781.6 495.0 %all-reduce.3.cloned.1.call-done = (f32[1,1024,3,512]{3,1,2,0:T(8,128)}, f32[1,512,1024]{2,1,0:T(8,128)}, f32[1,1024,1024]{2,1,0:T(8,128)}, f32[1,1024,1024]{2,1,0:T(8,128)}) async-done(((f32[1,1024,3,512]{3,1,2,0:T(8,128)}, f32[1,512,1024]{2,1,0:T(8,128)}, f32[1,1024,1024]{2,1,0:T(8,128)}, f32[1,1024,1024]{2,1,0:T(8,128)}), (f32[1,1024,3,512]{3,1,2,0:T(8,128)}, f32[1,512,1024]{2,1,0:T(8,128)}, ...) | async-done | bytes 16777232 | tf_op jit(solution)/shard_map/psum | solution.py:269
  1276.6 6.3 copy.227
  (374 shorter events, 223.2 us)
Async XLA Ops:
  7.2 96.7 %copy-start = (bf16[1,1024,1024]{2,1,0:T(8,128)(2,1)S(1)}, bf16[1,1024,1024]{2,1,0:T(8,128)(2,1)}, u32[]{:S(2)}) copy-start(bf16[1,1024,1024]{2,1,0:T(8,128)(2,1)} %param.13) | copy-start | bytes 6291460
  7.2 6.4 copy-start.72
  7.2 30.5 %all-gather.14.cloned.1.call-start = ((), (), s32[]{:S(2)}) async-start(), calls=%async_computation.13 | async-start | bytes 1572864 | tf_op jit(solution)/shard_map/all_gather | solution.py:54
  13.6 64.9 %reduce-scatter.16.cloned.1.call-start = ((), (), s32[]{:S(2)}) async-start(), calls=%async_computation.14 | async-start | bytes 1572864 | tf_op jit(solution)/shard_map/reduce_scatter | solution.py:62
  20.3 33.6 %copy-start.58 = (pred[512,512]{0,1:T(8,128)(4,1)}, pred[512,512]{0,1:T(8,128)(4,1)S(1)}, u32[]{:S(2)}) copy-start(pred[512,512]{0,1:T(8,128)(4,1)S(1)} %get-tuple-element.66) | copy-start | bytes 786436
  55.5 23.0 %copy-start.1 = (bf16[2,256,1024]{2,1,0:T(8,128)(2,1)S(1)}, bf16[2,256,1024]{2,1,0:T(8,128)(2,1)}, u32[]{:S(2)}) copy-start(bf16[2,256,1024]{2,1,0:T(8,128)(2,1)} %param.9) | copy-start | bytes 3145732
  58.0 45.8 %all-gather.16.cloned.1.call-start = ((), (), s32[]{:S(2)}) async-start(), calls=%async_computation.15 | async-start | bytes 1572864 | tf_op jit(solution)/shard_map/all_gather | solution.py:54
  82.4 48.3 %reduce-scatter.18.cloned.1.call-start = ((), (), s32[]{:S(2)}) async-start(), calls=%async_computation.16 | async-start | bytes 1572864 | tf_op jit(solution)/shard_map/reduce_scatter | solution.py:62
  110.2 48.5 %all-gather.18.cloned.1.call-start = ((), (), s32[]{:S(2)}) async-start(), calls=%async_computation.17 | async-start | bytes 1572864 | tf_op jit(solution)/shard_map/all_gather | solution.py:54
  130.7 4.8 copy-start.2
  132.3 3.3 collective-permute-start
  137.2 62.4 %reduce-scatter.20.cloned.1.call-start = ((), (), s32[]{:S(2)}) async-start(), calls=%async_computation.18 | async-start | bytes 1572864 | tf_op jit(solution)/shard_map/reduce_scatter | solution.py:62
  179.1 45.7 %all-gather.20.cloned.1.call-start = ((), (), s32[]{:S(2)}) async-start(), calls=%async_computation.19 | async-start | bytes 1572864 | tf_op jit(solution)/shard_map/all_gather | solution.py:54
  203.4 48.3 %reduce-scatter.22.cloned.1.call-start = ((), (), s32[]{:S(2)}) async-start(), calls=%async_computation.20 | async-start | bytes 1572864 | tf_op jit(solution)/shard_map/reduce_scatter | solution.py:62
  231.3 47.1 %all-gather.36.cloned.1.call-start = ((), (), s32[]{:S(2)}) async-start(), calls=%async_computation.36 | async-start | bytes 1572864 | tf_op jit(solution)/shard_map/all_gather | solution.py:58
  251.7 4.3 copy-start.35
  254.4 3.3 collective-permute-start.1
  256.9 44.8 %all-gather.22.cloned.1.call-start = ((), (), s32[]{:S(2)}) async-start(), calls=%async_computation.21 | async-start | bytes 1572864 | tf_op jit(solution)/shard_map/all_gather | solution.py:54
  259.9 68.8 %reduce-scatter.28.cloned.1.call-start = ((), (), s32[]{:S(2)}) async-start(), calls=%async_computation.25 | async-start | bytes 1572864 | tf_op jit(solution)/shard_map/reduce_scatter | solution.py:68
  286.6 62.6 %reduce-scatter.24.cloned.1.call-start = ((), (), s32[]{:S(2)}) async-start(), calls=%async_computation.22 | async-start | bytes 1572864 | tf_op jit(solution)/shard_map/reduce_scatter | solution.py:62
  328.4 47.8 %all-gather.26.cloned.1.call-start = ((), (), s32[]{:S(2)}) async-start(), calls=%async_computation.26 | async-start | bytes 1572864 | tf_op jit(solution)/shard_map/all_gather | solution.py:58
  354.7 72.1 %reduce-scatter.30.cloned.1.call-start = ((), (), s32[]{:S(2)}) async-start(), calls=%async_computation.27 | async-start | bytes 1572864 | tf_op jit(solution)/shard_map/reduce_scatter | solution.py:68
  406.3 22.6 %copy-start.70 = (f32[256]{0:T(256)S(1)}, f32[256]{0:T(256)}, u32[]{:S(2)}) copy-start(f32[256]{0:T(256)} %get-tuple-element.69) | copy-start | bytes 3076
  406.3 43.3 %all-gather.24.cloned.1.call-start = ((), (), s32[]{:S(2)}) async-start(), calls=%async_computation.23 | async-start | bytes 1572864 | tf_op jit(solution)/shard_map/all_gather | solution.py:54
  406.9 65.5 %all-gather.28.cloned.1.call-start = ((), (), s32[]{:S(2)}) async-start(), calls=%async_computation.28 | async-start | bytes 1572864 | tf_op jit(solution)/shard_map/all_gather | solution.py:58
  428.9 7.2 copy-start.36
  432.3 3.8 collective-permute-start.2
  437.0 64.2 %reduce-scatter.32.cloned.1.call-start = ((), (), s32[]{:S(2)}) async-start(), calls=%async_computation.29 | async-start | bytes 1572864 | tf_op jit(solution)/shard_map/reduce_scatter | solution.py:68
  480.7 46.6 %all-gather.30.cloned.1.call-start = ((), (), s32[]{:S(2)}) async-start(), calls=%async_computation.30 | async-start | bytes 1572864 | tf_op jit(solution)/shard_map/all_gather | solution.py:58
  505.8 72.2 %reduce-scatter.34.cloned.1.call-start = ((), (), s32[]{:S(2)}) async-start(), calls=%async_computation.31 | async-start | bytes 1572864 | tf_op jit(solution)/shard_map/reduce_scatter | solution.py:68
  557.5 22.6 %copy-start.71 = (f32[256]{0:T(256)S(1)}, f32[256]{0:T(256)}, u32[]{:S(2)}) copy-start(f32[256]{0:T(256)} %get-tuple-element.70) | copy-start | bytes 3076
  557.5 52.5 %all-gather.32.cloned.1.call-start = ((), (), s32[]{:S(2)}) async-start(), calls=%async_computation.32 | async-start | bytes 1572864 | tf_op jit(solution)/shard_map/all_gather | solution.py:58
  583.2 3.8 collective-permute-start.3
  588.6 50.3 %reduce-scatter.36.cloned.1.call-start = ((), (), s32[]{:S(2)}) async-start(), calls=%async_computation.33 | async-start | bytes 1572864 | tf_op jit(solution)/shard_map/reduce_scatter | solution.py:68
  618.4 46.5 %all-gather.34.cloned.1.call-start = ((), (), s32[]{:S(2)}) async-start(), calls=%async_computation.34 | async-start | bytes 1572864 | tf_op jit(solution)/shard_map/all_gather | solution.py:58
  643.4 96.7 %reduce-scatter.38.cloned.1.call-start = ((), (), s32[]{:S(2)}) async-start(), calls=%async_computation.35 | async-start | bytes 1572864 | tf_op jit(solution)/shard_map/reduce_scatter | solution.py:68
  695.1 52.3 %reduce-scatter.26.cloned.1.call-start = ((), (), s32[]{:S(2)}) async-start(), calls=%async_computation.24 | async-start | bytes 1572864 | tf_op jit(solution)/shard_map/reduce_scatter | solution.py:62
  695.1 5.1 copy-start.51
  695.2 5.1 copy-start.79
  695.2 5.1 copy-start.86
  706.3 51.5 %reduce-scatter.40.cloned.1.call-start = ((), (), s32[]{:S(2)}) async-start(), calls=%async_computation.37 | async-start | bytes 786432
  722.8 7.1 copy-start.3
  722.8 7.1 copy-start.17
  730.0 5.2 copy-start.15
  730.0 5.2 copy-start.30
  743.1 533.5 %all-reduce.3.cloned.1.call-start = ((), (), s32[]{:S(2)}) async-start(), calls=%async_computation.38 | async-start | bytes 33554432 | tf_op jit(solution)/shard_map/psum | solution.py:269
  747.3 4.1 copy-start.69
  1276.6 6.3 copy-start.44
  (72 other events, 181.6 us)
Sparse Core Ops, SparseCore 0:
  13.7 23.9 all-gather.13
  58.1 20.3 reduce-scatter.15
  82.5 21.2 all-gather.15
  110.3 20.3 reduce-scatter.17
  137.3 21.3 all-gather.17
  179.2 20.3 reduce-scatter.19
  203.5 21.2 all-gather.19
  231.4 20.3 reduce-scatter.21
  257.0 21.2 all-gather.35
  280.3 21.2 all-gather.21
  304.5 20.3 reduce-scatter.27
  328.5 20.6 reduce-scatter.23
  354.8 21.2 all-gather.25
  406.5 20.3 reduce-scatter.29
  428.3 21.2 all-gather.23
  451.1 21.2 all-gather.27
  480.8 20.3 reduce-scatter.31
  506.0 21.2 all-gather.29
  557.7 20.3 reduce-scatter.33
  588.8 21.2 all-gather.31
  618.5 20.3 reduce-scatter.35
  643.6 21.2 all-gather.33
  695.2 20.3 reduce-scatter.37
  718.3 20.3 reduce-scatter.25
  743.2 14.5 reduce-scatter.39
  763.9 512.6 all-reduce.2
where the time goes:
time: 1310 us; the launch traced here: 1300 us
  waiting for transfers between devices  905 us (69%)
  matrix products  211 us (16%)
  other arithmetic  71.9 us (5%)
  local copies, waits for them, and re-layouts  64.9 us (5%)
  blocking collectives  22.1 us (2%)
  between operations  15.5 us (1%)
    psum x1, waiting for transfers between devices, per_device(): lax.psum((part_qkv, part_out, part_up, part_down, norm_local), 'dp')  495 us
    all_gather x6, waiting for transfers between devices, gather_grads(): return lax.all_gather(shard, 'tensor', axis=0, tiled=True)  109 us
    all_gather x6, waiting for transfers between devices, gather_tokens(): return lax.all_gather(shard, 'tensor', axis=0, tiled=True)  109 us
    reduce_scatter x6, waiting for transfers between devices, sum_partials(): lax.psum_scatter(term_rows.astype(jnp.bfloat16), 'tensor', scatter_dimens...  98.7 us
    reduce_scatter x6, waiting for transfers between devices, sum_grad_partials(): lax.psum_scatter(term_rows.astype(jnp.bfloat16), 'tensor', scatter_dimens...  81.1 us
    unnamed x186, local copies, waits for them, and re-layouts  42.9 us
  transfers between devices with their start and end apart: 30, of which 27 were waited for; matrix products, arithmetic and copies ran while one was open for 10% of the time, Pallas kernels for 0%

commit v1 on v0

v1 whole, which is shorter than its diff:
```python
import functools

import jax
import jax.numpy as jnp
import numpy as np
from jax import lax
from jax.experimental import pallas as pl
from jax.experimental.pallas import tpu as pltpu
from jax.sharding import PartitionSpec as P

HEAD_DIM = 128
BAND = 128
EPSILON = 1e-05
MASKED = -1e30
VMEM = 56 * 1024 * 1024
bf16 = jnp.bfloat16
f32 = jnp.float32


def params(*semantics):
    return pltpu.CompilerParams(
        dimension_semantics=semantics or None, vmem_limit_bytes=VMEM
    )


def cost(flops, moved):
    return pl.CostEstimate(
        flops=int(flops), bytes_accessed=int(moved), transcendentals=0
    )


def dot(a, b):
    return jnp.dot(a, b, preferred_element_type=f32)


def dot_nt(a, b):
    return lax.dot_general(a, b, (((1,), (1,)), ((), ())), preferred_element_type=f32)


def dot_tn(a, b):
    return lax.dot_general(a, b, (((0,), (0,)), ((), ())), preferred_element_type=f32)


def unit_of(values):
    centre = values - jnp.mean(values, axis=-1, keepdims=True)
    spread = jnp.mean(centre * centre, axis=-1, keepdims=True)
    scale = lax.rsqrt(spread + EPSILON)
    return centre * scale, scale


def norm_back(incoming, values, gain):
    unit, scale = unit_of(values)
    scaled = incoming * gain
    inner = (
        scaled
        - jnp.mean(scaled, axis=-1, keepdims=True)
        - unit * jnp.mean(scaled * unit, axis=-1, keepdims=True)
    )
    grads = jnp.concatenate(
        [
            jnp.sum(incoming * unit, axis=0, keepdims=True),
            jnp.sum(incoming, axis=0, keepdims=True),
        ],
        axis=0,
    )
    return scale * inner, grads


def qkv_body(u_ref, gain_ref, bias_ref, w_ref, n1_ref, qkv_ref):
    @pl.when(pl.program_id(0) == 0)
    def _():
        unit, _ = unit_of(u_ref[...].astype(f32))
        n1_ref[...] = (unit * gain_ref[...] + bias_ref[...]).astype(bf16)

    qkv_ref[...] = dot(n1_ref[...], w_ref[...]).astype(bf16)


def qkv_call(u, gain, bias, w):
    rows, width = u.shape
    columns = w.shape[1]
    tile = 512
    return pl.pallas_call(
        qkv_body,
        grid=(columns // tile,),
        in_specs=[
            pl.BlockSpec((rows, width), lambda i: (0, 0)),
            pl.BlockSpec((1, width), lambda i: (0, 0)),
            pl.BlockSpec((1, width), lambda i: (0, 0)),
            pl.BlockSpec((width, tile), lambda i: (0, i)),
        ],
        out_specs=[
            pl.BlockSpec((rows, width), lambda i: (0, 0)),
            pl.BlockSpec((rows, tile), lambda i: (0, i)),
        ],
        out_shape=[
            jax.ShapeDtypeStruct((rows, width), bf16),
            jax.ShapeDtypeStruct((rows, columns), bf16),
        ],
        compiler_params=params("arbitrary"),
        cost_estimate=cost(
            2 * rows * width * columns, 2 * width * columns + 2 * rows * columns
        ),
        name="qkv",
    )(u, gain, bias, w)


def band_probs(q, k, start_ref, block):
    low = max(block - 1, 0) * BAND
    high = (block + 1) * BAND
    keys = k[low:high]
    scores = dot_nt(q[block * BAND : high], keys) * HEAD_DIM**-0.5
    row = lax.broadcasted_iota(jnp.int32, scores.shape, 0) + block * BAND
    column = lax.broadcasted_iota(jnp.int32, scores.shape, 1) + low
    first = start_ref[block * BAND : high, :]
    allowed = (column <= row) & (column >= first)
    scores = jnp.where(allowed, scores, MASKED)
    expo = jnp.exp(scores - jnp.max(scores, axis=-1, keepdims=True))
    return expo / jnp.sum(expo, axis=-1, keepdims=True), low, high


def attention_body(
    heads, q_ref, k_ref, v_ref, start_ref, w_ref, u_ref, gain_ref, bias_ref,
    o_ref, h_ref, n2_ref,
):
    step = pl.program_id(0)
    rows = q_ref.shape[0]
    for head in range(heads):
        cut = slice(head * HEAD_DIM, (head + 1) * HEAD_DIM)
        q, k, v = q_ref[:, cut], k_ref[:, cut], v_ref[:, cut]
        for block in range(rows // BAND):
            probs, low, high = band_probs(q, k, start_ref, block)
            o_ref[block * BAND : high, cut] = dot(probs.astype(bf16), v[low:high]).astype(bf16)
    term = dot(o_ref[...], w_ref[...])

    @pl.when(step == 0)
    def _():
        h_ref[...] = u_ref[...].astype(f32) + term

    @pl.when(step > 0)
    def _():
        h_ref[...] += term

    @pl.when(step == pl.num_programs(0) - 1)
    def _():
        unit, _ = unit_of(h_ref[...])
        n2_ref[...] = (unit * gain_ref[...] + bias_ref[...]).astype(bf16)


def attention_call(qkv, start, w_out, u, gain, bias):
    rows, width = u.shape
    heads = 2
    wide = heads * HEAD_DIM
    steps = w_out.shape[0] // wide
    return pl.pallas_call(
        functools.partial(attention_body, heads),
        grid=(steps,),
        in_specs=[
            pl.BlockSpec((rows, wide), lambda i: (0, i)),
            pl.BlockSpec((rows, wide), lambda i: (0, steps + i)),
            pl.BlockSpec((rows, wide), lambda i: (0, 2 * steps + i)),
            pl.BlockSpec((rows, 1), lambda i: (0, 0)),
            pl.BlockSpec((wide, width), lambda i: (i, 0)),
            pl.BlockSpec((rows, width), lambda i: (0, 0)),
            pl.BlockSpec((1, width), lambda i: (0, 0)),
            pl.BlockSpec((1, width), lambda i: (0, 0)),
        ],
        out_specs=[
            pl.BlockSpec((rows, wide), lambda i: (0, i)),
            pl.BlockSpec((rows, width), lambda i: (0, 0)),
            pl.BlockSpec((rows, width), lambda i: (0, 0)),
        ],
        out_shape=[
            jax.ShapeDtypeStruct((rows, steps * wide), bf16),
            jax.ShapeDtypeStruct((rows, width), f32),
            jax.ShapeDtypeStruct((rows, width), bf16),
        ],
        compiler_params=params("arbitrary"),
        cost_estimate=cost(8e9, 10e6),
        name="attention",
    )(qkv, qkv, qkv, start, w_out, u, gain, bias)


def mlp_body(n2_ref, h_ref, up_ref, down_ref, z_ref, slope_ref, y_ref, total):
    step = pl.program_id(0)
    a = dot(n2_ref[...], up_ref[...])
    c = np.float32(np.sqrt(2 / np.pi))
    square = a * a
    t = jnp.tanh(c * a * (1.0 + 0.044715 * square))
    half = 0.5 * (1.0 + t)
    z = (a * half).astype(bf16)
    slope = half + 0.5 * c * a * (1.0 - t * t) * (1.0 + 3 * 0.044715 * square)
    z_ref[...] = z
    slope_ref[...] = slope.astype(bf16)
    term = dot(z, down_ref[...])

    @pl.when(step == 0)
    def _():
        total[...] = h_ref[...] + term

    @pl.when(step > 0)
    def _():
        total[...] += term

    @pl.when(step == pl.num_programs(0) - 1)
    def _():
        y_ref[...] = total[...].astype(bf16)


def mlp_call(n2, h, w_up, w_down):
    rows, width = h.shape
    units = w_up.shape[1]
    tile = 512
    return pl.pallas_call(
        mlp_body,
        grid=(units // tile,),
        in_specs=[
            pl.BlockSpec((rows, width), lambda i: (0, 0)),
            pl.BlockSpec((rows, width), lambda i: (0, 0)),
            pl.BlockSpec((width, tile), lambda i: (0, i)),
            pl.BlockSpec((tile, width), lambda i: (i, 0)),
        ],
        out_specs=[
            pl.BlockSpec((rows, tile), lambda i: (0, i)),
            pl.BlockSpec((rows, tile), lambda i: (0, i)),
            pl.BlockSpec((rows, width), lambda i: (0, 0)),
        ],
        out_shape=[
            jax.ShapeDtypeStruct((rows, units), bf16),
            jax.ShapeDtypeStruct((rows, units), bf16),
            jax.ShapeDtypeStruct((rows, width), bf16),
        ],
        scratch_shapes=[pltpu.VMEM((rows, width), f32)],
        compiler_params=params("arbitrary"),
        cost_estimate=cost(4 * rows * width * units, 4 * width * units + 8 * rows * units),
        name="mlp",
    )(n2, h, w_up, w_down)


def mlp_back_body(
    gy_ref, slope_ref, up_ref, down_ref, h_ref, gain_ref,
    da_ref, dh_ref, gh_ref, grads_ref, total,
):
    step = pl.program_id(0)
    dz = dot_nt(gy_ref[...], down_ref[...])
    da = (dz * slope_ref[...].astype(f32)).astype(bf16)
    da_ref[...] = da
    term = dot_nt(da, up_ref[...])

    @pl.when(step == 0)
    def _():
        total[...] = term

    @pl.when(step > 0)
    def _():
        total[...] += term

    @pl.when(step == pl.num_programs(0) - 1)
    def _():
        back, grads = norm_back(total[...], h_ref[...], gain_ref[...])
        dh = gy_ref[...].astype(f32) + back
        dh_ref[...] = dh
        gh_ref[...] = dh.astype(bf16)
        grads_ref[...] = grads


def mlp_back_call(gy, slope, w_up, w_down, h, gain):
    rows, width = h.shape
    units = w_up.shape[1]
    tile = 512
    return pl.pallas_call(
        mlp_back_body,
        grid=(units // tile,),
        in_specs=[
            pl.BlockSpec((rows, width), lambda i: (0, 0)),
            pl.BlockSpec((rows, tile), lambda i: (0, i)),
            pl.BlockSpec((width, tile), lambda i: (0, i)),
            pl.BlockSpec((tile, width), lambda i: (i, 0)),
            pl.BlockSpec((rows, width), lambda i: (0, 0)),
            pl.BlockSpec((1, width), lambda i: (0, 0)),
        ],
        out_specs=[
            pl.BlockSpec((rows, tile), lambda i: (0, i)),
            pl.BlockSpec((rows, width), lambda i: (0, 0)),
            pl.BlockSpec((rows, width), lambda i: (0, 0)),
            pl.BlockSpec((2, width), lambda i: (0, 0)),
        ],
        out_shape=[
            jax.ShapeDtypeStruct((rows, units), bf16),
            jax.ShapeDtypeStruct((rows, width), f32),
            jax.ShapeDtypeStruct((rows, width), bf16),
            jax.ShapeDtypeStruct((2, width), f32),
        ],
        scratch_shapes=[pltpu.VMEM((rows, width), f32)],
        compiler_params=params("arbitrary"),
        cost_estimate=cost(4 * rows * width * units, 4 * width * units + 8 * rows * units),
        name="mlp_back",
    )(gy, slope, w_up, w_down, h, gain)


def mlp_grads_body(sec_ref, z_ref, gy_ref, n2_ref, da_ref, out_ref):
    half = out_ref.shape[0] // 2
    out_ref[:half, :] = dot_tn(z_ref[...], gy_ref[...]).astype(bf16)
    out_ref[half:, :] = dot_tn(n2_ref[...], da_ref[...]).astype(bf16)


def mlp_grads_call(sec, z, gy, n2, da):
    rows, width = gy.shape
    units = width
    half = units // 2

    def pick(i, sec_ref):
        return lax.rem(sec_ref[0] + 1 + i, 2)

    return pl.pallas_call(
        mlp_grads_body,
        grid_spec=pltpu.PrefetchScalarGridSpec(
            num_scalar_prefetch=1,
            grid=(2,),
            in_specs=[
                pl.BlockSpec((rows, half), lambda i, s: (0, pick(i, s))),
                pl.BlockSpec((rows, width), lambda i, s: (0, 0)),
                pl.BlockSpec((rows, width // 2), lambda i, s: (0, pick(i, s))),
                pl.BlockSpec((rows, units), lambda i, s: (0, 0)),
            ],
            out_specs=pl.BlockSpec((None, 2 * half, width), lambda i, s: (i, 0, 0)),
        ),
        out_shape=jax.ShapeDtypeStruct((2, 2 * half, width), bf16),
        compiler_params=params("arbitrary"),
        cost_estimate=cost(4 * rows * width * units, 8 * width * units),
        name="mlp_grads",
    )(sec, z, gy, n2, da)


def attention_back_body(
    heads, q_ref, k_ref, v_ref, start_ref, gh_ref, w_ref, dq_ref, dk_ref, dv_ref
):
    rows = q_ref.shape[0]
    blocks = rows // BAND
    do_all = dot_nt(gh_ref[...], w_ref[...]).astype(bf16)
    for head in range(heads):
        cut = slice(head * HEAD_DIM, (head + 1) * HEAD_DIM)
        q, k, v = q_ref[:, cut], k_ref[:, cut], v_ref[:, cut]
        do = do_all[:, cut]
        dk_parts, dv_parts = [None] * blocks, [None] * blocks

        def put(parts, block, term, low):
            for piece in range(term.shape[0] // BAND):
                place = low // BAND + piece
                add = term[piece * BAND : (piece + 1) * BAND]
                parts[place] = add if parts[place] is None else parts[place] + add

        for block in range(blocks):
            probs, low, high = band_probs(q, k, start_ref, block)
            here = slice(block * BAND, high)
            dp = dot_nt(do[here], v[low:high])
            inner = jnp.sum(probs * dp, axis=-1, keepdims=True)
            ds = (probs * (dp - inner) * HEAD_DIM**-0.5).astype(bf16)
            dq_ref[here, cut] = dot(ds, k[low:high]).astype(bf16)
            put(dk_parts, block, dot_tn(ds, q[here]), low)
            put(dv_parts, block, dot_tn(probs.astype(bf16), do[here]), low)
        for block in range(blocks):
            here = slice(block * BAND, (block + 1) * BAND)
            dk_ref[here, cut] = dk_parts[block].astype(bf16)
            dv_ref[here, cut] = dv_parts[block].astype(bf16)


def attention_back_call(qkv, start, gh, w_out):
    rows, width = gh.shape
    heads = 2
    wide = heads * HEAD_DIM
    steps = w_out.shape[0] // wide
    out = jax.ShapeDtypeStruct((rows, steps * wide), bf16)
    return pl.pallas_call(
        functools.partial(attention_back_body, heads),
        grid=(steps,),
        in_specs=[
            pl.BlockSpec((rows, wide), lambda i: (0, i)),
            pl.BlockSpec((rows, wide), lambda i: (0, steps + i)),
            pl.BlockSpec((rows, wide), lambda i: (0, 2 * steps + i)),
            pl.BlockSpec((rows, 1), lambda i: (0, 0)),
            pl.BlockSpec((rows, width), lambda i: (0, 0)),
            pl.BlockSpec((wide, width), lambda i: (i, 0)),
        ],
        out_specs=[pl.BlockSpec((rows, wide), lambda i: (0, i))] * 3,
        out_shape=[out] * 3,
        compiler_params=params("arbitrary"),
        cost_estimate=cost(12e9, 10e6),
        name="attention_back",
    )(qkv, qkv, qkv, start, gh, w_out)


def attention_grads_body(
    sec_ref, o_ref, gh_ref, n1_ref, dq_ref, dk_ref, dv_ref, out_ref
):
    first = o_ref.shape[1]
    local = dq_ref.shape[1]
    out_ref[:first, :] = dot_tn(o_ref[...], gh_ref[...]).astype(bf16)
    for place, ref in enumerate((dq_ref, dk_ref, dv_ref)):
        term = dot_tn(n1_ref[...], ref[...]).astype(bf16)
        deep = term.shape[0] // 2
        at = first + place * deep
        out_ref[at : at + deep, :local] = term[:deep]
        out_ref[at : at + deep, local:] = term[deep:]


def attention_grads_call(sec, o, gh, n1, dq, dk, dv):
    rows, width = gh.shape
    local = width // 2

    def pick(i, sec_ref):
        return lax.rem(sec_ref[0] + 1 + i, 2)

    whole = local // 2 + 3 * width // 4
    return pl.pallas_call(
        attention_grads_body,
        grid_spec=pltpu.PrefetchScalarGridSpec(
            num_scalar_prefetch=1,
            grid=(2,),
            in_specs=[
                pl.BlockSpec((rows, local // 2), lambda i, s: (0, pick(i, s))),
                pl.BlockSpec((rows, width), lambda i, s: (0, 0)),
                pl.BlockSpec((rows, width // 2), lambda i, s: (0, pick(i, s))),
                pl.BlockSpec((rows, local), lambda i, s: (0, 0)),
                pl.BlockSpec((rows, local), lambda i, s: (0, 0)),
                pl.BlockSpec((rows, local), lambda i, s: (0, 0)),
            ],
            out_specs=pl.BlockSpec((None, whole, width), lambda i, s: (i, 0, 0)),
        ),
        out_shape=jax.ShapeDtypeStruct((2, whole, width), bf16),
        compiler_params=params("arbitrary"),
        cost_estimate=cost(4 * rows * width * width, 8 * width * width),
        name="attention_grads",
    )(sec, o, gh, n1, dq, dk, dv)


def input_back_body(
    dq_ref, dk_ref, dv_ref, wq_ref, wk_ref, wv_ref, dh_ref, u_ref, gain_ref,
    du_ref, grads_ref, total,
):
    step = pl.program_id(0)
    term = (
        dot_nt(dq_ref[...], wq_ref[...])
        + dot_nt(dk_ref[...], wk_ref[...])
        + dot_nt(dv_ref[...], wv_ref[...])
    )

    @pl.when(step == 0)
    def _():
        total[...] = term

    @pl.when(step > 0)
    def _():
        total[...] += term

    @pl.when(step == pl.num_programs(0) - 1)
    def _():
        back, grads = norm_back(total[...], u_ref[...].astype(f32), gain_ref[...])
        du_ref[...] = (dh_ref[...] + back).astype(bf16)
        grads_ref[...] = grads


def input_back_call(dq, dk, dv, w_qkv, dh, u, gain):
    rows, width = dh.shape
    tile = 512
    steps = dq.shape[1] // tile
    return pl.pallas_call(
        input_back_body,
        grid=(steps,),
        in_specs=[pl.BlockSpec((rows, tile), lambda i: (0, i))] * 3
        + [
            pl.BlockSpec((width, tile), functools.partial(lambda j, i: (0, j * steps + i), j))
            for j in range(3)
        ]
        + [
            pl.BlockSpec((rows, width), lambda i: (0, 0)),
            pl.BlockSpec((rows, width), lambda i: (0, 0)),
            pl.BlockSpec((1, width), lambda i: (0, 0)),
        ],
        out_specs=[
            pl.BlockSpec((rows, width), lambda i: (0, 0)),
            pl.BlockSpec((2, width), lambda i: (0, 0)),
        ],
        out_shape=[
            jax.ShapeDtypeStruct((rows, width), bf16),
            jax.ShapeDtypeStruct((2, width), f32),
        ],
        scratch_shapes=[pltpu.VMEM((rows, width), f32)],
        compiler_params=params("arbitrary"),
        cost_estimate=cost(
            2 * rows * width * w_qkv.shape[1], 2 * width * w_qkv.shape[1] + 8 * rows * width
        ),
        name="input_back",
    )(dq, dk, dv, w_qkv, w_qkv, w_qkv, dh, u, gain)


def ring_places(count):
    size = min(8, count)
    walk = list(range(0, size, 2)) + list(range(1, size, 2))[::-1]
    return size, walk


def ring_routes(count):
    size, walk = ring_places(count)
    up = []
    for base in range(0, count, size):
        for place in range(size):
            up.append((base + walk[place], base + walk[(place + 1) % size]))
    return up, [(b, a) for a, b in up]


def ring_gather(piece, up, down, size):
    rows = piece.shape[0]
    ups, downs = [piece], [piece]
    reach = (size - 1) // 2
    for _ in range(reach):
        ups.append(lax.ppermute(ups[-1], "dp", up))
        downs.append(lax.ppermute(downs[-1], "dp", down))
    far_up = lax.ppermute(ups[-1][: rows // 2], "dp", up)
    far_down = lax.ppermute(downs[-1][rows // 2 :], "dp", down)
    return jnp.concatenate(ups + downs[1:] + [far_up, far_down], axis=0)


def slot_places(place, size):
    reach = (size - 1) // 2
    steps = list(range(0, -reach - 1, -1)) + list(range(1, reach + 1)) + [size // 2]
    return lax.rem(place + np.asarray(steps, np.int32) + size, size).astype(jnp.int32)


def halving_order(count):
    bits = count.bit_length() - 1
    first = list(range(bits))
    second = [1, 0] + first[2:] if bits > 1 else first
    return first, second


def pairs_of(count, step):
    routes = []
    for core, order in enumerate(halving_order(count)):
        for i in range(count):
            routes.append((core * count + i, core * count + (i ^ (1 << order[step]))))
    return routes


def own_bits(sec, rank, count):
    first, second = halving_order(count)
    return [
        lax.rem(rank >> jnp.where(sec == 0, a, b), 2) for a, b in zip(first, second)
    ]


def halving_sum(kept, received, bits, count):
    rows = kept.shape[0] // 2

    def both(side):
        a = lax.dynamic_slice_in_dim(kept, side * rows, rows, 0).astype(f32)
        b = lax.dynamic_slice_in_dim(received, side * rows, rows, 0).astype(f32)
        return a + b

    away = lax.ppermute(both(1 - bits[0]).astype(bf16), ("section", "dp"), pairs_of(count, 0))
    held = (both(bits[0]) + away.astype(f32)).astype(bf16)
    for step in range(1, len(bits)):
        rows //= 2
        send = lax.dynamic_slice_in_dim(held, (1 - bits[step]) * rows, rows, 0)
        keep = lax.dynamic_slice_in_dim(held, bits[step] * rows, rows, 0)
        away = lax.ppermute(send, ("section", "dp"), pairs_of(count, step))
        held = (keep.astype(f32) + away.astype(f32)).astype(bf16)
    return held


def doubling_gather(held, bits, count):
    for step in reversed(range(len(bits))):
        away = lax.ppermute(held, ("section", "dp"), pairs_of(count, step))
        low = bits[step] == 0
        held = jnp.concatenate([jnp.where(low, held, away), jnp.where(low, away, held)], axis=0)
    return held


def place_attention_body(
    size, sec_ref, at_ref, mine_qkv, swap_qkv, mine_out, swap_out, own_ref, far_ref,
    qkv_ref, out_ref, sem,
):
    layer, sec = at_ref[size], sec_ref[0]
    width = out_ref.shape[1]
    local = width // 2
    copies = []

    def put(source, target):
        copies.append(pltpu.make_async_copy(source, target, sem.at[len(copies)]))

    def put_own(qkv, out):
        for j in range(3):
            yield pltpu.make_async_copy(
                qkv.at[:, j * local : (j + 1) * local],
                qkv_ref.at[:, j * width : j * width + local],
                sem.at[j],
            )
        yield pltpu.make_async_copy(out, out_ref.at[:local, :], sem.at[3])

    @pl.when(layer == sec)
    def _():
        for c in put_own(mine_qkv, mine_out):
            c.start()

    @pl.when(layer != sec)
    def _():
        for c in put_own(swap_qkv, swap_out):
            c.start()

    rows = width // size // 2
    out_rows = local // size // 2

    def each(act):
        def body(slot, _):
            place = at_ref[slot]
            for side, ref in ((0, own_ref), (1, far_ref)):
                core = lax.rem(sec + side, 2)
                source = slot * 2 * rows
                row = place * 2 * rows + core * rows
                out_row = local + place * 2 * out_rows + core * out_rows
                base = 4 + side
                act(
                    ref.at[pl.ds(source, rows), :local],
                    qkv_ref.at[pl.ds(row, rows), local:width],
                    sem.at[base],
                )
                act(
                    ref.at[pl.ds(source, rows), local:],
                    qkv_ref.at[pl.ds(row, rows), width + local : 2 * width],
                    sem.at[base],
                )
                for part in range(2):
                    act(
                        ref.at[pl.ds(source + rows, rows // 2), part * local : (part + 1) * local],
                        qkv_ref.at[
                            pl.ds(row + part * (rows // 2), rows // 2), 2 * width + local :
                        ],
                        sem.at[base],
                    )
                act(
                    ref.at[pl.ds(source + rows + rows // 2, out_rows), :],
                    out_ref.at[pl.ds(out_row, out_rows), :],
                    sem.at[base],
                )
            return 0

        lax.fori_loop(0, size, body, 0)

    each(lambda a, b, s: pltpu.make_async_copy(a, b, s).start())
    for c in put_own(mine_qkv, mine_out):
        c.wait()
    for side, ref in ((0, own_ref), (1, far_ref)):
        pltpu.make_async_copy(ref, ref, sem.at[4 + side]).wait()


def any_specs(n):
    return [pl.BlockSpec(memory_space=pl.ANY)] * n


def place_attention_call(size, sec, at, mine_qkv, swap_qkv, mine_out, swap_out, own, far):
    width = mine_qkv.shape[0]
    return pl.pallas_call(
        functools.partial(place_attention_body, size),
        in_specs=[pl.BlockSpec(memory_space=pltpu.SMEM)] * 2 + any_specs(6),
        out_specs=[pl.BlockSpec(memory_space=pltpu.VMEM)] * 2,
        out_shape=[
            jax.ShapeDtypeStruct((width, 3 * width), bf16),
            jax.ShapeDtypeStruct((width, width), bf16),
        ],
        scratch_shapes=[pltpu.SemaphoreType.DMA((6,))],
        compiler_params=params(),
        cost_estimate=cost(0, 16 * width * width),
        name="place_attention",
    )(sec, at, mine_qkv, swap_qkv, mine_out, swap_out, own, far)


def place_mlp_body(
    size, direct, sec_ref, at_ref, mine_up, swap_up, mine_down, swap_down, own_ref, far_ref,
    up_ref, down_ref, sem,
):
    layer, sec = at_ref[size], sec_ref[0]
    units = up_ref.shape[1] // 2

    def put_own(up, down):
        yield pltpu.make_async_copy(up, up_ref.at[:, :units], sem.at[0])
        yield pltpu.make_async_copy(down, down_ref.at[:units, :], sem.at[1])

    @pl.when(layer == sec)
    def _():
        for c in put_own(mine_up, mine_down):
            c.start()

    @pl.when(layer != sec)
    def _():
        for c in put_own(swap_up, swap_down):
            c.start()

    rows = units // 2 if direct else units // size // 2

    def body(slot, _):
        place = 0 if direct else at_ref[slot]
        for side, ref in ((0, own_ref), (1, far_ref)):
            core = lax.rem(sec + side, 2)
            source = slot * 2 * rows
            row = place * 2 * rows + core * rows
            pltpu.make_async_copy(
                ref.at[pl.ds(source, rows), :],
                up_ref.at[pl.ds(row, rows), units:],
                sem.at[2 + side],
            ).start()
            pltpu.make_async_copy(
                ref.at[pl.ds(source + rows, rows), :],
                down_ref.at[pl.ds(units + row, rows), :],
                sem.at[2 + side],
            ).start()
        return 0

    lax.fori_loop(0, 1 if direct else size, body, 0)
    for c in put_own(mine_up, mine_down):
        c.wait()
    for side, ref in ((0, own_ref), (1, far_ref)):
        pltpu.make_async_copy(ref, ref, sem.at[2 + side]).wait()


def place_mlp_call(size, direct, sec, at, mine_up, swap_up, mine_down, swap_down, own, far):
    width, units = mine_up.shape
    return pl.pallas_call(
        functools.partial(place_mlp_body, size, direct),
        in_specs=[pl.BlockSpec(memory_space=pltpu.SMEM)] * 2 + any_specs(6),
        out_specs=[pl.BlockSpec(memory_space=pltpu.VMEM)] * 2,
        out_shape=[
            jax.ShapeDtypeStruct((width, 2 * units), bf16),
            jax.ShapeDtypeStruct((2 * units, width), bf16),
        ],
        scratch_shapes=[pltpu.SemaphoreType.DMA((4,))],
        compiler_params=params(),
        cost_estimate=cost(0, 16 * width * units),
        name="place_mlp",
    )(sec, at, mine_up, swap_up, mine_down, swap_down, own, far)


def final_mlp_body(
    sec_ref, own0, far0, own1, far1, down_ref, up_ref, held, sem
):
    sec = sec_ref[0]
    whole = held.shape[1]

    def start(own, far):
        for side, ref in ((0, own), (1, far)):
            pltpu.make_async_copy(ref, held.at[side], sem.at[side]).start()

    @pl.when(sec == 0)
    def _():
        start(own0, far0)

    @pl.when(sec != 0)
    def _():
        start(own1, far1)

    half = whole // 2
    for side in range(2):
        pltpu.make_async_copy(own0, held.at[side], sem.at[side]).wait()
    for side in range(2):
        at = pl.multiple_of(lax.rem(sec + side, 2) * half, half)
        down_ref[pl.ds(at, half), :] = held[side, :half, :].astype(f32)
        up_ref[pl.ds(at, half), :] = held[side, half:, :].astype(f32)


def final_mlp_call(sec, own0, far0, own1, far1):
    whole, width = own0.shape
    return pl.pallas_call(
        final_mlp_body,
        in_specs=[pl.BlockSpec(memory_space=pltpu.SMEM)] + any_specs(4),
        out_specs=[pl.BlockSpec(memory_space=pltpu.VMEM)] * 2,
        out_shape=[jax.ShapeDtypeStruct((whole, width), f32)] * 2,
        scratch_shapes=[
            pltpu.VMEM((2, whole, width), bf16),
            pltpu.SemaphoreType.DMA((2,)),
        ],
        compiler_params=params(),
        cost_estimate=cost(0, 12 * whole * width),
        name="final_mlp",
    )(sec, own0, far0, own1, far1)


def final_attention_body(
    sec_ref, own0, far0, own1, far1, out_ref, qkv_ref, held, sem
):
    sec = sec_ref[0]
    whole = held.shape[1]

    def start(own, far):
        for side, ref in ((0, own), (1, far)):
            pltpu.make_async_copy(ref, held.at[side], sem.at[side]).start()

    @pl.when(sec == 0)
    def _():
        start(own0, far0)

    @pl.when(sec != 0)
    def _():
        start(own1, far1)

    first = out_ref.shape[0] // 2
    local = qkv_ref.shape[2]
    deep = qkv_ref.shape[1] // 4
    for side in range(2):
        pltpu.make_async_copy(own0, held.at[side], sem.at[side]).wait()
    for side in range(2):
        core = lax.rem(sec + side, 2)
        at = pl.multiple_of(core * first, first)
        out_ref[pl.ds(at, first), :] = held[side, :first, :].astype(f32)
        low = pl.multiple_of(core * 2 * deep, 2 * deep)
        for j in range(3):
            block = held[side, first + j * deep : first + (j + 1) * deep, :].astype(f32)
            qkv_ref[j, pl.ds(low, deep), :] = block[:, :local]
            qkv_ref[j, pl.ds(low + deep, deep), :] = block[:, local:]


def final_attention_call(sec, own0, far0, own1, far1):
    whole, width = own0.shape
    local = width // 2
    return pl.pallas_call(
        final_attention_body,
        in_specs=[pl.BlockSpec(memory_space=pltpu.SMEM)] + any_specs(4),
        out_specs=[pl.BlockSpec(memory_space=pltpu.VMEM)] * 2,
        out_shape=[
            jax.ShapeDtypeStruct((local, width), f32),
            jax.ShapeDtypeStruct((3, width, local), f32),
        ],
        scratch_shapes=[
            pltpu.VMEM((2, whole, width), bf16),
            pltpu.SemaphoreType.DMA((2,)),
        ],
        compiler_params=params(),
        cost_estimate=cost(0, 12 * whole * width),
        name="final_attention",
    )(sec, own0, far0, own1, far1)


def series_starts(lengths, rows):
    ends = jnp.cumsum(lengths)
    places = jnp.arange(rows, dtype=jnp.int32)
    passed = jnp.where(ends[None, :] <= places[:, None], ends[None, :], 0)
    return jnp.max(passed, axis=1, keepdims=True).astype(jnp.int32)


def per_device(tokens, lengths, w_qkv, w_out, w_up, w_down, norm_gain, norm_bias, cotangent):
    sec = lax.axis_index("section")
    tensor = lax.axis_index("tensor")
    rank = lax.axis_index("dp")
    count = lax.axis_size("dp")
    own_rows = tokens.shape[1]
    rows = 2 * own_rows
    width = tokens.shape[2]
    local = width // 2
    swap = [(0, 1), (1, 0)]
    size, walk = ring_places(count)
    up, down = ring_routes(count)
    place = jnp.asarray(np.argsort(walk), jnp.int32)[lax.rem(rank, size)]
    slots = slot_places(place, size)
    sec_one = sec.astype(jnp.int32).reshape(1)
    bits = own_bits(sec, rank, count)
    at_layer = [
        jnp.concatenate([slots, jnp.full((1,), layer, jnp.int32)]) for layer in range(2)
    ]

    def across(shard):
        other = lax.ppermute(shard, "tensor", swap)
        return jnp.where(
            tensor == 0,
            jnp.concatenate([shard, other], axis=0),
            jnp.concatenate([other, shard], axis=0),
        )

    def to_other_core(value):
        return lax.ppermute(value, "section", swap)

    mine = (w_qkv[0].reshape(width, 3 * local), w_out[0], w_up[0], w_down[0])
    u0 = across(lax.dynamic_index_in_dim(tokens, sec, 0, False))
    gy1 = across(lax.dynamic_index_in_dim(cotangent, sec, 0, False))
    start = series_starts(lax.dynamic_index_in_dim(lengths[0], sec, 0, False), rows)
    norms = jnp.concatenate([norm_gain[0], norm_bias[0]], axis=0)
    swap_norms = to_other_core(norms)
    norm_of = [
        jnp.where(sec == 0, norms, swap_norms),
        jnp.where(sec == 0, swap_norms, norms),
    ]

    step = width // size
    fine = step // 2

    def attention_piece(core):
        low = place * step + core * fine
        q, k, v = (
            lax.dynamic_slice(mine[0], (low, j * local), (fine, local)) for j in range(3)
        )
        out = lax.dynamic_slice_in_dim(
            mine[1], place * (step // 2) + core * (fine // 2), fine // 2, 0
        )
        return jnp.concatenate(
            [
                jnp.concatenate([q, k], axis=1),
                jnp.concatenate([v[: fine // 2], v[fine // 2 :]], axis=1),
                out,
            ],
            axis=0,
        )

    def mlp_piece(core, pieces):
        span = width // pieces
        low = (place if pieces > 1 else 0) * span + core * (span // 2)
        return jnp.concatenate(
            [
                lax.dynamic_slice_in_dim(mine[2], low, span // 2, 0),
                lax.dynamic_slice_in_dim(mine[3], low, span // 2, 0),
            ],
            axis=0,
        )

    def shares(make):
        kept = make(sec)
        came = to_other_core(make(1 - sec))
        return jnp.where(sec == 0, kept, came), jnp.where(sec == 0, came, kept)

    attention_share = shares(attention_piece)
    mlp_share = shares(lambda core: mlp_piece(core, size))
    direct_share = shares(lambda core: mlp_piece(core, 1))

    def through_ring(piece):
        crossed = lax.ppermute(piece, "tensor", swap)
        own = ring_gather(crossed, up, down, size)
        return own, to_other_core(own)

    swapped = tuple(to_other_core(w) for w in mine)

    weights = []
    for layer in range(2):
        own, far = through_ring(attention_share[layer])
        qkv_full, out_full = place_attention_call(
            size, sec_one, at_layer[layer], mine[0], swapped[0], mine[1], swapped[1], own, far
        )
        if layer == 0:
            own, far = through_ring(mlp_share[layer])
        else:
            own = lax.ppermute(direct_share[layer], "tensor", swap)
            far = to_other_core(own)
        up_full, down_full = place_mlp_call(
            size, layer == 1, sec_one, at_layer[layer], mine[2], swapped[2], mine[3], swapped[3], own, far
        )
        weights.append((qkv_full, out_full, up_full, down_full))

    kept = []
    u = u0
    layer_out = []
    for layer in range(2):
        qkv_full, out_full, up_full, down_full = weights[layer]
        norm = norm_of[layer]
        n1, qkv = qkv_call(u, norm[0:1], norm[2:3], qkv_full)
        o, h, n2 = attention_call(qkv, start, out_full, u, norm[1:2], norm[3:4])
        z, slope, y = mlp_call(n2, h, up_full, down_full)
        kept.append((u, n1, qkv, o, h, n2, z, slope))
        layer_out.append(y)
        u = y

    gy = gy1
    totals = [None, None]
    norm_grads = [None, None]
    grad_in = [None, None]
    for layer in (1, 0):
        qkv_full, out_full, up_full, down_full = weights[layer]
        norm = norm_of[layer]
        u, n1, qkv, o, h, n2, z, slope = kept[layer]
        da, dh, gh, grads_two = mlp_back_call(gy, slope, up_full, down_full, h, norm[1:2])
        both = mlp_grads_call(sec_one, z, gy, n2, da)
        mlp_total = doubling_gather(
            halving_sum(both[1], to_other_core(both[0]), bits, count), bits, count
        )
        gh = lax.optimization_barrier((gh, both))[0]
        dq, dk, dv = attention_back_call(qkv, start, gh, out_full)
        both = attention_grads_call(sec_one, o, gh, n1, dq, dk, dv)
        attention_total = doubling_gather(
            halving_sum(both[1], to_other_core(both[0]), bits, count), bits, count
        )
        dh = lax.optimization_barrier((dh, both))[0]
        du, grads_one = input_back_call(dq, dk, dv, qkv_full, dh, u, norm[0:1])
        send = [(1 - layer, layer)]
        totals[layer] = (
            mlp_total,
            lax.ppermute(mlp_total, "section", send),
            attention_total,
            lax.ppermute(attention_total, "section", send),
        )
        norm_grads[layer] = jnp.concatenate([grads_one[:1], grads_two[:1], grads_one[1:], grads_two[1:]])
        grad_in[layer] = du
        gy = du

    grad_down, grad_up = final_mlp_call(
        sec_one, totals[0][0], totals[0][1], totals[1][0], totals[1][1]
    )
    grad_out, grad_qkv = final_attention_call(
        sec_one, totals[0][2], totals[0][3], totals[1][2], totals[1][3]
    )

    def butterfly(part):
        part = part + to_other_core(part)
        distance = 1
        while distance < count:
            part = part + lax.ppermute(part, "dp", [(i, i ^ distance) for i in range(count)])
            distance *= 2
        return part

    norm_total = [butterfly(part) for part in norm_grads]
    norm_sum = jnp.where(sec == 0, norm_total[0], norm_total[1])
    norm_sum = lax.dynamic_slice_in_dim(norm_sum, tensor * local, local, 1)

    def to_outputs(pair):
        rows_of = [
            lax.dynamic_slice_in_dim(value, tensor * own_rows, own_rows, 0) for value in pair
        ]
        stay = jnp.where(sec == 0, rows_of[0], rows_of[1])
        go = jnp.where(sec == 0, rows_of[1], rows_of[0])
        came = to_other_core(go)
        return jnp.where(sec == 0, jnp.stack([stay, came]), jnp.stack([came, stay]))[None]

    return (
        to_outputs(layer_out),
        to_outputs(grad_in),
        jnp.transpose(grad_qkv, (1, 0, 2))[None],
        grad_out[None],
        grad_up[None],
        grad_down[None],
        norm_sum[None, :2],
        norm_sum[None, 2:],
    )


def solution(mesh):
    in_specs = (
        P(None, ("dp", "tensor"), None),
        P("dp", None, None),
        P("section", None, None, "tensor"),
        P("section", "tensor", None),
        P("section", None, "tensor"),
        P("section", "tensor", None),
        P("section", None, None),
        P("section", None, None),
        P(None, ("dp", "tensor"), None),
    )
    out_specs = (
        P("section", None, ("dp", "tensor"), None),
        P("section", None, ("dp", "tensor"), None),
        P("section", None, None, "tensor"),
        P("section", "tensor", None),
        P("section", None, "tensor"),
        P("section", "tensor", None),
        P("section", None, "tensor"),
        P("section", None, "tensor"),
    )
    return jax.shard_map(
        per_device, mesh=mesh, in_specs=in_specs, out_specs=out_specs, check_vma=False
    )
```

time: 1310 us -> 664 us (0.51)
  waiting for transfers between devices: 905 us -> 243 us
  Pallas kernels: 0 us -> 218 us
  matrix products: 211 us -> 0 us
  starting transfers between devices: 8.6 us -> 91.8 us
  other arithmetic: 71.9 us -> 44.6 us
  blocking collectives: 22.1 us -> 0 us
    psum x1 -> x0, waiting for transfers between devices: 495 us -> none  [per_device(): lax.psum((part_qkv, part_out, part_up, part_down, norm_local), 'dp')]
    ppermute x4 -> x84, waiting for transfers between devices: 6.87 us -> 243 us  [the longest x12 76.2 us: doubling_gather(): away = lax.ppermute(held, ('section', 'dp'), pairs_of(count, step))]
    all_gather x12 -> x0, waiting for transfers between devices: 218 us -> none  [the longest x6 109 us: gather_grads(): return lax.all_gather(shard, 'tensor', axis=0, tiled=True)]
    pallas_call x0 -> x22, Pallas kernels: none -> 218 us  [the longest x2 37.7 us: attention_back_call(): pl.pallas_call(functools.partial(attention_back_body, heads), grid=(steps...]
    dot_general x57 -> x0, matrix products: 211 us -> none  [the longest x3 25.4 us: layer_backward(): jnp.einsum('hts,shd->thd', score_grad, key_rows, preferred_element_type=j...]
    reduce_scatter x12 -> x0, waiting for transfers between devices: 180 us -> none  [the longest x6 98.7 us: sum_partials(): lax.psum_scatter(term_rows.astype(jnp.bfloat16), 'tensor', scatter_dimens...]
    ppermute x4 -> x84, starting transfers between devices: 5.94 us -> 91.8 us  [the longest x12 17 us: doubling_gather(): away = lax.ppermute(held, ('section', 'dp'), pairs_of(count, step))]
    reduce_sum x22 -> x0, other arithmetic: 28.6 us -> none  [the longest x6 14.1 us: normalize_back(): jnp.sum(incoming * unit_rows, axis=0)]
  transfers between devices with their start and end apart: 30 -> 84, of which waited for: 27 -> 47; matrix products, arithmetic and copies ran while one was open for 10% -> 11% of each run, Pallas kernels for 0% -> 15%
where the time goes in v1:
time: 664 us; the launch traced here: 656 us
  waiting for transfers between devices  243 us (37%)
  Pallas kernels  218 us (33%)
  starting transfers between devices  91.8 us (14%)
  local copies, waits for them, and re-layouts  55.7 us (8%)
  other arithmetic  44.6 us (7%)
    ppermute x12, waiting for transfers between devices, doubling_gather(): away = lax.ppermute(held, ('section', 'dp'), pairs_of(count, step))  76.2 us
    ppermute x8, waiting for transfers between devices, halving_sum(): away = lax.ppermute(send, ('section', 'dp'), pairs_of(count, step))  42.4 us
    ppermute x4, waiting for transfers between devices, halving_sum(): lax.ppermute(both(1 - bits[0]).astype(bf16), ('section', 'dp'), pairs_of(...  40.7 us
    pallas_call x2, Pallas kernels, attention_back_call(): pl.pallas_call(functools.partial(attention_back_body, heads), grid=(steps...  37.7 us
    pallas_call x2, Pallas kernels, mlp_back_call(): pl.pallas_call(mlp_back_body, grid=(units // tile,), in_specs=[pl.BlockSp...  26.2 us
    pallas_call x2, Pallas kernels, attention_call(): pl.pallas_call(functools.partial(attention_body, heads), grid=(steps,), i...  26.1 us
    ppermute x9, waiting for transfers between devices, ring_gather(): downs.append(lax.ppermute(downs[-1], 'dp', down))  23.9 us
    pallas_call x2, Pallas kernels, mlp_call(): pl.pallas_call(mlp_body, grid=(units // tile,), in_specs=[pl.BlockSpec((r...  23.2 us
  transfers between devices with their start and end apart: 84, of which 47 were waited for; matrix products, arithmetic and copies ran while one was open for 11% of the time, Pallas kernels for 15%

profile of v1, /device:TPU:0, one launch (start us, length us, event | category | flops | bytes accessed | tf_op | source)
XLA Modules:
  0.0 655.7 jit_solution(2942839966611880604)
XLA Ops:
  3.3 4.6 copy.36
  8.0 4.8 copy.44.mine_qkv
  30.3 11.7 %collective-permute-done.28 = bf16[128,1024]{1,0:T(8,128)(2,1)S(1)} collective-permute-done((bf16[128,1024]{1,0:T(8,128)(2,1)S(1)}, bf16[128,1024]{1,0:T(8,128)(2,1)S(1)}, u32[]{:S(2)}, u32[]{:S(2)}) %collective-permute-start.28) | collective-permute-done | bytes 262176 | tf_op jit(solution)/shard_map/ppermute | solution.py:930
  64.6 4.7 collective-permute-done.22
  88.7 6.5 collective-permute-done.10
  149.6 7.4 %place_attention.3 = (bf16[1024,3072]{1,0:T(8,128)(2,1)}, bf16[1024,1024]{1,0:T(8,128)(2,1)}) custom-call(s32[1]{0:T(128)} %bitcast.3.sec_ref, s32[9]{0:T(128)} %get-tuple-element.184.at_ref, bf16[1024,1536]{1,0:T(8,128)(2,1)} %copy.44.mine_qkv, bf16[1024,1536]{1,0:T(8,128)(2,1)} %copy-done.6, bf16[512,1024]{1,0:T(8,128)(2,1)} %bitcast.87, ...), custom_call_target="tpu_custom_call" | custom-call | bytes 16777216 | tf_op jit(solution)/shard_map/place_attention/pallas_call | solution.py:661
  157.0 7.6 %place_attention.2 = (bf16[1024,3072]{1,0:T(8,128)(2,1)}, bf16[1024,1024]{1,0:T(8,128)(2,1)}) custom-call(s32[1]{0:T(128)} %bitcast.3.sec_ref, s32[9]{0:T(128)} %get-tuple-element.185.at_ref, bf16[1024,1536]{1,0:T(8,128)(2,1)} %copy.44.mine_qkv, bf16[1024,1536]{1,0:T(8,128)(2,1)} %copy-done.6, bf16[512,1024]{1,0:T(8,128)(2,1)} %bitcast.88, ...), custom_call_target="tpu_custom_call" | custom-call | bytes 16777216 | tf_op jit(solution)/shard_map/place_attention/pallas_call | solution.py:661
  164.6 7.5 %place_mlp.2 = (bf16[1024,2048]{1,0:T(8,128)(2,1)}, bf16[2048,1024]{1,0:T(8,128)(2,1)}) custom-call(s32[1]{0:T(128)} %bitcast.3.sec_ref, s32[9]{0:T(128)} %get-tuple-element.185.at_ref, bf16[1024,1024]{1,0:T(8,128)(2,1)} %bitcast.83, bf16[1024,1024]{1,0:T(8,128)(2,1)} %collective-permute-done.15.swap_up, bf16[1024,1024]{1,0:T(8,128)(2,1)} %bitcast.12.mine_down, ...), custom_call_target="tpu_custom_call" | custom-call | bytes 16777216 | tf_op jit(solution)/shard_map/place_mlp/pallas_call | solution.py:726
  172.1 9.0 %qkv.2 = (bf16[512,1024]{1,0:T(8,128)(2,1)}, bf16[512,3072]{1,0:T(8,128)(2,1)}) custom-call(bf16[512,1024]{1,0:T(8,128)(2,1)} %maximum_select_fusion.1.u_ref, f32[1,1024]{1,0:T(1,128)} %get-tuple-element.173.gain_ref, f32[1,1024]{1,0:T(1,128)} %get-tuple-element.172.bias_ref, bf16[1024,3072]{1,0:T(8,128)(2,1)} %get-tuple-element.58.w_ref.wq_ref.wk_ref.wv_ref), custom_call_target="tpu_custom_call" | custom-call | flops 3221225472 | bytes 9437184 | tf_op jit(solution)/shard_map/qkv/pallas_call | solution.py:82
  181.1 5.7 collective-permute-done.39.own_ref
  186.9 13.1 %attention.2 = (bf16[512,1024]{1,0:T(8,128)(2,1)}, f32[512,1024]{1,0:T(8,128)}, bf16[512,1024]{1,0:T(8,128)(2,1)}) custom-call(bf16[512,3072]{1,0:T(8,128)(2,1)} %get-tuple-element.59.q_ref.k_ref.v_ref, bf16[512,3072]{1,0:T(8,128)(2,1)} %get-tuple-element.59.q_ref.k_ref.v_ref, bf16[512,3072]{1,0:T(8,128)(2,1)} %get-tuple-element.59.q_ref.k_ref.v_ref, ...), custom_call_target="tpu_custom_call" | custom-call | flops 8000000000 | bytes 10000000 | tf_op jit(solution)/shard_map/attention/pallas_call | solution.py:154
  199.9 11.6 %mlp.2 = (bf16[512,2048]{1,0:T(8,128)(2,1)}, bf16[512,2048]{1,0:T(8,128)(2,1)}, bf16[512,1024]{1,0:T(8,128)(2,1)}) custom-call(bf16[512,1024]{1,0:T(8,128)(2,1)} %get-tuple-element.61.n2_ref, f32[512,1024]{1,0:T(8,128)} %get-tuple-element.62.h_ref, bf16[1024,2048]{1,0:T(8,128)(2,1)} %get-tuple-element.63.up_ref, bf16[2048,1024]{1,0:T(8,128)(2,1)} %get-tuple-element.64.down_ref), custom_call_target="tpu_custom_call" | custom-call | flops 4294967296 | bytes 16777216 | tf_op jit(solution)/shard_map/mlp/pallas_call | solution.py:213
  211.5 9.1 %qkv.3 = (bf16[512,1024]{1,0:T(8,128)(2,1)}, bf16[512,3072]{1,0:T(8,128)(2,1)}) custom-call(bf16[512,1024]{1,0:T(8,128)(2,1)} %get-tuple-element.65.u_ref, f32[1,1024]{1,0:T(1,128)} %get-tuple-element.169.gain_ref, f32[1,1024]{1,0:T(1,128)} %get-tuple-element.168.bias_ref, bf16[1024,3072]{1,0:T(8,128)(2,1)} %get-tuple-element.66.w_ref.wq_ref.wk_ref.wv_ref), custom_call_target="tpu_custom_call" | custom-call | flops 3221225472 | bytes 9437184 | tf_op jit(solution)/shard_map/qkv/pallas_call | solution.py:82
  220.6 13.0 %attention.3 = (bf16[512,1024]{1,0:T(8,128)(2,1)}, f32[512,1024]{1,0:T(8,128)}, bf16[512,1024]{1,0:T(8,128)(2,1)}) custom-call(bf16[512,3072]{1,0:T(8,128)(2,1)} %get-tuple-element.67.q_ref.k_ref.v_ref, bf16[512,3072]{1,0:T(8,128)(2,1)} %get-tuple-element.67.q_ref.k_ref.v_ref, bf16[512,3072]{1,0:T(8,128)(2,1)} %get-tuple-element.67.q_ref.k_ref.v_ref, ...), custom_call_target="tpu_custom_call" | custom-call | flops 8000000000 | bytes 10000000 | tf_op jit(solution)/shard_map/attention/pallas_call | solution.py:154
  235.1 7.3 %place_mlp.3 = (bf16[1024,2048]{1,0:T(8,128)(2,1)}, bf16[2048,1024]{1,0:T(8,128)(2,1)}) custom-call(s32[1]{0:T(128)} %bitcast.3.sec_ref, s32[9]{0:T(128)} %get-tuple-element.184.at_ref, bf16[1024,1024]{1,0:T(8,128)(2,1)} %bitcast.84, bf16[1024,1024]{1,0:T(8,128)(2,1)} %collective-permute-done.15.swap_up, bf16[1024,1024]{1,0:T(8,128)(2,1)} %bitcast.12.mine_down, ...), custom_call_target="tpu_custom_call" | custom-call | bytes 16777216 | tf_op jit(solution)/shard_map/place_mlp/pallas_call | solution.py:726
  242.4 11.6 %mlp.3 = (bf16[512,2048]{1,0:T(8,128)(2,1)}, bf16[512,2048]{1,0:T(8,128)(2,1)}, bf16[512,1024]{1,0:T(8,128)(2,1)}) custom-call(bf16[512,1024]{1,0:T(8,128)(2,1)} %get-tuple-element.69.n2_ref, f32[512,1024]{1,0:T(8,128)} %get-tuple-element.70.h_ref, bf16[1024,2048]{1,0:T(8,128)(2,1)} %get-tuple-element.71.up_ref, bf16[2048,1024]{1,0:T(8,128)(2,1)} %get-tuple-element.72.down_ref), custom_call_target="tpu_custom_call" | custom-call | flops 4294967296 | bytes 16777216 | tf_op jit(solution)/shard_map/mlp/pallas_call | solution.py:213
  254.0 13.2 %mlp_back.2 = (bf16[512,2048]{1,0:T(8,128)(2,1)}, f32[512,1024]{1,0:T(8,128)}, bf16[512,1024]{1,0:T(8,128)(2,1)}, f32[2,1024]{1,0:T(2,128)}) custom-call(bf16[512,1024]{1,0:T(8,128)(2,1)} %maximum_select_fusion.3.gy_ref, bf16[512,2048]{1,0:T(8,128)(2,1)} %get-tuple-element.74.slope_ref, bf16[1024,2048]{1,0:T(8,128)(2,1)} %get-tuple-element.71.up_ref, ...), custom_call_target="tpu_custom_call" | custom-call | flops 4294967296 | bytes 16777216 | tf_op jit(solution)/shard_map/mlp_back/pallas_call | solution.py:270
  267.2 5.9 mlp_grads.2
  277.0 18.7 %attention_back.2 = (bf16[512,1024]{1,0:T(8,128)(2,1)}, bf16[512,1024]{1,0:T(8,128)(2,1)}, bf16[512,1024]{1,0:T(8,128)(2,1)}) custom-call(bf16[512,3072]{1,0:T(8,128)(2,1)} %get-tuple-element.67.q_ref.k_ref.v_ref, bf16[512,3072]{1,0:T(8,128)(2,1)} %get-tuple-element.67.q_ref.k_ref.v_ref, bf16[512,3072]{1,0:T(8,128)(2,1)} %get-tuple-element.67.q_ref.k_ref.v_ref, ...), custom_call_target="tpu_custom_call" | custom-call | flops 12000000000 | bytes 10000000 | tf_op jit(solution)/shard_map/attention_back/pallas_call | solution.py:373
  295.8 5.9 attention_grads.2
  301.7 10.4 %input_back.2 = (bf16[512,1024]{1,0:T(8,128)(2,1)}, f32[2,1024]{1,0:T(2,128)}) custom-call(bf16[512,1024]{1,0:T(8,128)(2,1)} %get-tuple-element.79.dq_ref, bf16[512,1024]{1,0:T(8,128)(2,1)} %get-tuple-element.80.dk_ref, bf16[512,1024]{1,0:T(8,128)(2,1)} %get-tuple-element.81.dv_ref, bf16[1024,3072]{1,0:T(8,128)(2,1)} %get-tuple-element.66.w_ref.wq_ref.wk_ref.wv_ref, ...), custom_call_target="tpu_custom_call" | custom-call | flops 3221225472 | bytes 10485760 | tf_op jit(solution)/shard_map/input_back/pallas_call | solution.py:466
  312.1 13.0 %mlp_back.3 = (bf16[512,2048]{1,0:T(8,128)(2,1)}, f32[512,1024]{1,0:T(8,128)}, bf16[512,1024]{1,0:T(8,128)(2,1)}, f32[2,1024]{1,0:T(2,128)}) custom-call(bf16[512,1024]{1,0:T(8,128)(2,1)} %get-tuple-element.86.gy_ref, bf16[512,2048]{1,0:T(8,128)(2,1)} %get-tuple-element.87.slope_ref, bf16[1024,2048]{1,0:T(8,128)(2,1)} %get-tuple-element.63.up_ref, ...), custom_call_target="tpu_custom_call" | custom-call | flops 4294967296 | bytes 16777216 | tf_op jit(solution)/shard_map/mlp_back/pallas_call | solution.py:270
  325.0 5.8 mlp_grads.3
  330.9 18.9 %attention_back.3 = (bf16[512,1024]{1,0:T(8,128)(2,1)}, bf16[512,1024]{1,0:T(8,128)(2,1)}, bf16[512,1024]{1,0:T(8,128)(2,1)}) custom-call(bf16[512,3072]{1,0:T(8,128)(2,1)} %get-tuple-element.59.q_ref.k_ref.v_ref, bf16[512,3072]{1,0:T(8,128)(2,1)} %get-tuple-element.59.q_ref.k_ref.v_ref, bf16[512,3072]{1,0:T(8,128)(2,1)} %get-tuple-element.59.q_ref.k_ref.v_ref, ...), custom_call_target="tpu_custom_call" | custom-call | flops 12000000000 | bytes 10000000 | tf_op jit(solution)/shard_map/attention_back/pallas_call | solution.py:373
  356.5 5.8 attention_grads.3
  362.3 4.7 fusion.22
  367.5 10.5 %input_back.3 = (bf16[512,1024]{1,0:T(8,128)(2,1)}, f32[2,1024]{1,0:T(2,128)}) custom-call(bf16[512,1024]{1,0:T(8,128)(2,1)} %get-tuple-element.92.dq_ref, bf16[512,1024]{1,0:T(8,128)(2,1)} %get-tuple-element.93.dk_ref, bf16[512,1024]{1,0:T(8,128)(2,1)} %get-tuple-element.94.dv_ref, bf16[1024,3072]{1,0:T(8,128)(2,1)} %get-tuple-element.58.w_ref.wq_ref.wk_ref.wv_ref, ...), custom_call_target="tpu_custom_call" | custom-call | flops 3221225472 | bytes 10485760 | tf_op jit(solution)/shard_map/input_back/pallas_call | solution.py:466
  389.5 6.0 collective-permute-done.69
  398.8 8.0 %collective-permute-done.61 = bf16[512,1024]{1,0:T(8,128)(2,1)S(1)} collective-permute-done((bf16[512,1024]{1,0:T(8,128)(2,1)S(1)}, bf16[512,1024]{1,0:T(8,128)(2,1)S(1)}, u32[]{:S(2)}, u32[]{:S(2)}) %collective-permute-start.61) | collective-permute-done | bytes 1048608 | tf_op jit(solution)/shard_map/ppermute | solution.py:559
  410.2 13.4 %collective-permute-done.53 = bf16[512,1024]{1,0:T(8,128)(2,1)S(1)} collective-permute-done((bf16[512,1024]{1,0:T(8,128)(2,1)S(1)}, bf16[512,1024]{1,0:T(8,128)(2,1)S(1)}, u32[]{:S(2)}, u32[]{:S(2)}) %collective-permute-start.53) | collective-permute-done | bytes 1048608 | tf_op jit(solution)/shard_map/ppermute | solution.py:559
  427.1 13.4 %collective-permute-done.45 = bf16[512,1024]{1,0:T(8,128)(2,1)S(1)} collective-permute-done((bf16[512,1024]{1,0:T(8,128)(2,1)S(1)}, bf16[512,1024]{1,0:T(8,128)(2,1)S(1)}, u32[]{:S(2)}, u32[]{:S(2)}) %collective-permute-start.45) | collective-permute-done | bytes 1048608 | tf_op jit(solution)/shard_map/ppermute | solution.py:559
  447.6 5.7 collective-permute-done.54
  456.1 8.4 %collective-permute-done.46 = bf16[256,1024]{1,0:T(8,128)(2,1)S(1)} collective-permute-done((bf16[256,1024]{1,0:T(8,128)(2,1)S(1)}, bf16[256,1024]{1,0:T(8,128)(2,1)S(1)}, u32[]{:S(2)}, u32[]{:S(2)}) %collective-permute-start.46) | collective-permute-done | bytes 524320 | tf_op jit(solution)/shard_map/ppermute | solution.py:565
  471.7 10.7 %collective-permute-done.63 = bf16[128,1024]{1,0:T(8,128)(2,1)S(1)} collective-permute-done((bf16[128,1024]{1,0:T(8,128)(2,1)S(1)}, bf16[128,1024]{1,0:T(8,128)(2,1)S(1)}, u32[]{:S(2)}, u32[]{:S(2)}) %collective-permute-start.63) | collective-permute-done | bytes 262176 | tf_op jit(solution)/shard_map/ppermute | solution.py:565
  482.4 8.3 %collective-permute-done.55 = bf16[128,1024]{1,0:T(8,128)(2,1)S(1)} collective-permute-done((bf16[128,1024]{1,0:T(8,128)(2,1)S(1)}, bf16[128,1024]{1,0:T(8,128)(2,1)S(1)}, u32[]{:S(2)}, u32[]{:S(2)}) %collective-permute-start.55) | collective-permute-done | bytes 262176 | tf_op jit(solution)/shard_map/ppermute | solution.py:565
  490.9 8.3 %collective-permute-done.47 = bf16[128,1024]{1,0:T(8,128)(2,1)S(1)} collective-permute-done((bf16[128,1024]{1,0:T(8,128)(2,1)S(1)}, bf16[128,1024]{1,0:T(8,128)(2,1)S(1)}, u32[]{:S(2)}, u32[]{:S(2)}) %collective-permute-start.47) | collective-permute-done | bytes 262176 | tf_op jit(solution)/shard_map/ppermute | solution.py:565
  499.3 8.3 %collective-permute-done.72 = bf16[128,1024]{1,0:T(8,128)(2,1)S(1)} collective-permute-done((bf16[128,1024]{1,0:T(8,128)(2,1)S(1)}, bf16[128,1024]{1,0:T(8,128)(2,1)S(1)}, u32[]{:S(2)}, u32[]{:S(2)}) %collective-permute-start.72) | collective-permute-done | bytes 262176 | tf_op jit(solution)/shard_map/ppermute | solution.py:572
  507.7 8.3 %collective-permute-done.64 = bf16[128,1024]{1,0:T(8,128)(2,1)S(1)} collective-permute-done((bf16[128,1024]{1,0:T(8,128)(2,1)S(1)}, bf16[128,1024]{1,0:T(8,128)(2,1)S(1)}, u32[]{:S(2)}, u32[]{:S(2)}) %collective-permute-start.64) | collective-permute-done | bytes 262176 | tf_op jit(solution)/shard_map/ppermute | solution.py:572
  516.1 11.4 %collective-permute-start.73 = (bf16[256,1024]{1,0:T(8,128)(2,1)S(1)}, bf16[256,1024]{1,0:T(8,128)(2,1)S(1)}, u32[]{:S(2)}, u32[]{:S(2)}) collective-permute-start(bf16[256,1024]{1,0:T(8,128)(2,1)S(1)} %pad_maximum_fusion.12), channel_id=1, source_target_pairs={{0,4},{2,6},{4,0},{6,2},{8,12},{10,14},{12,8},{14,10},{16,18},{18,... | collective-permute-start | bytes 1572872 | tf_op jit(solution)/shard_map/ppermute | solution.py:572
  527.6 5.4 collective-permute-done.56
  537.6 6.7 %collective-permute-done.73 = bf16[256,1024]{1,0:T(8,128)(2,1)S(1)} collective-permute-done((bf16[256,1024]{1,0:T(8,128)(2,1)S(1)}, bf16[256,1024]{1,0:T(8,128)(2,1)S(1)}, u32[]{:S(2)}, u32[]{:S(2)}) %collective-permute-start.73) | collective-permute-done | bytes 524320 | tf_op jit(solution)/shard_map/ppermute | solution.py:572
  544.6 10.9 %collective-permute-done.65 = bf16[256,1024]{1,0:T(8,128)(2,1)S(1)} collective-permute-done((bf16[256,1024]{1,0:T(8,128)(2,1)S(1)}, bf16[256,1024]{1,0:T(8,128)(2,1)S(1)}, u32[]{:S(2)}, u32[]{:S(2)}) %collective-permute-start.65) | collective-permute-done | bytes 524320 | tf_op jit(solution)/shard_map/ppermute | solution.py:572
  557.2 9.5 %collective-permute-done.57 = bf16[256,1024]{1,0:T(8,128)(2,1)S(1)} collective-permute-done((bf16[256,1024]{1,0:T(8,128)(2,1)S(1)}, bf16[256,1024]{1,0:T(8,128)(2,1)S(1)}, u32[]{:S(2)}, u32[]{:S(2)}) %collective-permute-start.57) | collective-permute-done | bytes 524320 | tf_op jit(solution)/shard_map/ppermute | solution.py:572
  568.5 9.5 %collective-permute-done.49 = bf16[256,1024]{1,0:T(8,128)(2,1)S(1)} collective-permute-done((bf16[256,1024]{1,0:T(8,128)(2,1)S(1)}, bf16[256,1024]{1,0:T(8,128)(2,1)S(1)}, u32[]{:S(2)}, u32[]{:S(2)}) %collective-permute-start.49) | collective-permute-done | bytes 524320 | tf_op jit(solution)/shard_map/ppermute | solution.py:572
  587.2 5.6 collective-permute-done.58
  596.2 7.8 %collective-permute-done.50 = bf16[512,1024]{1,0:T(8,128)(2,1)S(1)} collective-permute-done((bf16[512,1024]{1,0:T(8,128)(2,1)S(1)}, bf16[512,1024]{1,0:T(8,128)(2,1)S(1)}, u32[]{:S(2)}, u32[]{:S(2)}) %collective-permute-start.50) | collective-permute-done | bytes 1048608 | tf_op jit(solution)/shard_map/ppermute | solution.py:572
  643.0 6.0 final_mlp.1
  649.1 6.2 final_attention.1
  (343 shorter events, 226.2 us)
Async XLA Ops:
  20.5 34.9 %collective-permute-start = (bf16[256,1024]{1,0:T(8,128)(2,1)}, bf16[256,1024]{1,0:T(8,128)(2,1)}, u32[]{:S(2)}, u32[]{:S(2)}) collective-permute-start(bf16[256,1024]{1,0:T(8,128)(2,1)} %dynamic-slice_bitcast_fusion.5), channel_id=1, source_target_pairs={{0,1},{1,0},{2,3},{3,2},{4,5},{5,4},{6,7},{7,6},{8,9},{9,8},{10,11... | collective-permute-start | bytes 1572872 | tf_op jit(solution)/shard_map/ppermute | solution.py:868
  24.1 20.1 %collective-permute-start.1 = (f32[4,1024]{1,0:T(4,128)}, f32[4,1024]{1,0:T(4,128)}, u32[]{:S(2)}, u32[]{:S(2)}) collective-permute-start(f32[4,1024]{1,0:T(4,128)} %pad_maximum_fusion.16), channel_id=1, source_target_pairs={{0,16},{16,0},{1,17},{17,1},{2,18},{18,2},{3,19},{19,3},{4,20},{20... | collective-permute-start | bytes 49160 | tf_op jit(solution)/shard_map/ppermute | solution.py:876
  26.3 15.7 %collective-permute-start.28 = (bf16[128,1024]{1,0:T(8,128)(2,1)S(1)}, bf16[128,1024]{1,0:T(8,128)(2,1)S(1)}, u32[]{:S(2)}, u32[]{:S(2)}) collective-permute-start(bf16[128,1024]{1,0:T(8,128)(2,1)S(1)} %get-tuple-element.162), channel_id=1, source_target_pairs={{0,1},{1,0},{2,3},{3,2},{4,5},{5,4},{6,7},{7,6},{8,9},{9,8},{10,11... | collective-permute-start | bytes 786440 | tf_op jit(solution)/shard_map/ppermute | solution.py:930
  26.5 21.2 %collective-permute-start.18 = (bf16[128,1024]{1,0:T(8,128)(2,1)S(1)}, bf16[128,1024]{1,0:T(8,128)(2,1)S(1)}, u32[]{:S(2)}, u32[]{:S(2)}) collective-permute-start(bf16[128,1024]{1,0:T(8,128)(2,1)S(1)} %maximum_select_fusion.5), channel_id=1, source_target_pairs={{0,1},{1,0},{2,3},{3,2},{4,5},{5,4},{6,7},{7,6},{8,9},{9,8},{10,11... | collective-permute-start | bytes 786440 | tf_op jit(solution)/shard_map/ppermute | solution.py:930
  30.2 22.4 %collective-permute-start.5 = (bf16[128,1024]{1,0:T(8,128)(2,1)S(1)}, bf16[128,1024]{1,0:T(8,128)(2,1)S(1)}, u32[]{:S(2)}, u32[]{:S(2)}) collective-permute-start(bf16[128,1024]{1,0:T(8,128)(2,1)S(1)} %get-tuple-element.163), channel_id=1, source_target_pairs={{0,1},{1,0},{2,3},{3,2},{4,5},{5,4},{6,7},{7,6},{8,9},{9,8},{10,11... | collective-permute-start | bytes 786440 | tf_op jit(solution)/shard_map/ppermute | solution.py:930
  52.6 80.5 %collective-permute-start.2 = (bf16[1024,1536]{1,0:T(8,128)(2,1)S(1)}, bf16[1024,1536]{1,0:T(8,128)(2,1)S(1)}, u32[]{:S(2)}, u32[]{:S(2)}) collective-permute-start(bf16[1024,1536]{1,0:T(8,128)(2,1)S(1)} %copy-done.2), channel_id=1, source_target_pairs={{0,16},{16,0},{1,17},{17,1},{2,18},{18,2},{3,19},{19,3},{4,20},{20... | collective-permute-start | bytes 9437192 | tf_op jit(solution)/shard_map/ppermute | solution.py:876
  86.1 46.9 %collective-permute-start.38 = (bf16[1024,1024]{1,0:T(8,128)(2,1)S(1)}, bf16[1024,1024]{1,0:T(8,128)(2,1)S(1)}, u32[]{:S(2)}, u32[]{:S(2)}) collective-permute-start(bf16[1024,1024]{1,0:T(8,128)(2,1)S(1)} %pad_maximum_fusion), channel_id=1, source_target_pairs={{0,16},{16,0},{1,17},{17,1},{2,18},{18,2},{3,19},{19,3},{4,20},{20... | collective-permute-start | bytes 6291464 | tf_op jit(solution)/shard_map/ppermute | solution.py:876
  95.2 42.4 %collective-permute-start.37 = (bf16[1024,1024]{1,0:T(8,128)(2,1)S(1)}, bf16[1024,1024]{1,0:T(8,128)(2,1)S(1)}, u32[]{:S(2)}, u32[]{:S(2)}) collective-permute-start(bf16[1024,1024]{1,0:T(8,128)(2,1)S(1)} %constant_dynamic-update-slice_fusion.18.own_ref), channel_id=1, source_target_pairs={{0,16},{16,0},{1,17},{17,1},{2,18},{18,2},{3,19},{19,3},{4,20},{20... | collective-permute-start | bytes 6291464 | tf_op jit(solution)/shard_map/ppermute | solution.py:876
  110.3 22.2 %collective-permute-start.3 = (bf16[512,1024]{1,0:T(8,128)(2,1)S(1)}, bf16[512,1024]{1,0:T(8,128)(2,1)S(1)}, u32[]{:S(2)}, u32[]{:S(2)}) collective-permute-start(bf16[512,1024]{1,0:T(8,128)(2,1)S(1)} %bitcast.89), channel_id=1, source_target_pairs={{0,16},{16,0},{1,17},{17,1},{2,18},{18,2},{3,19},{19,3},{4,20},{20... | collective-permute-start | bytes 3145736 | tf_op jit(solution)/shard_map/ppermute | solution.py:876
  132.5 32.1 %collective-permute-start.15 = (bf16[1024,1024]{1,0:T(8,128)(2,1)S(1)}, bf16[1024,1024]{1,0:T(8,128)(2,1)}, u32[]{:S(2)}, u32[]{:S(2)}) collective-permute-start(bf16[1024,1024]{1,0:T(8,128)(2,1)S(1)} %bitcast.85), channel_id=1, source_target_pairs={{0,16},{16,0},{1,17},{17,1},{2,18},{18,2},{3,19},{19,3},{4,20},{20... | collective-permute-start | bytes 6291464 | tf_op jit(solution)/shard_map/ppermute | solution.py:876
  132.5 32.0 %collective-permute-start.16 = (bf16[1024,1024]{1,0:T(8,128)(2,1)}, bf16[1024,1024]{1,0:T(8,128)(2,1)}, u32[]{:S(2)}, u32[]{:S(2)}) collective-permute-start(bf16[1024,1024]{1,0:T(8,128)(2,1)} %bitcast.12.mine_down), channel_id=1, source_target_pairs={{0,16},{16,0},{1,17},{17,1},{2,18},{18,2},{3,19},{19,3},{4,20},{20... | collective-permute-start | bytes 6291464 | tf_op jit(solution)/shard_map/ppermute | solution.py:876
  133.0 31.6 %collective-permute-start.27 = (bf16[1024,1024]{1,0:T(8,128)(2,1)}, bf16[1024,1024]{1,0:T(8,128)(2,1)}, u32[]{:S(2)}, u32[]{:S(2)}) collective-permute-start(bf16[1024,1024]{1,0:T(8,128)(2,1)} %constant_dynamic-update-slice_fusion.9.own_ref), channel_id=1, source_target_pairs={{0,16},{16,0},{1,17},{17,1},{2,18},{18,2},{3,19},{19,3},{4,20},{20... | collective-permute-start | bytes 6291464 | tf_op jit(solution)/shard_map/ppermute | solution.py:876
  134.8 22.2 %collective-permute-start.14 = (bf16[1024,1024]{1,0:T(8,128)(2,1)}, bf16[1024,1024]{1,0:T(8,128)(2,1)}, u32[]{:S(2)}, u32[]{:S(2)}) collective-permute-start(bf16[1024,1024]{1,0:T(8,128)(2,1)} %constant_dynamic-update-slice_fusion.own_ref), channel_id=1, source_target_pairs={{0,16},{16,0},{1,17},{17,1},{2,18},{18,2},{3,19},{19,3},{4,20},{20... | collective-permute-start | bytes 6291464 | tf_op jit(solution)/shard_map/ppermute | solution.py:876
  138.9 47.9 %collective-permute-start.39 = (bf16[1024,1024]{1,0:T(8,128)(2,1)}, bf16[1024,1024]{1,0:T(8,128)(2,1)}, u32[]{:S(2)}, u32[]{:S(2)}) collective-permute-start(bf16[1024,1024]{1,0:T(8,128)(2,1)} %maximum_select_fusion), channel_id=1, source_target_pairs={{0,1},{1,0},{2,3},{3,2},{4,5},{5,4},{6,7},{7,6},{8,9},{9,8},{10,11... | collective-permute-start | bytes 6291464 | tf_op jit(solution)/shard_map/ppermute | solution.py:945
  186.9 46.8 %collective-permute-start.40 = (bf16[1024,1024]{1,0:T(8,128)(2,1)}, bf16[1024,1024]{1,0:T(8,128)(2,1)S(1)}, u32[]{:S(2)}, u32[]{:S(2)}) collective-permute-start(bf16[1024,1024]{1,0:T(8,128)(2,1)} %collective-permute-done.39.own_ref), channel_id=1, source_target_pairs={{0,16},{16,0},{1,17},{17,1},{2,18},{18,2},{3,19},{19,3},{4,20},{20... | collective-permute-start | bytes 6291464 | tf_op jit(solution)/shard_map/ppermute | solution.py:876
  349.8 29.2 %collective-permute-start.68 = (bf16[1024,1024]{1,0:T(8,128)(2,1)}, bf16[1024,1024]{1,0:T(8,128)(2,1)}, u32[]{:S(2)}, u32[]{:S(2)}) collective-permute-start(bf16[1024,1024]{1,0:T(8,128)(2,1)} %get-tuple-element.109), channel_id=1, source_target_pairs={{0,16},{16,0},{1,17},{17,1},{2,18},{18,2},{3,19},{19,3},{4,20},{20... | collective-permute-start | bytes 6291464 | tf_op jit(solution)/shard_map/ppermute | solution.py:876
  352.9 29.3 %collective-permute-start.60 = (bf16[1024,1024]{1,0:T(8,128)(2,1)}, bf16[1024,1024]{1,0:T(8,128)(2,1)}, u32[]{:S(2)}, u32[]{:S(2)}) collective-permute-start(bf16[1024,1024]{1,0:T(8,128)(2,1)} %get-tuple-element.111), channel_id=1, source_target_pairs={{0,16},{16,0},{1,17},{17,1},{2,18},{18,2},{3,19},{19,3},{4,20},{20... | collective-permute-start | bytes 6291464 | tf_op jit(solution)/shard_map/ppermute | solution.py:876
  356.5 28.8 %collective-permute-start.52 = (bf16[1024,1024]{1,0:T(8,128)(2,1)}, bf16[1024,1024]{1,0:T(8,128)(2,1)}, u32[]{:S(2)}, u32[]{:S(2)}) collective-permute-start(bf16[1024,1024]{1,0:T(8,128)(2,1)} %get-tuple-element.113), channel_id=1, source_target_pairs={{0,16},{16,0},{1,17},{17,1},{2,18},{18,2},{3,19},{19,3},{4,20},{20... | collective-permute-start | bytes 6291464 | tf_op jit(solution)/shard_map/ppermute | solution.py:876
  367.0 20.7 %collective-permute-start.44 = (bf16[1024,1024]{1,0:T(8,128)(2,1)}, bf16[1024,1024]{1,0:T(8,128)(2,1)}, u32[]{:S(2)}, u32[]{:S(2)}) collective-permute-start(bf16[1024,1024]{1,0:T(8,128)(2,1)} %get-tuple-element.115), channel_id=1, source_target_pairs={{0,16},{16,0},{1,17},{17,1},{2,18},{18,2},{3,19},{19,3},{4,20},{20... | collective-permute-start | bytes 6291464 | tf_op jit(solution)/shard_map/ppermute | solution.py:876
  380.6 14.9 %collective-permute-start.69 = (bf16[512,1024]{1,0:T(8,128)(2,1)S(1)}, bf16[512,1024]{1,0:T(8,128)(2,1)S(1)}, u32[]{:S(2)}, u32[]{:S(2)}) collective-permute-start(bf16[512,1024]{1,0:T(8,128)(2,1)S(1)} %fusion), channel_id=1, source_target_pairs={{0,2},{2,0},{4,6},{6,4},{8,10},{10,8},{12,14},{14,12},{16,20},{18,... | collective-permute-start | bytes 3145736 | tf_op jit(solution)/shard_map/ppermute | solution.py:559
  382.1 227.6 %collective-permute-start.76 = (f32[4,1024]{1,0:T(4,128)S(1)}, f32[4,1024]{1,0:T(4,128)S(1)}, u32[]{:S(2)}, u32[]{:S(2)}) collective-permute-start(f32[4,1024]{1,0:T(4,128)S(1)} %pad_maximum_fusion.17), channel_id=1, source_target_pairs={{0,16},{16,0},{1,17},{17,1},{2,18},{18,2},{3,19},{19,3},{4,20},{20... | collective-permute-start | bytes 49160 | tf_op jit(solution)/shard_map/ppermute | solution.py:876
  383.8 22.9 %collective-permute-start.61 = (bf16[512,1024]{1,0:T(8,128)(2,1)S(1)}, bf16[512,1024]{1,0:T(8,128)(2,1)S(1)}, u32[]{:S(2)}, u32[]{:S(2)}) collective-permute-start(bf16[512,1024]{1,0:T(8,128)(2,1)S(1)} %fusion.3), channel_id=1, source_target_pairs={{0,2},{2,0},{4,6},{6,4},{8,10},{10,8},{12,14},{14,12},{16,20},{18,... | collective-permute-start | bytes 3145736 | tf_op jit(solution)/shard_map/ppermute | solution.py:559
  386.9 36.7 %collective-permute-start.53 = (bf16[512,1024]{1,0:T(8,128)(2,1)S(1)}, bf16[512,1024]{1,0:T(8,128)(2,1)S(1)}, u32[]{:S(2)}, u32[]{:S(2)}) collective-permute-start(bf16[512,1024]{1,0:T(8,128)(2,1)S(1)} %fusion.6), channel_id=1, source_target_pairs={{0,2},{2,0},{4,6},{6,4},{8,10},{10,8},{12,14},{14,12},{16,20},{18,... | collective-permute-start | bytes 3145736 | tf_op jit(solution)/shard_map/ppermute | solution.py:559
  387.7 223.3 %collective-permute-start.80 = (f32[4,1024]{1,0:T(4,128)S(1)}, f32[4,1024]{1,0:T(4,128)S(1)}, u32[]{:S(2)}, u32[]{:S(2)}) collective-permute-start(f32[4,1024]{1,0:T(4,128)S(1)} %pad_maximum_fusion.18), channel_id=1, source_target_pairs={{0,16},{16,0},{1,17},{17,1},{2,18},{18,2},{3,19},{19,3},{4,20},{20... | collective-permute-start | bytes 49160 | tf_op jit(solution)/shard_map/ppermute | solution.py:876
  395.5 44.9 %collective-permute-start.45 = (bf16[512,1024]{1,0:T(8,128)(2,1)S(1)}, bf16[512,1024]{1,0:T(8,128)(2,1)S(1)}, u32[]{:S(2)}, u32[]{:S(2)}) collective-permute-start(bf16[512,1024]{1,0:T(8,128)(2,1)S(1)} %fusion.9), channel_id=1, source_target_pairs={{0,2},{2,0},{4,6},{6,4},{8,10},{10,8},{12,14},{14,12},{16,20},{18,... | collective-permute-start | bytes 3145736 | tf_op jit(solution)/shard_map/ppermute | solution.py:559
  406.7 37.2 %collective-permute-start.70 = (bf16[256,1024]{1,0:T(8,128)(2,1)S(1)}, bf16[256,1024]{1,0:T(8,128)(2,1)S(1)}, u32[]{:S(2)}, u32[]{:S(2)}) collective-permute-start(bf16[256,1024]{1,0:T(8,128)(2,1)S(1)} %constant_dynamic-slice_fusion.1), channel_id=1, source_target_pairs={{0,4},{2,6},{4,0},{6,2},{8,12},{10,14},{12,8},{14,10},{16,18},{18,... | collective-permute-start | bytes 1572872 | tf_op jit(solution)/shard_map/ppermute | solution.py:565
  423.6 21.1 %collective-permute-start.62 = (bf16[256,1024]{1,0:T(8,128)(2,1)S(1)}, bf16[256,1024]{1,0:T(8,128)(2,1)S(1)}, u32[]{:S(2)}, u32[]{:S(2)}) collective-permute-start(bf16[256,1024]{1,0:T(8,128)(2,1)S(1)} %constant_dynamic-slice_fusion.5), channel_id=1, source_target_pairs={{0,4},{2,6},{4,0},{6,2},{8,12},{10,14},{12,8},{14,10},{16,18},{18,... | collective-permute-start | bytes 1572872 | tf_op jit(solution)/shard_map/ppermute | solution.py:565
  443.9 20.6 %collective-permute-start.46 = (bf16[256,1024]{1,0:T(8,128)(2,1)S(1)}, bf16[256,1024]{1,0:T(8,128)(2,1)S(1)}, u32[]{:S(2)}, u32[]{:S(2)}) collective-permute-start(bf16[256,1024]{1,0:T(8,128)(2,1)S(1)} %constant_dynamic-slice_fusion.10), channel_id=1, source_target_pairs={{0,4},{2,6},{4,0},{6,2},{8,12},{10,14},{12,8},{14,10},{16,18},{18,... | collective-permute-start | bytes 1572872 | tf_op jit(solution)/shard_map/ppermute | solution.py:565
  444.7 23.5 %collective-permute-start.71 = (bf16[128,1024]{1,0:T(8,128)(2,1)S(1)}, bf16[128,1024]{1,0:T(8,128)(2,1)S(1)}, u32[]{:S(2)}, u32[]{:S(2)}) collective-permute-start(bf16[128,1024]{1,0:T(8,128)(2,1)S(1)} %constant_dynamic-slice_fusion), channel_id=1, source_target_pairs={{0,8},{2,10},{4,12},{6,14},{8,0},{10,2},{12,4},{14,6},{16,24},{18,... | collective-permute-start | bytes 786440 | tf_op jit(solution)/shard_map/ppermute | solution.py:565
  453.3 29.0 %collective-permute-start.63 = (bf16[128,1024]{1,0:T(8,128)(2,1)S(1)}, bf16[128,1024]{1,0:T(8,128)(2,1)S(1)}, u32[]{:S(2)}, u32[]{:S(2)}) collective-permute-start(bf16[128,1024]{1,0:T(8,128)(2,1)S(1)} %constant_dynamic-slice_fusion.4), channel_id=1, source_target_pairs={{0,8},{2,10},{4,12},{6,14},{8,0},{10,2},{12,4},{14,6},{16,24},{18,... | collective-permute-start | bytes 786440 | tf_op jit(solution)/shard_map/ppermute | solution.py:565
  464.6 26.2 %collective-permute-start.55 = (bf16[128,1024]{1,0:T(8,128)(2,1)S(1)}, bf16[128,1024]{1,0:T(8,128)(2,1)S(1)}, u32[]{:S(2)}, u32[]{:S(2)}) collective-permute-start(bf16[128,1024]{1,0:T(8,128)(2,1)S(1)} %constant_dynamic-slice_fusion.7), channel_id=1, source_target_pairs={{0,8},{2,10},{4,12},{6,14},{8,0},{10,2},{12,4},{14,6},{16,24},{18,... | collective-permute-start | bytes 786440 | tf_op jit(solution)/shard_map/ppermute | solution.py:565
  468.2 31.1 %collective-permute-start.47 = (bf16[128,1024]{1,0:T(8,128)(2,1)S(1)}, bf16[128,1024]{1,0:T(8,128)(2,1)S(1)}, u32[]{:S(2)}, u32[]{:S(2)}) collective-permute-start(bf16[128,1024]{1,0:T(8,128)(2,1)S(1)} %constant_dynamic-slice_fusion.9), channel_id=1, source_target_pairs={{0,8},{2,10},{4,12},{6,14},{8,0},{10,2},{12,4},{14,6},{16,24},{18,... | collective-permute-start | bytes 786440 | tf_op jit(solution)/shard_map/ppermute | solution.py:565
  482.4 25.3 %collective-permute-start.72 = (bf16[128,1024]{1,0:T(8,128)(2,1)S(1)}, bf16[128,1024]{1,0:T(8,128)(2,1)S(1)}, u32[]{:S(2)}, u32[]{:S(2)}) collective-permute-start(bf16[128,1024]{1,0:T(8,128)(2,1)S(1)} %add_convert_fusion.4), channel_id=1, source_target_pairs={{0,8},{2,10},{4,12},{6,14},{8,0},{10,2},{12,4},{14,6},{16,24},{18,... | collective-permute-start | bytes 786440 | tf_op jit(solution)/shard_map/ppermute | solution.py:572
  490.8 25.3 %collective-permute-start.64 = (bf16[128,1024]{1,0:T(8,128)(2,1)S(1)}, bf16[128,1024]{1,0:T(8,128)(2,1)S(1)}, u32[]{:S(2)}, u32[]{:S(2)}) collective-permute-start(bf16[128,1024]{1,0:T(8,128)(2,1)S(1)} %add_convert_fusion.5), channel_id=1, source_target_pairs={{0,8},{2,10},{4,12},{6,14},{8,0},{10,2},{12,4},{14,6},{16,24},{18,... | collective-permute-start | bytes 786440 | tf_op jit(solution)/shard_map/ppermute | solution.py:572
  499.2 33.8 %collective-permute-start.56 = (bf16[128,1024]{1,0:T(8,128)(2,1)S(1)}, bf16[128,1024]{1,0:T(8,128)(2,1)S(1)}, u32[]{:S(2)}, u32[]{:S(2)}) collective-permute-start(bf16[128,1024]{1,0:T(8,128)(2,1)S(1)} %add_convert_fusion.6), channel_id=1, source_target_pairs={{0,8},{2,10},{4,12},{6,14},{8,0},{10,2},{12,4},{14,6},{16,24},{18,... | collective-permute-start | bytes 786440 | tf_op jit(solution)/shard_map/ppermute | solution.py:572
  507.7 29.3 %collective-permute-start.48 = (bf16[128,1024]{1,0:T(8,128)(2,1)S(1)}, bf16[128,1024]{1,0:T(8,128)(2,1)S(1)}, u32[]{:S(2)}, u32[]{:S(2)}) collective-permute-start(bf16[128,1024]{1,0:T(8,128)(2,1)S(1)} %add_convert_fusion.7), channel_id=1, source_target_pairs={{0,8},{2,10},{4,12},{6,14},{8,0},{10,2},{12,4},{14,6},{16,24},{18,... | collective-permute-start | bytes 786440 | tf_op jit(solution)/shard_map/ppermute | solution.py:572
  516.1 28.2 %collective-permute-start.73 = (bf16[256,1024]{1,0:T(8,128)(2,1)S(1)}, bf16[256,1024]{1,0:T(8,128)(2,1)S(1)}, u32[]{:S(2)}, u32[]{:S(2)}) collective-permute-start(bf16[256,1024]{1,0:T(8,128)(2,1)S(1)} %pad_maximum_fusion.12), channel_id=1, source_target_pairs={{0,4},{2,6},{4,0},{6,2},{8,12},{10,14},{12,8},{14,10},{16,18},{18,... | collective-permute-start | bytes 1572872 | tf_op jit(solution)/shard_map/ppermute | solution.py:572
  533.0 22.5 %collective-permute-start.65 = (bf16[256,1024]{1,0:T(8,128)(2,1)S(1)}, bf16[256,1024]{1,0:T(8,128)(2,1)S(1)}, u32[]{:S(2)}, u32[]{:S(2)}) collective-permute-start(bf16[256,1024]{1,0:T(8,128)(2,1)S(1)} %pad_maximum_fusion.11), channel_id=1, source_target_pairs={{0,4},{2,6},{4,0},{6,2},{8,12},{10,14},{12,8},{14,10},{16,18},{18,... | collective-permute-start | bytes 1572872 | tf_op jit(solution)/shard_map/ppermute | solution.py:572
  536.9 29.8 %collective-permute-start.57 = (bf16[256,1024]{1,0:T(8,128)(2,1)S(1)}, bf16[256,1024]{1,0:T(8,128)(2,1)S(1)}, u32[]{:S(2)}, u32[]{:S(2)}) collective-permute-start(bf16[256,1024]{1,0:T(8,128)(2,1)S(1)} %pad_maximum_fusion.10), channel_id=1, source_target_pairs={{0,4},{2,6},{4,0},{6,2},{8,12},{10,14},{12,8},{14,10},{16,18},{18,... | collective-permute-start | bytes 1572872 | tf_op jit(solution)/shard_map/ppermute | solution.py:572
  544.3 33.7 %collective-permute-start.49 = (bf16[256,1024]{1,0:T(8,128)(2,1)S(1)}, bf16[256,1024]{1,0:T(8,128)(2,1)S(1)}, u32[]{:S(2)}, u32[]{:S(2)}) collective-permute-start(bf16[256,1024]{1,0:T(8,128)(2,1)S(1)} %pad_maximum_fusion.9), channel_id=1, source_target_pairs={{0,4},{2,6},{4,0},{6,2},{8,12},{10,14},{12,8},{14,10},{16,18},{18,... | collective-permute-start | bytes 1572872 | tf_op jit(solution)/shard_map/ppermute | solution.py:572
  555.5 24.2 %collective-permute-start.74 = (bf16[512,1024]{1,0:T(8,128)(2,1)S(1)}, bf16[512,1024]{1,0:T(8,128)(2,1)S(1)}, u32[]{:S(2)}, u32[]{:S(2)}) collective-permute-start(bf16[512,1024]{1,0:T(8,128)(2,1)S(1)} %pad_maximum_fusion.8), channel_id=1, source_target_pairs={{0,2},{2,0},{4,6},{6,4},{8,10},{10,8},{12,14},{14,12},{16,20},{18,... | collective-permute-start | bytes 3145736 | tf_op jit(solution)/shard_map/ppermute | solution.py:572
  566.8 14.8 %collective-permute-start.66 = (bf16[512,1024]{1,0:T(8,128)(2,1)S(1)}, bf16[512,1024]{1,0:T(8,128)(2,1)S(1)}, u32[]{:S(2)}, u32[]{:S(2)}) collective-permute-start(bf16[512,1024]{1,0:T(8,128)(2,1)S(1)} %pad_maximum_fusion.7), channel_id=1, source_target_pairs={{0,2},{2,0},{4,6},{6,4},{8,10},{10,8},{12,14},{14,12},{16,20},{18,... | collective-permute-start | bytes 3145736 | tf_op jit(solution)/shard_map/ppermute | solution.py:572
  578.0 14.8 %collective-permute-start.58 = (bf16[512,1024]{1,0:T(8,128)(2,1)S(1)}, bf16[512,1024]{1,0:T(8,128)(2,1)S(1)}, u32[]{:S(2)}, u32[]{:S(2)}) collective-permute-start(bf16[512,1024]{1,0:T(8,128)(2,1)S(1)} %pad_maximum_fusion.6), channel_id=1, source_target_pairs={{0,2},{2,0},{4,6},{6,4},{8,10},{10,8},{12,14},{14,12},{16,20},{18,... | collective-permute-start | bytes 3145736 | tf_op jit(solution)/shard_map/ppermute | solution.py:572
  579.7 24.3 %collective-permute-start.50 = (bf16[512,1024]{1,0:T(8,128)(2,1)S(1)}, bf16[512,1024]{1,0:T(8,128)(2,1)S(1)}, u32[]{:S(2)}, u32[]{:S(2)}) collective-permute-start(bf16[512,1024]{1,0:T(8,128)(2,1)S(1)} %pad_maximum_fusion.5), channel_id=1, source_target_pairs={{0,2},{2,0},{4,6},{6,4},{8,10},{10,8},{12,14},{14,12},{16,20},{18,... | collective-permute-start | bytes 3145736 | tf_op jit(solution)/shard_map/ppermute | solution.py:572
  581.6 61.4 %collective-permute-start.75 = (bf16[1024,1024]{1,0:T(8,128)(2,1)S(1)}, bf16[1024,1024]{1,0:T(8,128)(2,1)}, u32[]{:S(2)}, u32[]{:S(2)}) collective-permute-start(bf16[1024,1024]{1,0:T(8,128)(2,1)S(1)} %pad_maximum_fusion.4.own1), channel_id=1, source_target_pairs={{0,16},{1,17},{2,18},{3,19},{4,20},{5,21},{6,22},{7,23},{8,24},{9,... | collective-permute-start | bytes 6291464 | tf_op jit(solution)/shard_map/ppermute | solution.py:989
  592.8 50.2 %collective-permute-start.67 = (bf16[1024,1024]{1,0:T(8,128)(2,1)}, bf16[1024,1024]{1,0:T(8,128)(2,1)}, u32[]{:S(2)}, u32[]{:S(2)}) collective-permute-start(bf16[1024,1024]{1,0:T(8,128)(2,1)} %pad_maximum_fusion.3.own0), channel_id=1, source_target_pairs={{16,0},{17,1},{18,2},{19,3},{20,4},{21,5},{22,6},{23,7},{24,8},{25... | collective-permute-start | bytes 6291464 | tf_op jit(solution)/shard_map/ppermute | solution.py:989
  604.0 45.0 %collective-permute-start.59 = (bf16[1024,1024]{1,0:T(8,128)(2,1)}, bf16[1024,1024]{1,0:T(8,128)(2,1)}, u32[]{:S(2)}, u32[]{:S(2)}) collective-permute-start(bf16[1024,1024]{1,0:T(8,128)(2,1)} %pad_maximum_fusion.2.own1), channel_id=1, source_target_pairs={{0,16},{1,17},{2,18},{3,19},{4,20},{5,21},{6,22},{7,23},{8,24},{9,... | collective-permute-start | bytes 6291464 | tf_op jit(solution)/shard_map/ppermute | solution.py:991
  609.7 39.3 %collective-permute-start.51 = (bf16[1024,1024]{1,0:T(8,128)(2,1)}, bf16[1024,1024]{1,0:T(8,128)(2,1)}, u32[]{:S(2)}, u32[]{:S(2)}) collective-permute-start(bf16[1024,1024]{1,0:T(8,128)(2,1)} %pad_maximum_fusion.1.own0), channel_id=1, source_target_pairs={{16,0},{17,1},{18,2},{19,3},{20,4},{21,5},{22,6},{23,7},{24,8},{25... | collective-permute-start | bytes 6291464 | tf_op jit(solution)/shard_map/ppermute | solution.py:991
  (69 other events, 655.5 us)

commit v2 on v0

v2 whole, which is shorter than its diff:
```python
import functools

import jax
import jax.numpy as jnp
import numpy as np
from jax import lax
from jax.experimental import pallas as pl
from jax.experimental.pallas import tpu as pltpu
from jax.sharding import PartitionSpec as P

HEAD_DIM = 128
BAND = 128
EPSILON = 1e-05
MASKED = -1e30
VMEM = 60 * 1024 * 1024
bf16 = jnp.bfloat16
f32 = jnp.float32


def params():
    return pltpu.CompilerParams(vmem_limit_bytes=VMEM)


def cost(flops, moved):
    return pl.CostEstimate(
        flops=int(flops), bytes_accessed=int(moved), transcendentals=0
    )


def dot(a, b):
    return jnp.dot(a, b, preferred_element_type=f32)


def dot_nt(a, b):
    return lax.dot_general(a, b, (((1,), (1,)), ((), ())), preferred_element_type=f32)


def dot_tn(a, b):
    return lax.dot_general(a, b, (((0,), (0,)), ((), ())), preferred_element_type=f32)


def unit_of(values):
    centre = values - jnp.mean(values, axis=-1, keepdims=True)
    spread = jnp.mean(centre * centre, axis=-1, keepdims=True)
    scale = lax.rsqrt(spread + EPSILON)
    return centre * scale, scale


def norm_back(incoming, values, gain):
    unit, scale = unit_of(values)
    scaled = incoming * gain
    inner = (
        scaled
        - jnp.mean(scaled, axis=-1, keepdims=True)
        - unit * jnp.mean(scaled * unit, axis=-1, keepdims=True)
    )
    grads = jnp.concatenate(
        [
            jnp.sum(incoming * unit, axis=0, keepdims=True),
            jnp.sum(incoming, axis=0, keepdims=True),
        ],
        axis=0,
    )
    return scale * inner, grads


def any_specs(n):
    return [pl.BlockSpec(memory_space=pl.ANY)] * n


class Own:
    def __init__(self, layer, sec, mine, swapped):
        self.scalars = jnp.stack([sec, jnp.full_like(sec, layer)])
        self.mine, self.swapped = mine, swapped

    def operands(self, names):
        return [self.mine[n] for n in names] + [self.swapped[n] for n in names]

    def start(self, names, scalars, refs, targets, sems):
        mine, swapped = refs[: len(names)], refs[len(names) :]
        for condition, side in ((True, mine), (False, swapped)):

            @pl.when((scalars[0] == scalars[1]) == condition)
            def _():
                for n, (ref, target) in enumerate(zip(side, targets)):
                    pltpu.make_async_copy(ref, target, sems.at[n, 0]).start()

    def wait(self, n, name, target, sems):
        pltpu.make_async_copy(target, target, sems.at[n, 0]).wait()


class Pieces:
    def __init__(self, sec, places, own, far):
        self.count = len(own)
        self.scalars = jnp.concatenate([sec.reshape(1), places])
        self.arrays, self.index = [], []
        for side in (own, far):
            rows = []
            for slot in side:
                parts = []
                for array, row in slot:
                    known = [n for n, x in enumerate(self.arrays) if x is array]
                    if not known:
                        self.arrays.append(array)
                        known = [len(self.arrays) - 1]
                    parts.append((known[0], row))
                rows.append(parts)
            self.index.append(rows)

    def operands(self, names):
        return self.arrays

    def start(self, names, scalars, refs, targets, sems):
        every = slice(None)
        for side, slots in enumerate(self.index):
            core = lax.rem(scalars[0] + side, 2)
            for slot, ((n0, row0), (n1, row1)) in enumerate(slots):
                spot = scalars[1 + slot] * 2 + core
                first, second = refs[n0], refs[n1]
                for n, (name, target) in enumerate(zip(names, targets)):

                    def put(source, place):
                        pltpu.make_async_copy(source, place, sems.at[n, side]).start()

                    if name == "qkv":
                        deep, local = target.shape[1], target.shape[2]
                        fine = deep // self.count // 2
                        half = fine // 2
                        row = spot * fine
                        for j in range(2):
                            columns = slice(j * local, (j + 1) * local)
                            put(
                                first.at[row0 : row0 + fine, columns],
                                target.at[j, pl.ds(row, fine), :],
                            )
                            put(
                                second.at[row1 : row1 + half, columns],
                                target.at[2, pl.ds(row + j * half, half), :],
                            )
                    elif name == "out":
                        fine = target.shape[0] // self.count // 2
                        put(
                            second.at[row1 + fine : row1 + 2 * fine, every],
                            target.at[pl.ds(spot * fine, fine), :],
                        )
                    else:
                        fine = target.shape[0] // self.count // 2
                        source = second.at[row1 : row1 + fine, every] if name == "down" else first.at[row0 : row0 + fine, every]
                        put(source, target.at[pl.ds(spot * fine, fine), :])

    def wait(self, n, name, target, sems):
        for side in range(2):
            if name == "qkv":
                part = target.at[:, : target.shape[1] // 2, :]
            else:
                part = target.at[: target.shape[0] // 2, :]
            pltpu.make_async_copy(part, part, sems.at[n, side]).wait()


def struct(shape, dtype):
    return jax.ShapeDtypeStruct(shape, dtype)


class Room:
    def __init__(self, refs, sources, sinks, in_sems, out_sems, weights):
        self.refs, self.sources, self.sinks = refs, sources, sinks
        self.in_sems, self.out_sems, self.weights = in_sems, out_sems, weights
        self.waited, self.leaving = set(), []

    def start(self, names):
        for n, name in enumerate(names):
            pltpu.make_async_copy(self.sources[name], self.refs[name], self.in_sems.at[n]).start()
        self.order = list(names)

    def get(self, name):
        if name in self.sources and name not in self.waited:
            self.waited.add(name)
            ref = self.refs[name]
            pltpu.make_async_copy(ref, ref, self.in_sems.at[self.order.index(name)]).wait()
        return self.refs[name]

    def weight(self, name):
        loader, place, kind, target, sems = self.weights[name]
        if name not in self.waited:
            self.waited.add(name)
            loader.wait(place, kind, target, sems)
        return target

    def send(self, pairs):
        for source, sink in pairs:
            copy = pltpu.make_async_copy(source, sink, self.out_sems.at[len(self.leaving)])
            copy.start()
            self.leaving.append(copy)

    def flush(self, *names):
        self.send([(self.refs[name], self.sinks[name]) for name in names])

    def close(self):
        for copy in self.leaving:
            copy.wait()


def room_call(name, body, scalars, weights, inputs, outputs, scratch, copies, flops):
    in_names, out_names, temp_names = list(inputs), list(outputs), list(scratch)
    operands = [loader.operands([k for k, _ in kinds]) for _, loader, kinds in weights]
    scalar_list = [scalars] + [loader.scalars for _, loader, _ in weights]
    local_out = [n for n in out_names if n not in scratch]

    def whole(*refs):
        refs = list(refs)

        def take(n):
            got = refs[:n]
            del refs[:n]
            return got

        scalar_refs = take(len(scalar_list))
        sources = dict(zip(in_names, take(len(in_names))))
        weight_sources = [take(len(o)) for o in operands]
        sinks = dict(zip(out_names, take(len(out_names))))
        held = dict(zip(in_names, take(len(in_names))))
        held.update(zip(local_out, take(len(local_out))))
        held.update(zip(temp_names, take(len(temp_names))))
        in_sems, out_sems = take(2)
        table = {}
        starts = []
        for (prefix, loader, kinds), source, scalar in zip(weights, weight_sources, scalar_refs[1:]):
            targets = take(len(kinds))
            sems = take(1)[0]
            starts.append((loader, [k for k, _ in kinds], scalar, source, targets, sems))
            for place, (kind, _) in enumerate(kinds):
                table[prefix + kind] = (loader, place, kind, targets[place], sems)
        room = Room(held, sources, sinks, in_sems, out_sems, table)
        room.start(in_names)
        for loader, kinds, scalar, source, targets, sems in starts:
            loader.start(kinds, scalar, source, targets, sems)
        body(room, scalar_refs[0])
        for name in in_names:
            room.get(name)
        for key in table:
            room.weight(key)
        room.close()

    vmem = [pltpu.VMEM(inputs[n].shape, inputs[n].dtype) for n in in_names]
    vmem += [pltpu.VMEM(outputs[n].shape, outputs[n].dtype) for n in local_out]
    vmem += [pltpu.VMEM(*scratch[n]) for n in temp_names]
    vmem += [pltpu.SemaphoreType.DMA((max(len(in_names), 1),)), pltpu.SemaphoreType.DMA((copies,))]
    for _, _, kinds in weights:
        vmem += [pltpu.VMEM(shape, bf16) for _, shape in kinds]
        vmem.append(pltpu.SemaphoreType.DMA((len(kinds), 2)))
    flat = [x for o in operands for x in o]
    moved = sum(x.size * x.dtype.itemsize for x in list(inputs.values()) + list(outputs.values()))
    moved += sum(2 * int(np.prod(shape)) for _, _, kinds in weights for _, shape in kinds)
    result = pl.pallas_call(
        whole,
        in_specs=[pl.BlockSpec(memory_space=pltpu.SMEM)] * len(scalar_list)
        + any_specs(len(in_names) + len(flat)),
        out_specs=any_specs(len(out_names)),
        out_shape=[outputs[n] for n in out_names],
        scratch_shapes=vmem,
        compiler_params=params(),
        cost_estimate=cost(flops, moved),
        name=name,
    )(*scalar_list, *inputs.values(), *flat)
    return dict(zip(out_names, result))


def band_probs(q, k, start_ref, block):
    low = max(block - 1, 0) * BAND
    high = (block + 1) * BAND
    scores = dot_nt(q[block * BAND : high], k[low:high]) * HEAD_DIM**-0.5
    row = lax.broadcasted_iota(jnp.int32, scores.shape, 0) + block * BAND
    column = lax.broadcasted_iota(jnp.int32, scores.shape, 1) + low
    first = start_ref[block * BAND : high, :]
    allowed = (column <= row) & (column >= first)
    scores = jnp.where(allowed, scores, MASKED)
    expo = jnp.exp(scores - jnp.max(scores, axis=-1, keepdims=True))
    return expo / jnp.sum(expo, axis=-1, keepdims=True), low, high


def heads_of(qkv_ref, head, local):
    return [
        qkv_ref[:, j * local + head * HEAD_DIM : j * local + (head + 1) * HEAD_DIM] for j in range(3)
    ]


def attend(qkv_ref, start_ref, o_ref):
    rows, local = o_ref.shape
    for head in range(local // HEAD_DIM):
        cut = slice(head * HEAD_DIM, (head + 1) * HEAD_DIM)
        q, k, v = heads_of(qkv_ref, head, local)
        for block in range(rows // BAND):
            probs, low, high = band_probs(q, k, start_ref, block)
            o_ref[block * BAND : high, cut] = dot(probs.astype(bf16), v[low:high]).astype(bf16)


def project(left, w, out_ref):
    local = w.shape[2]
    for j in range(3):
        out_ref[:, j * local : (j + 1) * local] = dot(left[...], w[j]).astype(bf16)


def activate(n2_ref, up, z_ref, slope_ref):
    c = np.float32(np.sqrt(2 / np.pi))
    tile = 512
    for i in range(z_ref.shape[1] // tile):
        cut = slice(i * tile, (i + 1) * tile)
        a = dot(n2_ref[...], up[:, cut])
        square = a * a
        t = jnp.tanh(c * a * (1.0 + 0.044715 * square))
        half = 0.5 * (1.0 + t)
        slope = half + 0.5 * c * a * (1.0 - t * t) * (1.0 + 3 * 0.044715 * square)
        z_ref[:, cut] = (a * half).astype(bf16)
        slope_ref[:, cut] = slope.astype(bf16)


def sizes(width):
    local, units = width // 2, width
    return {
        "qkv": (3, width, local),
        "out": (local, width),
        "up": (width, units),
        "down": (units, width),
    }


def group(prefix, loader, kinds, width):
    return prefix, loader, [(k, sizes(width)[k]) for k in kinds]


def first_call(scalars, own, u, start, gain, bias):
    rows, width = u.shape
    local = width // 2

    def body(room, _):
        u_ref = room.get("u")
        unit, _ = unit_of(u_ref[...].astype(f32))
        n1 = room.get("n1")
        n1[...] = (unit * room.get("gain")[...] + room.get("bias")[...]).astype(bf16)
        project(n1, room.weight("own_qkv"), room.get("qkv"))
        room.flush("n1", "qkv")
        attend(room.get("qkv"), room.get("start"), room.get("o"))
        room.flush("o")
        room.get("h")[...] = u_ref[...].astype(f32) + dot(room.get("o")[...], room.weight("own_out")[...])
        room.flush("h")

    return room_call(
        "first", body, scalars, [group("own_", own, ["qkv", "out"], width)],
        dict(u=u, start=start, gain=gain, bias=bias),
        dict(n1=struct((rows, width), bf16), qkv=struct((rows, 3 * local), bf16),
             o=struct((rows, local), bf16), h=struct((rows, width), f32)),
        {}, 4, 9 * rows * width * local,
    )


def second_call(scalars, far, n1, start, base, gain, bias):
    rows, width = base.shape
    local = width // 2

    def body(room, _):
        project(room.get("n1"), room.weight("far_qkv"), room.get("qkv"))
        room.flush("qkv")
        attend(room.get("qkv"), room.get("start"), room.get("o"))
        h = room.get("base")[...] + dot(room.get("o")[...], room.weight("far_out")[...])
        room.get("h")[...] = h
        unit, _ = unit_of(h)
        n2 = room.get("n2")
        n2[...] = (unit * room.get("gain")[...] + room.get("bias")[...]).astype(bf16)
        room.flush("h", "n2")

    return room_call(
        "second", body, scalars, [group("far_", far, ["qkv", "out"], width)],
        dict(n1=n1, start=start, base=base, gain=gain, bias=bias),
        dict(qkv=struct((rows, 3 * local), bf16), h=struct((rows, width), f32),
             n2=struct((rows, width), bf16)),
        dict(o=((rows, local), bf16)), 3, 9 * rows * width * local,
    )


def feed_call(scalars, own, far_two, n2, h):
    rows, width = h.shape
    units = width

    def body(room, _):
        n2 = room.get("n2")
        activate(n2, room.weight("own_up"), room.get("z"), room.get("slope"))
        room.flush("z", "slope")
        activate(n2, room.weight("two_up"), room.get("z_far"), room.get("slope_far"))
        room.flush("slope_far")
        y = room.get("h")[...] + dot(room.get("z")[...], room.weight("own_down")[...])
        room.get("y")[...] = (y + dot(room.get("z_far")[...], room.weight("two_down")[...])).astype(bf16)
        room.flush("y")

    tall = struct((rows, width), bf16)
    return room_call(
        "feed", body, scalars,
        [group("own_", own, ["up", "down"], width), group("two_", far_two, ["up", "down"], width)],
        dict(n2=n2, h=h), dict(z=tall, slope=tall, slope_far=tall, y=tall),
        dict(z_far=((rows, units), bf16)), 4, 8 * rows * width * units,
    )


def feed_back_call(scalars, own, far_two, gy, slope, slope_far, h, z, n2, gain):
    rows, width = gy.shape
    units = width
    half = units // 2

    def body(room, scalar):
        gy_ref = room.get("gy")
        dz = dot_nt(gy_ref[...], room.weight("own_down")[...])
        da = room.get("da")
        da[...] = (dz * room.get("slope")[...].astype(f32)).astype(bf16)
        down, up = room.get("grad_down"), room.get("grad_up")
        down[...] = dot_tn(room.get("z")[...], gy_ref[...]).astype(bf16)
        up[...] = dot_tn(room.get("n2")[...], da[...]).astype(bf16)
        for name, which in (("give", 1 - scalar[0]), ("keep", scalar[0])):
            at = pl.multiple_of(which * half, half)
            sink = room.sinks[name]
            room.send([(down.at[pl.ds(at, half), :], sink.at[:half, :])])
            room.send([(up.at[pl.ds(at, half), :], sink.at[half:, :])])
        term = dot_nt(da[...], room.weight("own_up")[...])
        dz = dot_nt(gy_ref[...], room.weight("two_down")[...])
        da = (dz * room.get("slope_far")[...].astype(f32)).astype(bf16)
        term = term + dot_nt(da, room.weight("two_up")[...])
        back, grads = norm_back(term, room.get("h")[...], room.get("gain")[...])
        dh = gy_ref[...].astype(f32) + back
        room.get("dh")[...] = dh
        room.get("gh")[...] = dh.astype(bf16)
        room.get("grads")[...] = grads
        room.flush("dh", "gh", "grads")

    part = struct((2 * half, width), bf16)
    tall = ((rows, width), bf16)
    return room_call(
        "feed_back", body, scalars,
        [group("own_", own, ["down", "up"], width), group("two_", far_two, ["down", "up"], width)],
        dict(gy=gy, slope=slope, z=z, n2=n2, slope_far=slope_far, h=h, gain=gain),
        dict(give=part, keep=part, dh=struct((rows, width), f32), gh=struct((rows, width), bf16),
             grads=struct((2, width), f32)),
        dict(da=tall, grad_down=((units, width), bf16), grad_up=((width, units), bf16),
             give=((16, 128), bf16), keep=((16, 128), bf16)),
        7, 12 * rows * width * units,
    )


def attend_back(qkv_ref, start_ref, do_all, out):
    rows, local = do_all.shape
    blocks = rows // BAND
    for head in range(local // HEAD_DIM):
        q, k, v = heads_of(qkv_ref, head, local)
        do = do_all[:, head * HEAD_DIM : (head + 1) * HEAD_DIM]
        columns = [
            slice(j * local + head * HEAD_DIM, j * local + (head + 1) * HEAD_DIM) for j in range(3)
        ]
        dk_parts, dv_parts = [None] * blocks, [None] * blocks

        def put(parts, term, low):
            for piece in range(term.shape[0] // BAND):
                place = low // BAND + piece
                add = term[piece * BAND : (piece + 1) * BAND]
                parts[place] = add if parts[place] is None else parts[place] + add

        for block in range(blocks):
            probs, low, high = band_probs(q, k, start_ref, block)
            here = slice(block * BAND, high)
            dp = dot_nt(do[here], v[low:high])
            inner = jnp.sum(probs * dp, axis=-1, keepdims=True)
            ds = (probs * (dp - inner) * HEAD_DIM**-0.5).astype(bf16)
            out[here, columns[0]] = dot(ds, k[low:high]).astype(bf16)
            put(dk_parts, dot_tn(ds, q[here]), low)
            put(dv_parts, dot_tn(probs.astype(bf16), do[here]), low)
        for block in range(blocks):
            here = slice(block * BAND, (block + 1) * BAND)
            out[here, columns[1]] = dk_parts[block].astype(bf16)
            out[here, columns[2]] = dv_parts[block].astype(bf16)


def heads_back_call(scalars, own, qkv, start, gh, o, n1):
    rows, width = gh.shape
    local = width // 2
    first, deep = local // 2, width // 4

    def body(room, scalar):
        gh_ref = room.get("gh")
        do_all = dot_nt(gh_ref[...], room.weight("own_out")[...]).astype(bf16)
        d = room.get("d")
        attend_back(room.get("qkv"), room.get("start"), do_all, d)
        room.flush("d")
        grad_out, grad_qkv = room.get("grad_out"), room.get("grad_qkv")
        grad_out[...] = dot_tn(room.get("o")[...], gh_ref[...]).astype(bf16)
        grad_qkv[...] = dot_tn(room.get("n1")[...], d[...]).astype(bf16)
        for name, which in (("give", 1 - scalar[0]), ("keep", scalar[0])):
            sink = room.sinks[name]
            at = pl.multiple_of(which * first, first)
            room.send([(grad_out.at[pl.ds(at, first), :], sink.at[:first, :])])
            for side in range(2):
                at = pl.multiple_of((which * 2 + side) * deep, deep)
                for j in range(3):
                    room.send([(
                        grad_qkv.at[pl.ds(at, deep), j * local : (j + 1) * local],
                        sink.at[
                            first + j * deep : first + (j + 1) * deep,
                            side * local : (side + 1) * local,
                        ],
                    )])

    part = struct((first + 3 * deep, width), bf16)
    return room_call(
        "heads_back", body, scalars, [group("own_", own, ["out"], width)],
        dict(gh=gh, qkv=qkv, start=start, o=o, n1=n1),
        dict(give=part, keep=part, d=struct((rows, 3 * local), bf16)),
        dict(grad_out=((local, width), bf16), grad_qkv=((width, 3 * local), bf16),
             give=((16, 128), bf16), keep=((16, 128), bf16)),
        15, 17 * rows * width * local,
    )


def input_back_call(scalars, own, far, qkv_far, start, gh, d, dh, u, gain):
    rows, width = gh.shape
    local = width // 2

    def body(room, _):
        do_all = dot_nt(room.get("gh")[...], room.weight("far_out")[...]).astype(bf16)
        d_far = room.get("d_far")
        attend_back(room.get("qkv"), room.get("start"), do_all, d_far)
        term = None
        for ref, w in ((room.get("d"), room.weight("own_qkv")), (d_far, room.weight("far_qkv"))):
            for j in range(3):
                part = dot_nt(ref[:, j * local : (j + 1) * local], w[j])
                term = part if term is None else term + part
        back, grads = norm_back(term, room.get("u")[...].astype(f32), room.get("gain")[...])
        room.get("du")[...] = (room.get("dh")[...] + back).astype(bf16)
        room.get("grads")[...] = grads
        room.flush("du", "grads")

    return room_call(
        "input_back", body, scalars,
        [group("far_", far, ["out", "qkv"], width), group("own_", own, ["qkv"], width)],
        dict(gh=gh, qkv=qkv_far, start=start, d=d, u=u, gain=gain, dh=dh),
        dict(du=struct((rows, width), bf16), grads=struct((2, width), f32)),
        dict(d_far=((rows, 3 * local), bf16)), 2, 21 * rows * width * local,
    )


def ring_walk(size):
    return list(range(0, size, 2)) + list(range(1, size, 2))[::-1]


def ring_routes(count, size):
    walk = ring_walk(size)
    up = []
    for base in range(0, count, size):
        for place in range(size):
            up.append((base + walk[place], base + walk[(place + 1) % size]))
    return up, [(b, a) for a, b in up]


def slot_steps(size):
    return list(range(0, -size // 2, -1)) + list(range(1, size // 2)) + [size // 2]


def halving_order(count):
    bits = count.bit_length() - 1
    first = list(range(bits))
    second = [1, 0] + first[2:] if bits > 1 else first
    return first, second


def pairs_of(count, step):
    routes = []
    for core, order in enumerate(halving_order(count)):
        for i in range(count):
            routes.append((core * count + i, core * count + (i ^ (1 << order[step]))))
    return routes


def own_bits(sec, rank, count):
    first, second = halving_order(count)
    return [
        lax.rem(rank >> jnp.where(sec == 0, a, b), 2) for a, b in zip(first, second)
    ]


class Flow:
    def __init__(self, steps):
        self.steps, self.results, self.value, self.done = steps, None, None, False

    def advance(self, after=None):
        if after is not None and self.results is not None:
            self.results, _ = lax.optimization_barrier((self.results, after))
        try:
            operands, send = self.steps.send(self.results)
        except StopIteration as stop:
            self.value, self.done = stop.value, True
            return ()
        self.results = send(operands)
        return operands


def finished(flow):
    while not flow.done:
        flow.advance()
    return flow.value


def together(flows, *others):
    moving = [flow for flow in flows if not flow.done]
    results, others = lax.optimization_barrier(([flow.results for flow in moving], others))
    for flow, result in zip(moving, results):
        flow.results = result
    return [flow.advance() for flow in moving], others


def kernel_after(kernel, moving, last, *inputs):
    operands = [flow.advance(last) for flow in moving if not flow.done]
    inputs, _ = lax.optimization_barrier((inputs, operands))
    return kernel(*inputs)


def cut_body(count, spots, qkv, out, up, down, attention, feed, sems):
    width = up.shape[0]
    local = qkv.shape[2]
    place, sec = spots[0], spots[1]
    fine = width // count // 2
    half = fine // 2
    for which in range(2):
        core = sec if which == 0 else 1 - sec
        row = (place * 2 + core) * fine
        base = which * 2 * fine

        def put(n, source, target):
            pltpu.make_async_copy(source, target, sems.at[n]).start()

        mid = base + fine
        put(0, qkv.at[0, pl.ds(row, fine), :], attention.at[base:mid, :local])
        put(0, qkv.at[1, pl.ds(row, fine), :], attention.at[base:mid, local:])
        put(0, qkv.at[2, pl.ds(row, half), :], attention.at[mid : mid + half, :local])
        put(0, qkv.at[2, pl.ds(row + half, half), :], attention.at[mid : mid + half, local:])
        put(0, out.at[pl.ds((place * 2 + core) * half, half), :], attention.at[mid + half : mid + fine, :])
        put(1, up.at[pl.ds(row, fine), :], feed.at[base:mid, :])
        put(1, down.at[pl.ds(row, fine), :], feed.at[mid : mid + fine, :])
    pltpu.make_async_copy(attention, attention, sems.at[0]).wait()
    pltpu.make_async_copy(feed, feed, sems.at[1]).wait()


def cut_call(spots, count, mine):
    width = mine[2].shape[0]
    shapes = [struct((2 * width // count, width), bf16)] * 2
    return pl.pallas_call(
        functools.partial(cut_body, count),
        grid=(1,),
        in_specs=[pl.BlockSpec(memory_space=pltpu.SMEM)] + any_specs(4),
        out_specs=[pl.BlockSpec(x.shape, lambda i: (0, 0)) for x in shapes],
        out_shape=shapes,
        scratch_shapes=[pltpu.SemaphoreType.DMA((2,))],
        compiler_params=params(),
        cost_estimate=cost(0, 4 * width * width),
        name="cut",
    )(spots, *mine)


def final_call(name, body, scalars, sums, outputs):
    whole, width = sums[0].shape

    def kernel(scalar_ref, own0, far0, own1, far1, *refs):
        refs = list(refs)
        sinks = refs[: len(outputs)]
        held, sems, out_sems, *wide = refs[len(outputs) :]
        sec = scalar_ref[0]
        for layer, sides in enumerate(((own0, far0), (own1, far1))):

            @pl.when(sec == layer)
            def _():
                for side, ref in enumerate(sides):
                    pltpu.make_async_copy(ref, held.at[side], sems.at[side]).start()

        leaving = []
        for side in range(2):
            pltpu.make_async_copy(held.at[side], held.at[side], sems.at[side]).wait()
            for source, sink in body(held, side, lax.rem(sec + side, 2), wide, sinks):
                copy = pltpu.make_async_copy(source, sink, out_sems.at[len(leaving)])
                copy.start()
                leaving.append(copy)
        for copy in leaving:
            copy.wait()

    return pl.pallas_call(
        kernel,
        in_specs=[pl.BlockSpec(memory_space=pltpu.SMEM)] + any_specs(4),
        out_specs=any_specs(len(outputs)),
        out_shape=outputs,
        scratch_shapes=[
            pltpu.VMEM((2, whole, width), bf16),
            pltpu.SemaphoreType.DMA((2,)),
            pltpu.SemaphoreType.DMA((16,)),
        ]
        + [pltpu.VMEM((2,) + x.shape[:-2] + (x.shape[-2] // 2, x.shape[-1]), f32) for x in outputs],
        compiler_params=params(),
        cost_estimate=cost(0, 12 * whole * width),
        name=name,
    )(scalars, *sums)


def final_mlp_call(scalars, sums, width):
    half = width // 2

    def body(held, side, core, wide, sinks):
        at = pl.multiple_of(core * half, half)
        for n in range(2):
            wide[n][side] = held[side, n * half : (n + 1) * half, :].astype(f32)
            yield wide[n].at[side], sinks[n].at[pl.ds(at, half), :]

    return final_call("final_mlp", body, scalars, sums, [struct((width, width), f32)] * 2)


def final_attention_call(scalars, sums, width):
    local = width // 2
    first, deep = local // 2, width // 4

    def body(held, side, core, wide, sinks):
        wide[0][side] = held[side, :first, :].astype(f32)
        yield wide[0].at[side], sinks[0].at[pl.ds(pl.multiple_of(core * first, first), first), :]
        low = pl.multiple_of(core * 2 * deep, 2 * deep)
        for j in range(3):
            block = held[side, first + j * deep : first + (j + 1) * deep, :].astype(f32)
            wide[1][side, j, :deep, :] = block[:, :local]
            wide[1][side, j, deep:, :] = block[:, local:]
            yield wide[1].at[side, j], sinks[1].at[j, pl.ds(low, 2 * deep), :]

    return final_call(
        "final_attention", body, scalars, sums,
        [struct((local, width), f32), struct((3, width, local), f32)],
    )


def series_starts(lengths, rows):
    ends = jnp.cumsum(lengths)
    places = jnp.arange(rows, dtype=jnp.int32)
    passed = jnp.where(ends[None, :] <= places[:, None], ends[None, :], 0)
    return jnp.max(passed, axis=1, keepdims=True).astype(jnp.int32)


def per_device(tokens, lengths, w_qkv, w_out, w_up, w_down, norm_gain, norm_bias, cotangent):
    sec = lax.axis_index("section").astype(jnp.int32)
    tensor = lax.axis_index("tensor")
    rank = lax.axis_index("dp")
    count = lax.axis_size("dp")
    own_rows = tokens.shape[1]
    rows = 2 * own_rows
    width = tokens.shape[2]
    local = width // 2
    swap = [(0, 1), (1, 0)]
    bits = own_bits(sec, rank, count)
    fan = min(3, len(bits))
    size = 1 << fan
    ring_up, ring_down = ring_routes(count, size)
    in_ring = lax.rem(rank, size)
    place = jnp.where(lax.rem(in_ring, 2) == 0, in_ring // 2, size - 1 - in_ring // 2)
    slot_places = lax.rem(place + np.asarray(slot_steps(size), np.int32) + size, size).astype(jnp.int32)

    def across(shard):
        other = lax.ppermute(shard, "tensor", swap)
        return jnp.where(
            tensor == 0,
            jnp.concatenate([shard, other], axis=0),
            jnp.concatenate([other, shard], axis=0),
        )

    def to_other_core(value):
        return lax.ppermute(value, "section", swap)

    def swap_cores(value):
        return lax.ppermute(value, "section", swap)

    def swap_tensor(value):
        return lax.ppermute(value, "tensor", swap)

    def move(axis, route):
        return lambda value: lax.ppermute(value, axis, route)

    def doubled(held, away, step):
        low = bits[step] == 0
        return jnp.concatenate([jnp.where(low, held, away), jnp.where(low, away, held)], axis=0)

    def sum_steps(layer, send, kept):
        received = yield send, swap_cores
        rows = kept.shape[0] // 2

        def both(side):
            a = lax.dynamic_slice_in_dim(kept, side * rows, rows, 0).astype(f32)
            b = lax.dynamic_slice_in_dim(received, side * rows, rows, 0).astype(f32)
            return a + b

        away = yield both(1 - bits[0]).astype(bf16), move(("section", "dp"), pairs_of(count, 0))
        held = (both(bits[0]) + away.astype(f32)).astype(bf16)
        for step in range(1, len(bits)):
            rows //= 2
            part = lax.dynamic_slice_in_dim(held, (1 - bits[step]) * rows, rows, 0)
            rest = lax.dynamic_slice_in_dim(held, bits[step] * rows, rows, 0)
            away = yield part, move(("section", "dp"), pairs_of(count, step))
            held = (rest.astype(f32) + away.astype(f32)).astype(bf16)
        for step in reversed(range(len(bits))):
            away = yield held, move(("section", "dp"), pairs_of(count, step))
            held = doubled(held, away, step)
        far = yield held, move("section", [(1 - layer, layer)])
        return held, far

    def around(pair):
        return lax.ppermute(pair[0], "dp", ring_up), lax.ppermute(pair[1], "dp", ring_down)

    def spread_steps(piece, route):
        send = move("section", route)

        def both_ways(pair):
            return around(pair) + (send(pair[0]), send(pair[1]))

        def first_way(pair):
            return around(pair) + (send(pair[0]),)

        a, b, far = yield (piece, piece), first_way
        ups, downs, far_ups, far_downs = [piece, a], [b], [far], []
        for _ in range(size // 2 - 2):
            a, b, c, d = yield (ups[-1], downs[-1]), both_ways
            ups.append(a)
            downs.append(b)
            far_ups.append(c)
            far_downs.append(d)
        half = piece.shape[0] // 2
        whole = ups[-1], downs[-1]

        def last_way(pair):
            return around((pair[0][:half], pair[1][half:])) + (send(pair[0]), send(pair[1]))

        a, b, c, d = yield whole, last_way
        far_ups.append(c)
        far_downs.append(d)
        c, d = yield (a, b), lambda pair: (send(pair[0]), send(pair[1]))
        return ups + downs + [a, b], far_ups + far_downs + [c, d]

    def butterfly_steps(part):
        away = yield part, swap_cores
        part = part + away
        distance = 1
        while distance < count:
            away = yield part, move("dp", [(i, i ^ distance) for i in range(count)])
            part = part + away
            distance *= 2
        return part

    mine = (jnp.transpose(w_qkv[0], (1, 0, 2)), w_out[0], w_up[0], w_down[0])
    u0 = across(lax.dynamic_index_in_dim(tokens, sec, 0, False))
    start = series_starts(lax.dynamic_index_in_dim(lengths[0], sec, 0, False), rows)
    norms = jnp.concatenate([norm_gain[0], norm_bias[0]], axis=0)
    swap_norms = to_other_core(norms)
    norm_of = [
        jnp.where(sec == 0, norms, swap_norms),
        jnp.where(sec == 0, swap_norms, norms),
    ]

    spots = jnp.stack([place, sec]).astype(jnp.int32)
    cuts = cut_call(spots, size, mine)

    swapped = tuple(to_other_core(w) for w in mine)
    names = ("qkv", "out", "up", "down")
    mine_of, swapped_of = dict(zip(names, mine)), dict(zip(names, swapped))
    def to_outputs(pair):
        rows_of = [
            lax.dynamic_slice_in_dim(value, tensor * own_rows, own_rows, 0) for value in pair
        ]
        stay = jnp.where(sec == 0, rows_of[0], rows_of[1])
        go = jnp.where(sec == 0, rows_of[1], rows_of[0])
        came = to_other_core(go)
        return jnp.where(sec == 0, jnp.stack([stay, came]), jnp.stack([came, stay]))[None]

    own_weights = [Own(layer, sec, mine_of, swapped_of) for layer in range(2)]
    here = sec.reshape(1)
    gains = [[norm_of[layer][i : i + 1] for i in range(4)] for layer in range(2)]

    both_cores = [(0, 1), (1, 0)]
    sections = ("section", "tensor")
    attention_cut = swap_tensor(cuts[0])
    feed_cut = lax.ppermute(cuts[1], sections, [(0, 1), (1, 0)])
    span = width // size
    came = swap_cores(jnp.concatenate([attention_cut[span:], feed_cut[span:]], axis=0))
    first_piece = jnp.where(
        sec == 0, jnp.concatenate([attention_cut[:span], feed_cut[:span]], axis=0), came
    )
    second_piece = jnp.where(sec == 1, attention_cut[:span], came[:span])

    def slots_of(arrays, rows, last):
        half = span // 2
        return [((x, rows), (x, rows + half)) for x in arrays[: size - 1]] + [last(arrays[size - 1 :])]

    def pieces_of(gathered, rows, last):
        return Pieces(sec, slot_places, *(slots_of(arrays, rows, last) for arrays in gathered))

    half = span // 2
    first_gather = Flow(spread_steps(first_piece, both_cores))
    second_gather = Flow(spread_steps(second_piece, both_cores))
    operand = first_gather.advance()
    (u0, start), _ = lax.optimization_barrier(((u0, start), operand))
    a0 = first_call(here, own_weights[0], u0, start, gains[0][0], gains[0][2])
    whole_up = lax.ppermute(mine[2], sections, [(2, 3), (3, 2)])
    whole_down = lax.ppermute(mine[3], sections, [(2, 3), (3, 2)])
    together([first_gather], a0["h"])
    together([first_gather])
    together([first_gather])
    operands, (n1_zero, whole_up) = together([first_gather, second_gather], a0["n1"], whole_up)
    a0 = dict(a0, n1=n1_zero)
    gathered = finished(first_gather)
    far_zero = pieces_of(gathered, 0, lambda x: ((x[0], 0), (x[0], half)))
    far_two_zero = pieces_of(gathered, span, lambda x: ((x[1], 0), (x[1], half)))
    b0 = kernel_after(
        lambda *x: second_call(here, far_zero, *x), [], None,
        a0["n1"], start, a0["h"], gains[0][1], gains[0][3],
    )
    late, _ = lax.optimization_barrier((lax.dynamic_index_in_dim(cotangent, sec, 0, False), b0["h"]))
    gy1 = across(late)
    operands, (n2_zero,) = together([second_gather], b0["n2"])
    b0 = dict(b0, n2=n2_zero)
    c0 = kernel_after(
        lambda *x: feed_call(here, own_weights[0], far_two_zero, *x), [], None, b0["n2"], b0["h"]
    )
    operands, (u1, whole_down) = together([second_gather], c0["y"], whole_down)
    a1 = kernel_after(
        lambda *x: first_call(here, own_weights[1], *x), [], None, u1, start, gains[1][0], gains[1][2]
    )
    together([second_gather], a1["h"])
    far_one = pieces_of(finished(second_gather), 0, lambda x: ((x[0], 0), (x[1], 0)))
    b1 = kernel_after(
        lambda *x: second_call(here, far_one, *x), [], None,
        a1["n1"], start, a1["h"], gains[1][1], gains[1][3],
    )
    to_first = move("section", [(1, 0)])
    far_two_one = Own(
        1, sec, dict(up=whole_up, down=whole_down), dict(up=to_first(whole_up), down=to_first(whole_down))
    )
    c1 = kernel_after(
        lambda *x: feed_call(here, own_weights[1], far_two_one, *x), [], None, b1["n2"], b1["h"]
    )
    outputs = to_outputs([c0["y"], c1["y"]])

    def feed_back(layer, far_two, moving, last, gy, b, c):
        return kernel_after(
            lambda *x: feed_back_call(here, own_weights[layer], far_two, *x), moving, last,
            gy, c["slope"], c["slope_far"], b["h"], c["z"], b["n2"], gains[layer][1],
        )

    def heads_back(layer, moving, last, a, e):
        return kernel_after(
            lambda *x: heads_back_call(here, own_weights[layer], *x), moving, last,
            a["qkv"], start, e["gh"], a["o"], a["n1"],
        )

    def input_back(layer, far, moving, last, a, b, e, f, u):
        return kernel_after(
            lambda *x: input_back_call(here, own_weights[layer], far, *x), moving, last,
            b["qkv"], start, e["gh"], f["d"], e["dh"], u, gains[layer][0],
        )

    e1 = feed_back(1, far_two_one, [], None, gy1, b1, c1)
    outputs, gh = lax.optimization_barrier((outputs, e1["gh"]))
    e1 = dict(e1, gh=gh)
    sums = [Flow(sum_steps(1, e1["give"], e1["keep"]))]
    f1 = heads_back(1, sums, gh, a1, e1)
    sums.append(Flow(sum_steps(1, f1["give"], f1["keep"])))
    g1 = input_back(1, far_one, sums, f1["d"], a1, b1, e1, f1, c0["y"])
    e0 = feed_back(0, far_two_zero, sums, g1["du"], g1["du"], b0, c0)
    sums.append(Flow(sum_steps(0, e0["give"], e0["keep"])))
    f0 = heads_back(0, sums, e0["gh"], a0, e0)
    sums.append(Flow(sum_steps(0, f0["give"], f0["keep"])))
    sums[3].advance()
    g0 = input_back(0, far_zero, sums, f0["d"], a0, b0, e0, f0, u0)
    norm_grads = [
        jnp.concatenate([g["grads"][:1], e["grads"][:1], g["grads"][1:], e["grads"][1:]])
        for g, e in ((g0, e0), (g1, e1))
    ]
    norm_flow = Flow(butterfly_steps(jnp.concatenate(norm_grads, axis=0)))
    norm_flow.advance()
    grads_in = to_outputs([g0["du"], g1["du"]])
    for flow in sums:
        flow.advance(g0["du"])
    (grads_in, results), _ = lax.optimization_barrier(((grads_in, sums[3].results), g0["du"]))
    sums[3].results = results
    while any(not flow.done for flow in sums + [norm_flow]):
        for flow in sums + [norm_flow]:
            if not flow.done:
                flow.advance()
    parts = [flow.value for flow in sums]
    grad_down, grad_up = final_mlp_call(here, [*parts[2], *parts[0]], width)
    grad_out, grad_qkv = final_attention_call(here, [*parts[3], *parts[1]], width)
    norm_total = norm_flow.value
    norm_sum = jnp.where(sec == 0, norm_total[:4], norm_total[4:])
    norm_sum = lax.dynamic_slice_in_dim(norm_sum, tensor * local, local, 1)

    return (
        outputs,
        grads_in,
        jnp.transpose(grad_qkv, (1, 0, 2))[None],
        grad_out[None],
        grad_up[None],
        grad_down[None],
        norm_sum[None, :2],
        norm_sum[None, 2:],
    )


def solution(mesh):
    in_specs = (
        P(None, ("dp", "tensor"), None),
        P("dp", None, None),
        P("section", None, None, "tensor"),
        P("section", "tensor", None),
        P("section", None, "tensor"),
        P("section", "tensor", None),
        P("section", None, None),
        P("section", None, None),
        P(None, ("dp", "tensor"), None),
    )
    out_specs = (
        P("section", None, ("dp", "tensor"), None),
        P("section", None, ("dp", "tensor"), None),
        P("section", None, None, "tensor"),
        P("section", "tensor", None),
        P("section", None, "tensor"),
        P("section", "tensor", None),
        P("section", None, "tensor"),
        P("section", None, "tensor"),
    )
    return jax.shard_map(
        per_device, mesh=mesh, in_specs=in_specs, out_specs=out_specs, check_vma=False
    )
```

time: 1310 us -> 525 us (0.40)
  waiting for transfers between devices: 905 us -> 176 us
  matrix products: 211 us -> 0 us
  Pallas kernels: 0 us -> 184 us
  starting transfers between devices: 8.6 us -> 83.2 us
  local copies, waits for them, and re-layouts: 64.9 us -> 22.6 us
  blocking collectives: 22.1 us -> 0 us
  other arithmetic: 71.9 us -> 50.1 us
  between operations: 15.5 us -> 2.01 us
    psum x1 -> x0, waiting for transfers between devices: 495 us -> none  [per_device(): lax.psum((part_qkv, part_out, part_up, part_down, norm_local), 'dp')]
    all_gather x12 -> x0, waiting for transfers between devices: 218 us -> none  [the longest x6 109 us: gather_grads(): return lax.all_gather(shard, 'tensor', axis=0, tiled=True)]
    dot_general x57 -> x0, matrix products: 211 us -> none  [the longest x3 25.4 us: layer_backward(): jnp.einsum('hts,shd->thd', score_grad, key_rows, preferred_element_type=j...]
    pallas_call x0 -> x15, Pallas kernels: none -> 184 us  [the longest x12 170 us: room_call(): pl.pallas_call(whole, in_specs=[pl.BlockSpec(memory_space=pltpu.SMEM)] *...]
    reduce_scatter x12 -> x0, waiting for transfers between devices: 180 us -> none  [the longest x6 98.7 us: sum_partials(): lax.psum_scatter(term_rows.astype(jnp.bfloat16), 'tensor', scatter_dimens...]
    ppermute x4 -> x86, waiting for transfers between devices: 6.87 us -> 176 us  [the longest x51 103 us: move(): return lambda value: lax.ppermute(value, axis, route)]
    ppermute x4 -> x86, starting transfers between devices: 5.94 us -> 83.2 us  [the longest x51 39.7 us: move(): return lambda value: lax.ppermute(value, axis, route)]
    unnamed x186 -> x90, local copies, waits for them, and re-layouts: 42.9 us -> 7.19 us
  transfers between devices with their start and end apart: 30 -> 86, of which waited for: 27 -> 31; matrix products, arithmetic and copies ran while one was open for 10% -> 12% of each run, Pallas kernels for 0% -> 32%
where the time goes in v2:
time: 525 us; the launch traced here: 517 us
  Pallas kernels  184 us (35%)
  waiting for transfers between devices  176 us (34%)
  starting transfers between devices  83.2 us (16%)
  other arithmetic  50.1 us (10%)
  local copies, waits for them, and re-layouts  22.6 us (4%)
    pallas_call x12, Pallas kernels, room_call(): pl.pallas_call(whole, in_specs=[pl.BlockSpec(memory_space=pltpu.SMEM)] *...  170 us
    ppermute x51, waiting for transfers between devices, move(): return lambda value: lax.ppermute(value, axis, route)  103 us
    ppermute x51, starting transfers between devices, move(): return lambda value: lax.ppermute(value, axis, route)  39.7 us
    ppermute x8, waiting for transfers between devices, around(): lax.ppermute(pair[0], 'dp', ring_up)  39.1 us
    ppermute x8, starting transfers between devices, around(): lax.ppermute(pair[1], 'dp', ring_down)  13.2 us
    ppermute x8, starting transfers between devices, around(): lax.ppermute(pair[0], 'dp', ring_up)  12.8 us
    ppermute x8, waiting for transfers between devices, around(): lax.ppermute(pair[1], 'dp', ring_down)  11.1 us
    ppermute x1, waiting for transfers between devices, per_device(): feed_cut = lax.ppermute(cuts[1], sections, [(0, 1), (1, 0)])  11 us
  transfers between devices with their start and end apart: 86, of which 31 were waited for; matrix products, arithmetic and copies ran while one was open for 12% of the time, Pallas kernels for 32%

profile of v2, /device:TPU:0, one launch (start us, length us, event | category | flops | bytes accessed | tf_op | source)
XLA Modules:
  0.0 517.2 jit_solution(590982495762366539)
XLA Ops:
  1.8 3.1 cut.1
  4.9 2.6 collective-permute-start
  12.3 8.1 %collective-permute-done = bf16[256,1024]{1,0:T(8,128)(2,1)S(1)} collective-permute-done((bf16[256,1024]{1,0:T(8,128)(2,1)}, bf16[256,1024]{1,0:T(8,128)(2,1)S(1)}, u32[]{:S(2)}, u32[]{:S(2)}) %collective-permute-start) | collective-permute-done | bytes 524320 | tf_op jit(solution)/shard_map/ppermute | solution.py:776
  20.5 11.0 %collective-permute-done.1 = bf16[256,1024]{1,0:T(8,128)(2,1)S(1)} collective-permute-done((bf16[256,1024]{1,0:T(8,128)(2,1)}, bf16[256,1024]{1,0:T(8,128)(2,1)S(1)}, u32[]{:S(2)}, u32[]{:S(2)}) %collective-permute-start.1) | collective-permute-done | bytes 524320 | tf_op jit(solution)/shard_map/ppermute | solution.py:882
  41.1 3.0 maximum_select_fusion.refs_2_.refs_7_
  44.9 10.4 %first.2 = (bf16[512,1024]{1,0:T(8,128)(2,1)}, bf16[512,1536]{1,0:T(8,128)(2,1)}, bf16[512,512]{1,0:T(8,128)(2,1)}, f32[512,1024]{1,0:T(8,128)}) custom-call(s32[1]{0:T(128)} %bitcast.refs_0_.scalar_ref, s32[2]{0:T(128)} %pad_add_fusion.refs_1_.refs_2_, bf16[512,1024]{1,0:T(8,128)(2,1)} %maximum_select_fusion.refs_2_.refs_7_, s32[512,1]{1,0:T(8,128)} %copy.29.refs_3_, ...), custom_call_target="tpu_custom_call" | custom-call | flops 2415919104 | bytes 10496000 | tf_op jit(solution)/shard_map/first/pallas_call | solution.py:254
  58.4 11.3 %collective-permute-done.13.refs_9_.refs_11_.refs_16_.refs_12_ = bf16[256,1024]{1,0:T(8,128)(2,1)S(1)} collective-permute-done((bf16[256,1024]{1,0:T(8,128)(2,1)S(1)}, bf16[256,1024]{1,0:T(8,128)(2,1)S(1)}, u32[]{:S(2)}, u32[]{:S(2)}) %collective-permute-start.13) | collective-permute-done | bytes 524320 | tf_op jit(solution)/shard_map/ppermute | solution.py:809
  69.7 2.5 collective-permute-done.14.refs_12_.refs_14_.refs_19_.refs_15_
  75.6 11.4 %collective-permute-done.17.refs_10_.refs_12_.refs_17_.refs_13_ = bf16[256,1024]{1,0:T(8,128)(2,1)S(1)} collective-permute-done((bf16[256,1024]{1,0:T(8,128)(2,1)S(1)}, bf16[256,1024]{1,0:T(8,128)(2,1)S(1)}, u32[]{:S(2)}, u32[]{:S(2)}) %collective-permute-start.17) | collective-permute-done | bytes 524320 | tf_op jit(solution)/shard_map/ppermute | solution.py:809
  92.6 6.5 %collective-permute-done.21.refs_14_.refs_17_ = bf16[128,1024]{1,0:T(8,128)(2,1)S(1)} collective-permute-done((bf16[128,1024]{1,0:T(8,128)(2,1)S(1)}, bf16[128,1024]{1,0:T(8,128)(2,1)S(1)}, u32[]{:S(2)}, u32[]{:S(2)}) %collective-permute-start.21) | collective-permute-done | bytes 262176 | tf_op jit(solution)/shard_map/ppermute | solution.py:809
  103.5 6.2 %collective-permute-done.3.refs_8_.refs_11_ = bf16[128,1024]{1,0:T(8,128)(2,1)} collective-permute-done((bf16[128,1024]{1,0:T(8,128)(2,1)}, bf16[128,1024]{1,0:T(8,128)(2,1)}, u32[]{:S(2)}, u32[]{:S(2)}) %collective-permute-start.3) | collective-permute-done | bytes 262176 | tf_op jit(solution)/shard_map/ppermute | solution.py:809
  114.1 11.8 %second.2 = (bf16[512,1536]{1,0:T(8,128)(2,1)}, f32[512,1024]{1,0:T(8,128)}, bf16[512,1024]{1,0:T(8,128)(2,1)}) custom-call(s32[1]{0:T(128)} %bitcast.refs_0_.scalar_ref, s32[9]{0:T(128)} %pad_add_fusion.1.refs_1_.refs_2_, bf16[512,1024]{1,0:T(8,128)(2,1)} %get-tuple-element.286.refs_2_.refs_6_, s32[512,1]{1,0:T(8,128)} %copy.30.refs_3_, ...), custom_call_target="tpu_custom_call" | custom-call | flops 2415919104 | bytes 12068864 | tf_op jit(solution)/shard_map/second/pallas_call | solution.py:254
  128.3 12.6 %feed.2 = (bf16[512,1024]{1,0:T(8,128)(2,1)}, bf16[512,1024]{1,0:T(8,128)(2,1)}, bf16[512,1024]{1,0:T(8,128)(2,1)}, bf16[512,1024]{1,0:T(8,128)(2,1)}) custom-call(s32[1]{0:T(128)} %bitcast.refs_0_.scalar_ref, s32[2]{0:T(128)} %pad_add_fusion.refs_1_.refs_2_, s32[9]{0:T(128)} %pad_add_fusion.1.refs_1_.refs_2_, ...), custom_call_target="tpu_custom_call" | custom-call | flops 4294967296 | bytes 15728640 | tf_op jit(solution)/shard_map/feed/pallas_call | solution.py:254
  148.3 3.7 collective-permute-done.35.refs_10_.refs_13_
  156.8 9.9 %first.3 = (bf16[512,1024]{1,0:T(8,128)(2,1)}, bf16[512,1536]{1,0:T(8,128)(2,1)}, bf16[512,512]{1,0:T(8,128)(2,1)}, f32[512,1024]{1,0:T(8,128)}) custom-call(s32[1]{0:T(128)} %bitcast.refs_0_.scalar_ref, s32[2]{0:T(128)} %pad_add_fusion.3.refs_1_.refs_2_, bf16[512,1024]{1,0:T(8,128)(2,1)} %get-tuple-element.259.refs_2_.refs_7_, s32[512,1]{1,0:T(8,128)} %copy.31.refs_3_, ...), custom_call_target="tpu_custom_call" | custom-call | flops 2415919104 | bytes 10496000 | tf_op jit(solution)/shard_map/first/pallas_call | solution.py:254
  169.6 9.9 %collective-permute-start.40 = (bf16[64,1024]{1,0:T(8,128)(2,1)S(1)}, bf16[64,1024]{1,0:T(8,128)(2,1)S(1)}, u32[]{:S(2)}, u32[]{:S(2)}) collective-permute-start(bf16[64,1024]{1,0:T(8,128)(2,1)S(1)} %slice.104), channel_id=1, source_target_pairs={{4,0},{8,4},{12,8},{14,12},{10,14},{6,10},{2,6},{0,2},{5,1},{9,5},... | collective-permute-start | bytes 393224 | tf_op jit(solution)/shard_map/ppermute | solution.py:809
  180.0 4.0 collective-permute-done.40.refs_15_.refs_18_
  188.9 11.6 %second.3 = (bf16[512,1536]{1,0:T(8,128)(2,1)}, f32[512,1024]{1,0:T(8,128)}, bf16[512,1024]{1,0:T(8,128)(2,1)}) custom-call(s32[1]{0:T(128)} %bitcast.refs_0_.scalar_ref, s32[9]{0:T(128)} %pad_add_fusion.1.refs_1_.refs_2_, bf16[512,1024]{1,0:T(8,128)(2,1)} %get-tuple-element.249.refs_2_.refs_6_, s32[512,1]{1,0:T(8,128)} %copy.32.refs_3_, ...), custom_call_target="tpu_custom_call" | custom-call | flops 2415919104 | bytes 12068864 | tf_op jit(solution)/shard_map/second/pallas_call | solution.py:254
  201.9 10.7 %feed.3 = (bf16[512,1024]{1,0:T(8,128)(2,1)}, bf16[512,1024]{1,0:T(8,128)(2,1)}, bf16[512,1024]{1,0:T(8,128)(2,1)}, bf16[512,1024]{1,0:T(8,128)(2,1)}) custom-call(s32[1]{0:T(128)} %bitcast.refs_0_.scalar_ref, s32[2]{0:T(128)} %pad_add_fusion.3.refs_1_.refs_2_, s32[2]{0:T(128)} %pad_add_fusion.3.refs_1_.refs_2_, ...), custom_call_target="tpu_custom_call" | custom-call | flops 4294967296 | bytes 15728640 | tf_op jit(solution)/shard_map/feed/pallas_call | solution.py:254
  215.9 16.7 %feed_back.2 = (bf16[1024,1024]{1,0:T(8,128)(2,1)}, bf16[1024,1024]{1,0:T(8,128)(2,1)}, f32[512,1024]{1,0:T(8,128)}, bf16[512,1024]{1,0:T(8,128)(2,1)}, f32[2,1024]{1,0:T(2,128)}) custom-call(s32[1]{0:T(128)} %bitcast.refs_0_.scalar_ref, s32[2]{0:T(128)} %pad_add_fusion.3.refs_1_.refs_2_, s32[2]{0:T(128)} %pad_add_fusion.3.refs_1_.refs_2_, ...), custom_call_target="tpu_custom_call" | custom-call | flops 6442450944 | bytes 23080960 | tf_op jit(solution)/shard_map/feed_back/pallas_call | solution.py:254
  234.6 16.4 %heads_back.2 = (bf16[1024,1024]{1,0:T(8,128)(2,1)}, bf16[1024,1024]{1,0:T(8,128)(2,1)}, bf16[512,1536]{1,0:T(8,128)(2,1)}) custom-call(s32[1]{0:T(128)} %bitcast.refs_0_.scalar_ref, s32[2]{0:T(128)} %pad_add_fusion.3.refs_1_.refs_2_, bf16[512,1024]{1,0:T(8,128)(2,1)} %get-tuple-element.255.refs_2_.refs_3_, bf16[512,1536]{1,0:T(8,128)(2,1)} %get-tuple-element.246.refs_3_, ...), custom_call_target="tpu_custom_call" | custom-call | flops 4563402752 | bytes 11012096 | tf_op jit(solution)/shard_map/heads_back/pallas_call | solution.py:254
  251.7 2.6 add_convert_fusion.7
  256.1 18.5 %input_back.2 = (bf16[512,1024]{1,0:T(8,128)(2,1)}, f32[2,1024]{1,0:T(2,128)}) custom-call(s32[1]{0:T(128)} %bitcast.refs_0_.scalar_ref, s32[9]{0:T(128)} %pad_add_fusion.1.refs_1_.refs_2_, s32[2]{0:T(128)} %pad_add_fusion.3.refs_1_.refs_2_, bf16[512,1024]{1,0:T(8,128)(2,1)} %get-tuple-element.255.refs_2_.refs_3_, ...), custom_call_target="tpu_custom_call" | custom-call | flops 5637144576 | bytes 15742976 | tf_op jit(solution)/shard_map/input_back/pallas_call | solution.py:254
  274.6 2.6 add_convert_fusion.5
  281.8 16.7 %feed_back.3 = (bf16[1024,1024]{1,0:T(8,128)(2,1)}, bf16[1024,1024]{1,0:T(8,128)(2,1)}, f32[512,1024]{1,0:T(8,128)}, bf16[512,1024]{1,0:T(8,128)(2,1)}, f32[2,1024]{1,0:T(2,128)}) custom-call(s32[1]{0:T(128)} %bitcast.refs_0_.scalar_ref, s32[2]{0:T(128)} %pad_add_fusion.refs_1_.refs_2_, s32[9]{0:T(128)} %pad_add_fusion.1.refs_1_.refs_2_, ...), custom_call_target="tpu_custom_call" | custom-call | flops 6442450944 | bytes 23080960 | tf_op jit(solution)/shard_map/feed_back/pallas_call | solution.py:254
  303.4 16.2 %heads_back.3 = (bf16[1024,1024]{1,0:T(8,128)(2,1)}, bf16[1024,1024]{1,0:T(8,128)(2,1)}, bf16[512,1536]{1,0:T(8,128)(2,1)}) custom-call(s32[1]{0:T(128)} %bitcast.refs_0_.scalar_ref, s32[2]{0:T(128)} %pad_add_fusion.refs_1_.refs_2_, bf16[512,1024]{1,0:T(8,128)(2,1)} %get-tuple-element.296.refs_2_.refs_3_, bf16[512,1536]{1,0:T(8,128)(2,1)} %get-tuple-element.283.refs_3_, ...), custom_call_target="tpu_custom_call" | custom-call | flops 4563402752 | bytes 11012096 | tf_op jit(solution)/shard_map/heads_back/pallas_call | solution.py:254
  321.5 14.2 %collective-permute-done.54 = bf16[128,1024]{1,0:T(8,128)(2,1)S(1)} collective-permute-done((bf16[128,1024]{1,0:T(8,128)(2,1)S(1)}, bf16[128,1024]{1,0:T(8,128)(2,1)S(1)}, u32[]{:S(2)}, u32[]{:S(2)}) %collective-permute-start.54) | collective-permute-done | bytes 262176 | tf_op jit(solution)/shard_map/ppermute | solution.py:779
  339.7 2.5 collective-permute-start.66
  345.2 2.6 add_convert_fusion.2
  349.7 18.6 %input_back.3 = (bf16[512,1024]{1,0:T(8,128)(2,1)}, f32[2,1024]{1,0:T(2,128)}) custom-call(s32[1]{0:T(128)} %bitcast.refs_0_.scalar_ref, s32[9]{0:T(128)} %pad_add_fusion.1.refs_1_.refs_2_, s32[2]{0:T(128)} %pad_add_fusion.refs_1_.refs_2_, bf16[512,1024]{1,0:T(8,128)(2,1)} %get-tuple-element.296.refs_2_.refs_3_, ...), custom_call_target="tpu_custom_call" | custom-call | flops 5637144576 | bytes 15742976 | tf_op jit(solution)/shard_map/input_back/pallas_call | solution.py:254
  376.9 5.5 %collective-permute-done.67 = bf16[128,1024]{1,0:T(8,128)(2,1)S(1)} collective-permute-done((bf16[128,1024]{1,0:T(8,128)(2,1)S(1)}, bf16[128,1024]{1,0:T(8,128)(2,1)S(1)}, u32[]{:S(2)}, u32[]{:S(2)}) %collective-permute-start.67) | collective-permute-done | bytes 262176 | tf_op jit(solution)/shard_map/ppermute | solution.py:779
  383.7 9.5 %collective-permute-done.72 = bf16[256,1024]{1,0:T(8,128)(2,1)S(1)} collective-permute-done((bf16[256,1024]{1,0:T(8,128)(2,1)S(1)}, bf16[256,1024]{1,0:T(8,128)(2,1)S(1)}, u32[]{:S(2)}, u32[]{:S(2)}) %collective-permute-start.72) | collective-permute-done | bytes 524320 | tf_op jit(solution)/shard_map/ppermute | solution.py:779
  395.9 3.8 collective-permute-done.79
  399.7 6.9 %collective-permute-done.68 = bf16[256,1024]{1,0:T(8,128)(2,1)S(1)} collective-permute-done((bf16[256,1024]{1,0:T(8,128)(2,1)S(1)}, bf16[256,1024]{1,0:T(8,128)(2,1)S(1)}, u32[]{:S(2)}, u32[]{:S(2)}) %collective-permute-start.68) | collective-permute-done | bytes 524320 | tf_op jit(solution)/shard_map/ppermute | solution.py:779
  407.2 4.3 collective-permute-done.73
  411.7 17.7 %collective-permute-done.60 = bf16[256,1024]{1,0:T(8,128)(2,1)S(1)} collective-permute-done((bf16[256,1024]{1,0:T(8,128)(2,1)S(1)}, bf16[256,1024]{1,0:T(8,128)(2,1)S(1)}, u32[]{:S(2)}, u32[]{:S(2)}) %collective-permute-start.60) | collective-permute-done | bytes 524320 | tf_op jit(solution)/shard_map/ppermute | solution.py:779
  431.8 7.6 %collective-permute-done.61 = bf16[128,1024]{1,0:T(8,128)(2,1)S(1)} collective-permute-done((bf16[128,1024]{1,0:T(8,128)(2,1)S(1)}, bf16[128,1024]{1,0:T(8,128)(2,1)S(1)}, u32[]{:S(2)}, u32[]{:S(2)}) %collective-permute-start.61) | collective-permute-done | bytes 262176 | tf_op jit(solution)/shard_map/ppermute | solution.py:779
  442.0 7.6 %collective-permute-done.62 = bf16[128,1024]{1,0:T(8,128)(2,1)} collective-permute-done((bf16[128,1024]{1,0:T(8,128)(2,1)S(1)}, bf16[128,1024]{1,0:T(8,128)(2,1)}, u32[]{:S(2)}, u32[]{:S(2)}) %collective-permute-start.62) | collective-permute-done | bytes 262176 | tf_op jit(solution)/shard_map/ppermute | solution.py:779
  450.9 7.5 %collective-permute-done.75 = bf16[256,1024]{1,0:T(8,128)(2,1)S(1)} collective-permute-done((bf16[256,1024]{1,0:T(8,128)(2,1)}, bf16[256,1024]{1,0:T(8,128)(2,1)S(1)}, u32[]{:S(2)}, u32[]{:S(2)}) %collective-permute-start.75) | collective-permute-done | bytes 524320 | tf_op jit(solution)/shard_map/ppermute | solution.py:779
  461.6 8.0 %collective-permute-done.63 = bf16[256,1024]{1,0:T(8,128)(2,1)S(1)} collective-permute-done((bf16[256,1024]{1,0:T(8,128)(2,1)S(1)}, bf16[256,1024]{1,0:T(8,128)(2,1)S(1)}, u32[]{:S(2)}, u32[]{:S(2)}) %collective-permute-start.63) | collective-permute-done | bytes 524320 | tf_op jit(solution)/shard_map/ppermute | solution.py:779
  471.2 2.6 collective-permute-start.81
  475.9 2.7 collective-permute-start.70
  482.2 2.7 collective-permute-done.64
  488.5 2.5 collective-permute-start.82
  494.2 2.9 collective-permute-done.83
  501.1 2.5 collective-permute-start.85
  506.5 5.2 %final_mlp.1 = (f32[1024,1024]{1,0:T(8,128)}, f32[1024,1024]{1,0:T(8,128)}) custom-call(s32[1]{0:T(128)} %bitcast.refs_0_.scalar_ref, bf16[1024,1024]{1,0:T(8,128)(2,1)} %pad_maximum_fusion.2.own0, bf16[1024,1024]{1,0:T(8,128)(2,1)} %collective-permute-done.77.far0, bf16[1024,1024]{1,0:T(8,128)(2,1)} %copy-done.5, ...), custom_call_target="tpu_custom_call" | custom-call | bytes 12582912 | tf_op jit(solution)/shard_map/final_mlp/pallas_call | solution.py:687
  511.8 5.2 %final_attention.1 = (f32[512,1024]{1,0:T(8,128)}, f32[3,1024,512]{2,1,0:T(8,128)}) custom-call(s32[1]{0:T(128)} %bitcast.refs_0_.scalar_ref, bf16[1024,1024]{1,0:T(8,128)(2,1)} %pad_maximum_fusion.own0, bf16[1024,1024]{1,0:T(8,128)(2,1)} %collective-permute-done.65.far0, bf16[1024,1024]{1,0:T(8,128)(2,1)} %pad_maximum_fusion.1.own1, ...), custom_call_target="tpu_custom_call" | custom-call | bytes 12582912 | tf_op jit(solution)/shard_map/final_attention/pallas_call | solution.py:687
  (326 shorter events, 132.4 us)
Async XLA Ops:
  0.6 44.2 %collective-permute-start.11 = (bf16[3,1024,512]{2,1,0:T(8,128)(2,1)}, bf16[3,1024,512]{2,1,0:T(8,128)(2,1)}, u32[]{:S(2)}, u32[]{:S(2)}) collective-permute-start(bf16[3,1024,512]{2,1,0:T(8,128)(2,1)} %bitcast.33), channel_id=1, source_target_pairs={{0,16},{16,0},{1,17},{17,1},{2,18},{18,2},{3,19},{19,3},{4,20},{20... | collective-permute-start | bytes 9437192 | tf_op jit(solution)/shard_map/ppermute | solution.py:770
  4.9 15.6 %collective-permute-start = (bf16[256,1024]{1,0:T(8,128)(2,1)}, bf16[256,1024]{1,0:T(8,128)(2,1)S(1)}, u32[]{:S(2)}, u32[]{:S(2)}) collective-permute-start(bf16[256,1024]{1,0:T(8,128)(2,1)} %get-tuple-element.163), channel_id=1, source_target_pairs={{0,1},{1,0},{2,3},{3,2},{4,5},{5,4},{6,7},{7,6},{8,9},{9,8},{10,11... | collective-permute-start | bytes 1572872 | tf_op jit(solution)/shard_map/ppermute | solution.py:776
  7.5 24.0 %collective-permute-start.1 = (bf16[256,1024]{1,0:T(8,128)(2,1)}, bf16[256,1024]{1,0:T(8,128)(2,1)S(1)}, u32[]{:S(2)}, u32[]{:S(2)}) collective-permute-start(bf16[256,1024]{1,0:T(8,128)(2,1)} %get-tuple-element.164), channel_id=1, source_target_pairs={{0,1},{1,0},{2,3},{3,2},{4,5},{5,4},{6,7},{7,6},{8,9},{9,8},{10,11... | collective-permute-start | bytes 1572872 | tf_op jit(solution)/shard_map/ppermute | solution.py:882
  9.4 29.7 %collective-permute-start.12 = (bf16[512,1024]{1,0:T(8,128)(2,1)}, bf16[512,1024]{1,0:T(8,128)(2,1)}, u32[]{:S(2)}, u32[]{:S(2)}) collective-permute-start(bf16[512,1024]{1,0:T(8,128)(2,1)} %bitcast.4.out.refs_7_), channel_id=1, source_target_pairs={{0,16},{16,0},{1,17},{17,1},{2,18},{18,2},{3,19},{19,3},{4,20},{20... | collective-permute-start | bytes 3145736 | tf_op jit(solution)/shard_map/ppermute | solution.py:770
  10.3 28.1 %collective-permute-start.9 = (bf16[256,1024]{1,0:T(8,128)(2,1)}, bf16[256,1024]{1,0:T(8,128)(2,1)}, u32[]{:S(2)}, u32[]{:S(2)}) collective-permute-start(bf16[256,1024]{1,0:T(8,128)(2,1)} %dynamic-slice_bitcast_fusion.1), channel_id=1, source_target_pairs={{0,1},{1,0},{2,3},{3,2},{4,5},{5,4},{6,7},{7,6},{8,9},{9,8},{10,11... | collective-permute-start | bytes 1572872 | tf_op jit(solution)/shard_map/ppermute | solution.py:762
  36.4 18.9 %collective-permute-start.6 = (bf16[256,1024]{1,0:T(8,128)(2,1)S(1)}, bf16[256,1024]{1,0:T(8,128)(2,1)S(1)}, u32[]{:S(2)}, u32[]{:S(2)}) collective-permute-start(bf16[256,1024]{1,0:T(8,128)(2,1)S(1)} %maximum_select_fusion.4.refs_7_.refs_9_.refs_14_.refs_10_), channel_id=1, source_target_pairs={{0,4},{4,8},{8,12},{12,14},{14,10},{10,6},{6,2},{2,0},{1,5},{5,9},... | collective-permute-start | bytes 1572872 | tf_op jit(solution)/shard_map/ppermute | solution.py:809
  38.2 17.1 %collective-permute-start.7 = (bf16[256,1024]{1,0:T(8,128)(2,1)S(1)}, bf16[256,1024]{1,0:T(8,128)(2,1)}, u32[]{:S(2)}, u32[]{:S(2)}) collective-permute-start(bf16[256,1024]{1,0:T(8,128)(2,1)S(1)} %maximum_select_fusion.4.refs_7_.refs_9_.refs_14_.refs_10_), channel_id=1, source_target_pairs={{4,0},{8,4},{12,8},{14,12},{10,14},{6,10},{2,6},{0,2},{5,1},{9,5},... | collective-permute-start | bytes 1572872 | tf_op jit(solution)/shard_map/ppermute | solution.py:809
  38.5 16.9 %collective-permute-start.8 = (bf16[256,1024]{1,0:T(8,128)(2,1)S(1)}, bf16[256,1024]{1,0:T(8,128)(2,1)}, u32[]{:S(2)}, u32[]{:S(2)}) collective-permute-start(bf16[256,1024]{1,0:T(8,128)(2,1)S(1)} %maximum_select_fusion.4.refs_7_.refs_9_.refs_14_.refs_10_), channel_id=1, source_target_pairs={{0,16},{16,0},{1,17},{17,1},{2,18},{18,2},{3,19},{19,3},{4,20},{20... | collective-permute-start | bytes 1572872 | tf_op jit(solution)/shard_map/ppermute | solution.py:779
  39.1 53.0 %collective-permute-start.25 = (bf16[1024,1024]{1,0:T(8,128)(2,1)S(1)}, bf16[1024,1024]{1,0:T(8,128)(2,1)}, u32[]{:S(2)}, u32[]{:S(2)}) collective-permute-start(bf16[1024,1024]{1,0:T(8,128)(2,1)S(1)} %bitcast.44), channel_id=1, source_target_pairs={{16,17},{17,16},{18,19},{19,18},{20,21},{21,20},{22,23},{23,22},{2... | collective-permute-start | bytes 6291464 | tf_op jit(solution)/shard_map/ppermute | solution.py:903
  57.2 15.0 %collective-permute-start.14 = (bf16[256,1024]{1,0:T(8,128)(2,1)}, bf16[256,1024]{1,0:T(8,128)(2,1)S(1)}, u32[]{:S(2)}, u32[]{:S(2)}) collective-permute-start(bf16[256,1024]{1,0:T(8,128)(2,1)} %collective-permute-done.7.refs_11_.refs_13_.refs_18_.refs_14_), channel_id=1, source_target_pairs={{4,0},{8,4},{12,8},{14,12},{10,14},{6,10},{2,6},{0,2},{5,1},{9,5},... | collective-permute-start | bytes 1572872 | tf_op jit(solution)/shard_map/ppermute | solution.py:809
  75.1 15.3 %collective-permute-start.20 = (bf16[256,1024]{1,0:T(8,128)(2,1)S(1)}, bf16[256,1024]{1,0:T(8,128)(2,1)}, u32[]{:S(2)}, u32[]{:S(2)}) collective-permute-start(bf16[256,1024]{1,0:T(8,128)(2,1)S(1)} %collective-permute-done.14.refs_12_.refs_14_.refs_19_.refs_15_), channel_id=1, source_target_pairs={{0,16},{16,0},{1,17},{17,1},{2,18},{18,2},{3,19},{19,3},{4,20},{20... | collective-permute-start | bytes 1572872 | tf_op jit(solution)/shard_map/ppermute | solution.py:779
  87.0 40.5 %collective-permute-start.27 = (bf16[1024,1024]{1,0:T(8,128)(2,1)S(1)}, bf16[1024,1024]{1,0:T(8,128)(2,1)}, u32[]{:S(2)}, u32[]{:S(2)}) collective-permute-start(bf16[1024,1024]{1,0:T(8,128)(2,1)S(1)} %bitcast.45), channel_id=1, source_target_pairs={{0,16},{16,0},{1,17},{17,1},{2,18},{18,2},{3,19},{19,3},{4,20},{20... | collective-permute-start | bytes 6291464 | tf_op jit(solution)/shard_map/ppermute | solution.py:770
  88.3 39.2 %collective-permute-start.28 = (bf16[1024,1024]{1,0:T(8,128)(2,1)}, bf16[1024,1024]{1,0:T(8,128)(2,1)}, u32[]{:S(2)}, u32[]{:S(2)}) collective-permute-start(bf16[1024,1024]{1,0:T(8,128)(2,1)} %bitcast.47), channel_id=1, source_target_pairs={{0,16},{16,0},{1,17},{17,1},{2,18},{18,2},{3,19},{19,3},{4,20},{20... | collective-permute-start | bytes 6291464 | tf_op jit(solution)/shard_map/ppermute | solution.py:770
  88.4 52.5 %collective-permute-start.34 = (bf16[1024,1024]{1,0:T(8,128)(2,1)}, bf16[1024,1024]{1,0:T(8,128)(2,1)}, u32[]{:S(2)}, u32[]{:S(2)}) collective-permute-start(bf16[1024,1024]{1,0:T(8,128)(2,1)} %bitcast.48), channel_id=1, source_target_pairs={{16,17},{17,16},{18,19},{19,18},{20,21},{21,20},{22,23},{23,22},{2... | collective-permute-start | bytes 6291464 | tf_op jit(solution)/shard_map/ppermute | solution.py:904
  112.2 16.0 %collective-permute-start.29 = (bf16[128,1024]{1,0:T(8,128)(2,1)}, bf16[128,1024]{1,0:T(8,128)(2,1)}, u32[]{:S(2)}, u32[]{:S(2)}) collective-permute-start(bf16[128,1024]{1,0:T(8,128)(2,1)} %collective-permute-done.22.refs_16_.refs_21_), channel_id=1, source_target_pairs={{0,16},{16,0},{1,17},{17,1},{2,18},{18,2},{3,19},{19,3},{4,20},{20... | collective-permute-start | bytes 786440 | tf_op jit(solution)/shard_map/ppermute | solution.py:779
  126.0 16.2 %collective-permute-start.30 = (bf16[128,1024]{1,0:T(8,128)(2,1)}, bf16[128,1024]{1,0:T(8,128)(2,1)}, u32[]{:S(2)}, u32[]{:S(2)}) collective-permute-start(bf16[128,1024]{1,0:T(8,128)(2,1)} %collective-permute-done.3.refs_8_.refs_11_), channel_id=1, source_target_pairs={{0,4},{4,8},{8,12},{12,14},{14,10},{10,6},{6,2},{2,0},{1,5},{5,9},... | collective-permute-start | bytes 786440 | tf_op jit(solution)/shard_map/ppermute | solution.py:809
  140.9 59.7 %collective-permute-start.45 = (bf16[1024,1024]{1,0:T(8,128)(2,1)}, bf16[1024,1024]{1,0:T(8,128)(2,1)S(1)}, u32[]{:S(2)}, u32[]{:S(2)}) collective-permute-start(bf16[1024,1024]{1,0:T(8,128)(2,1)} %collective-permute-done.25.refs_9_.refs_15_), channel_id=1, source_target_pairs={{16,0},{17,1},{18,2},{19,3},{20,4},{21,5},{22,6},{23,7},{24,8},{25... | collective-permute-start | bytes 6291464 | tf_op jit(solution)/shard_map/ppermute | solution.py:779
  142.9 57.7 %collective-permute-start.46 = (bf16[1024,1024]{1,0:T(8,128)(2,1)}, bf16[1024,1024]{1,0:T(8,128)(2,1)}, u32[]{:S(2)}, u32[]{:S(2)}) collective-permute-start(bf16[1024,1024]{1,0:T(8,128)(2,1)} %collective-permute-done.34.refs_10_.refs_14_), channel_id=1, source_target_pairs={{16,0},{17,1},{18,2},{19,3},{20,4},{21,5},{22,6},{23,7},{24,8},{25... | collective-permute-start | bytes 6291464 | tf_op jit(solution)/shard_map/ppermute | solution.py:779
  148.0 31.5 %collective-permute-start.48 = (bf16[256,1024]{1,0:T(8,128)(2,1)S(1)}, bf16[256,1024]{1,0:T(8,128)(2,1)S(1)}, u32[]{:S(2)}, u32[]{:S(2)}) collective-permute-start(bf16[256,1024]{1,0:T(8,128)(2,1)S(1)} %dynamic-slice_bitcast_fusion), channel_id=1, source_target_pairs={{0,1},{1,0},{2,3},{3,2},{4,5},{5,4},{6,7},{7,6},{8,9},{9,8},{10,11... | collective-permute-start | bytes 1572872 | tf_op jit(solution)/shard_map/ppermute | solution.py:762
  214.0 18.7 %collective-permute-start.47 = (bf16[256,1024]{1,0:T(8,128)(2,1)S(1)}, bf16[256,1024]{1,0:T(8,128)(2,1)S(1)}, u32[]{:S(2)}, u32[]{:S(2)}) collective-permute-start(bf16[256,1024]{1,0:T(8,128)(2,1)S(1)} %get-tuple-element.329), channel_id=1, source_target_pairs={{0,16},{16,0},{1,17},{17,1},{2,18},{18,2},{3,19},{19,3},{4,20},{20... | collective-permute-start | bytes 1572872 | tf_op jit(solution)/shard_map/ppermute | solution.py:770
  232.5 19.1 %collective-permute-start.49 = (bf16[1024,1024]{1,0:T(8,128)(2,1)}, bf16[1024,1024]{1,0:T(8,128)(2,1)}, u32[]{:S(2)}, u32[]{:S(2)}) collective-permute-start(bf16[1024,1024]{1,0:T(8,128)(2,1)} %get-tuple-element.244), channel_id=1, source_target_pairs={{0,16},{16,0},{1,17},{17,1},{2,18},{18,2},{3,19},{19,3},{4,20},{20... | collective-permute-start | bytes 6291464 | tf_op jit(solution)/shard_map/ppermute | solution.py:773
  251.1 23.5 %collective-permute-start.51 = (bf16[1024,1024]{1,0:T(8,128)(2,1)}, bf16[1024,1024]{1,0:T(8,128)(2,1)}, u32[]{:S(2)}, u32[]{:S(2)}) collective-permute-start(bf16[1024,1024]{1,0:T(8,128)(2,1)} %get-tuple-element.254), channel_id=1, source_target_pairs={{0,16},{16,0},{1,17},{17,1},{2,18},{18,2},{3,19},{19,3},{4,20},{20... | collective-permute-start | bytes 6291464 | tf_op jit(solution)/shard_map/ppermute | solution.py:773
  254.3 24.0 %collective-permute-start.50 = (bf16[512,1024]{1,0:T(8,128)(2,1)}, bf16[512,1024]{1,0:T(8,128)(2,1)S(1)}, u32[]{:S(2)}, u32[]{:S(2)}) collective-permute-start(bf16[512,1024]{1,0:T(8,128)(2,1)} %add_convert_fusion.7), channel_id=1, source_target_pairs={{0,2},{2,0},{4,6},{6,4},{8,10},{10,8},{12,14},{14,12},{16,20},{18,... | collective-permute-start | bytes 3145736 | tf_op jit(solution)/shard_map/ppermute | solution.py:779
  277.2 22.1 %collective-permute-start.53 = (bf16[512,1024]{1,0:T(8,128)(2,1)}, bf16[512,1024]{1,0:T(8,128)(2,1)S(1)}, u32[]{:S(2)}, u32[]{:S(2)}) collective-permute-start(bf16[512,1024]{1,0:T(8,128)(2,1)} %add_convert_fusion.5), channel_id=1, source_target_pairs={{0,2},{2,0},{4,6},{6,4},{8,10},{10,8},{12,14},{14,12},{16,20},{18,... | collective-permute-start | bytes 3145736 | tf_op jit(solution)/shard_map/ppermute | solution.py:779
  281.3 21.0 %collective-permute-start.52 = (bf16[256,1024]{1,0:T(8,128)(2,1)}, bf16[256,1024]{1,0:T(8,128)(2,1)S(1)}, u32[]{:S(2)}, u32[]{:S(2)}) collective-permute-start(bf16[256,1024]{1,0:T(8,128)(2,1)} %constant_dynamic-slice_fusion.9), channel_id=1, source_target_pairs={{0,4},{2,6},{4,0},{6,2},{8,12},{10,14},{12,8},{14,10},{16,18},{18,... | collective-permute-start | bytes 1572872 | tf_op jit(solution)/shard_map/ppermute | solution.py:779
  298.6 43.6 %collective-permute-start.56 = (bf16[1024,1024]{1,0:T(8,128)(2,1)}, bf16[1024,1024]{1,0:T(8,128)(2,1)}, u32[]{:S(2)}, u32[]{:S(2)}) collective-permute-start(bf16[1024,1024]{1,0:T(8,128)(2,1)} %get-tuple-element.281), channel_id=1, source_target_pairs={{0,16},{16,0},{1,17},{17,1},{2,18},{18,2},{3,19},{19,3},{4,20},{20... | collective-permute-start | bytes 6291464 | tf_op jit(solution)/shard_map/ppermute | solution.py:773
  319.7 25.5 %collective-permute-start.57 = (bf16[1024,1024]{1,0:T(8,128)(2,1)}, bf16[1024,1024]{1,0:T(8,128)(2,1)}, u32[]{:S(2)}, u32[]{:S(2)}) collective-permute-start(bf16[1024,1024]{1,0:T(8,128)(2,1)} %get-tuple-element.294), channel_id=1, source_target_pairs={{0,16},{16,0},{1,17},{17,1},{2,18},{18,2},{3,19},{19,3},{4,20},{20... | collective-permute-start | bytes 6291464 | tf_op jit(solution)/shard_map/ppermute | solution.py:773
  319.8 18.1 %collective-permute-start.55 = (bf16[256,1024]{1,0:T(8,128)(2,1)S(1)}, bf16[256,1024]{1,0:T(8,128)(2,1)S(1)}, u32[]{:S(2)}, u32[]{:S(2)}) collective-permute-start(bf16[256,1024]{1,0:T(8,128)(2,1)S(1)} %copy-done.26), channel_id=1, source_target_pairs={{0,4},{2,6},{4,0},{6,2},{8,12},{10,14},{12,8},{14,10},{16,18},{18,... | collective-permute-start | bytes 1572872 | tf_op jit(solution)/shard_map/ppermute | solution.py:779
  337.5 32.5 %collective-permute-start.78 = (bf16[128,1024]{1,0:T(8,128)(2,1)S(1)}, bf16[128,1024]{1,0:T(8,128)(2,1)}, u32[]{:S(2)}, u32[]{:S(2)}) collective-permute-start(bf16[128,1024]{1,0:T(8,128)(2,1)S(1)} %add_convert_fusion.15), channel_id=1, source_target_pairs={{0,8},{2,10},{4,12},{6,14},{8,0},{10,2},{12,4},{14,6},{16,24},{18,... | collective-permute-start | bytes 786440 | tf_op jit(solution)/shard_map/ppermute | solution.py:779
  339.7 28.6 %collective-permute-start.66 = (bf16[128,1024]{1,0:T(8,128)(2,1)}, bf16[128,1024]{1,0:T(8,128)(2,1)}, u32[]{:S(2)}, u32[]{:S(2)}) collective-permute-start(bf16[128,1024]{1,0:T(8,128)(2,1)} %constant_dynamic-slice_fusion.6), channel_id=1, source_target_pairs={{0,8},{2,10},{4,12},{6,14},{8,0},{10,2},{12,4},{14,6},{16,24},{18,... | collective-permute-start | bytes 786440 | tf_op jit(solution)/shard_map/ppermute | solution.py:779
  344.1 28.4 %collective-permute-start.71 = (bf16[512,1024]{1,0:T(8,128)(2,1)S(1)}, bf16[512,1024]{1,0:T(8,128)(2,1)}, u32[]{:S(2)}, u32[]{:S(2)}) collective-permute-start(bf16[512,1024]{1,0:T(8,128)(2,1)S(1)} %add_convert_fusion.3), channel_id=1, source_target_pairs={{0,2},{2,0},{4,6},{6,4},{8,10},{10,8},{12,14},{14,12},{16,20},{18,... | collective-permute-start | bytes 3145736 | tf_op jit(solution)/shard_map/ppermute | solution.py:779
  347.8 45.7 %collective-permute-start.59 = (bf16[512,1024]{1,0:T(8,128)(2,1)}, bf16[512,1024]{1,0:T(8,128)(2,1)}, u32[]{:S(2)}, u32[]{:S(2)}) collective-permute-start(bf16[512,1024]{1,0:T(8,128)(2,1)} %add_convert_fusion.2), channel_id=1, source_target_pairs={{0,2},{2,0},{4,6},{6,4},{8,10},{10,8},{12,14},{14,12},{16,20},{18,... | collective-permute-start | bytes 3145736 | tf_op jit(solution)/shard_map/ppermute | solution.py:779
  374.7 18.5 %collective-permute-start.72 = (bf16[256,1024]{1,0:T(8,128)(2,1)S(1)}, bf16[256,1024]{1,0:T(8,128)(2,1)S(1)}, u32[]{:S(2)}, u32[]{:S(2)}) collective-permute-start(bf16[256,1024]{1,0:T(8,128)(2,1)S(1)} %constant_dynamic-slice_fusion.2), channel_id=1, source_target_pairs={{0,4},{2,6},{4,0},{6,2},{8,12},{10,14},{12,8},{14,10},{16,18},{18,... | collective-permute-start | bytes 1572872 | tf_op jit(solution)/shard_map/ppermute | solution.py:779
  374.9 24.8 %collective-permute-start.79 = (bf16[256,1024]{1,0:T(8,128)(2,1)S(1)}, bf16[256,1024]{1,0:T(8,128)(2,1)S(1)}, u32[]{:S(2)}, u32[]{:S(2)}) collective-permute-start(bf16[256,1024]{1,0:T(8,128)(2,1)S(1)} %pad_maximum_fusion.12), channel_id=1, source_target_pairs={{0,4},{2,6},{4,0},{6,2},{8,12},{10,14},{12,8},{14,10},{16,18},{18,... | collective-permute-start | bytes 1572872 | tf_op jit(solution)/shard_map/ppermute | solution.py:779
  382.5 24.1 %collective-permute-start.68 = (bf16[256,1024]{1,0:T(8,128)(2,1)S(1)}, bf16[256,1024]{1,0:T(8,128)(2,1)S(1)}, u32[]{:S(2)}, u32[]{:S(2)}) collective-permute-start(bf16[256,1024]{1,0:T(8,128)(2,1)S(1)} %pad_maximum_fusion.10), channel_id=1, source_target_pairs={{0,4},{2,6},{4,0},{6,2},{8,12},{10,14},{12,8},{14,10},{16,18},{18,... | collective-permute-start | bytes 1572872 | tf_op jit(solution)/shard_map/ppermute | solution.py:779
  393.5 18.1 %collective-permute-start.73 = (bf16[128,1024]{1,0:T(8,128)(2,1)S(1)}, bf16[128,1024]{1,0:T(8,128)(2,1)S(1)}, u32[]{:S(2)}, u32[]{:S(2)}) collective-permute-start(bf16[128,1024]{1,0:T(8,128)(2,1)S(1)} %constant_dynamic-slice_fusion.1), channel_id=1, source_target_pairs={{0,8},{2,10},{4,12},{6,14},{8,0},{10,2},{12,4},{14,6},{16,24},{18,... | collective-permute-start | bytes 786440 | tf_op jit(solution)/shard_map/ppermute | solution.py:779
  395.8 33.6 %collective-permute-start.60 = (bf16[256,1024]{1,0:T(8,128)(2,1)S(1)}, bf16[256,1024]{1,0:T(8,128)(2,1)S(1)}, u32[]{:S(2)}, u32[]{:S(2)}) collective-permute-start(bf16[256,1024]{1,0:T(8,128)(2,1)S(1)} %constant_dynamic-slice_fusion.5), channel_id=1, source_target_pairs={{0,4},{2,6},{4,0},{6,2},{8,12},{10,14},{12,8},{14,10},{16,18},{18,... | collective-permute-start | bytes 1572872 | tf_op jit(solution)/shard_map/ppermute | solution.py:779
  411.6 20.2 %collective-permute-start.74 = (bf16[128,1024]{1,0:T(8,128)(2,1)S(1)}, bf16[128,1024]{1,0:T(8,128)(2,1)S(1)}, u32[]{:S(2)}, u32[]{:S(2)}) collective-permute-start(bf16[128,1024]{1,0:T(8,128)(2,1)S(1)} %add_convert_fusion.12), channel_id=1, source_target_pairs={{0,8},{2,10},{4,12},{6,14},{8,0},{10,2},{12,4},{14,6},{16,24},{18,... | collective-permute-start | bytes 786440 | tf_op jit(solution)/shard_map/ppermute | solution.py:779
  430.8 29.1 %collective-permute-start.80 = (bf16[512,1024]{1,0:T(8,128)(2,1)}, bf16[512,1024]{1,0:T(8,128)(2,1)}, u32[]{:S(2)}, u32[]{:S(2)}) collective-permute-start(bf16[512,1024]{1,0:T(8,128)(2,1)} %pad_maximum_fusion.7), channel_id=1, source_target_pairs={{0,2},{2,0},{4,6},{6,4},{8,10},{10,8},{12,14},{14,12},{16,20},{18,... | collective-permute-start | bytes 3145736 | tf_op jit(solution)/shard_map/ppermute | solution.py:779
  440.8 17.6 %collective-permute-start.75 = (bf16[256,1024]{1,0:T(8,128)(2,1)}, bf16[256,1024]{1,0:T(8,128)(2,1)S(1)}, u32[]{:S(2)}, u32[]{:S(2)}) collective-permute-start(bf16[256,1024]{1,0:T(8,128)(2,1)} %pad_maximum_fusion.11), channel_id=1, source_target_pairs={{0,4},{2,6},{4,0},{6,2},{8,12},{10,14},{12,8},{14,10},{16,18},{18,... | collective-permute-start | bytes 1572872 | tf_op jit(solution)/shard_map/ppermute | solution.py:779
  440.9 33.0 %collective-permute-start.69 = (bf16[512,1024]{1,0:T(8,128)(2,1)S(1)}, bf16[512,1024]{1,0:T(8,128)(2,1)S(1)}, u32[]{:S(2)}, u32[]{:S(2)}) collective-permute-start(bf16[512,1024]{1,0:T(8,128)(2,1)S(1)} %pad_maximum_fusion.5), channel_id=1, source_target_pairs={{0,2},{2,0},{4,6},{6,4},{8,10},{10,8},{12,14},{14,12},{16,20},{18,... | collective-permute-start | bytes 3145736 | tf_op jit(solution)/shard_map/ppermute | solution.py:779
  450.6 19.0 %collective-permute-start.63 = (bf16[256,1024]{1,0:T(8,128)(2,1)S(1)}, bf16[256,1024]{1,0:T(8,128)(2,1)S(1)}, u32[]{:S(2)}, u32[]{:S(2)}) collective-permute-start(bf16[256,1024]{1,0:T(8,128)(2,1)S(1)} %pad_maximum_fusion.9), channel_id=1, source_target_pairs={{0,4},{2,6},{4,0},{6,2},{8,12},{10,14},{12,8},{14,10},{16,18},{18,... | collective-permute-start | bytes 1572872 | tf_op jit(solution)/shard_map/ppermute | solution.py:779
  458.8 19.8 %collective-permute-start.76 = (bf16[512,1024]{1,0:T(8,128)(2,1)S(1)}, bf16[512,1024]{1,0:T(8,128)(2,1)S(1)}, u32[]{:S(2)}, u32[]{:S(2)}) collective-permute-start(bf16[512,1024]{1,0:T(8,128)(2,1)S(1)} %pad_maximum_fusion.6), channel_id=1, source_target_pairs={{0,2},{2,0},{4,6},{6,4},{8,10},{10,8},{12,14},{14,12},{16,20},{18,... | collective-permute-start | bytes 3145736 | tf_op jit(solution)/shard_map/ppermute | solution.py:779
  470.0 14.9 %collective-permute-start.64 = (bf16[512,1024]{1,0:T(8,128)(2,1)S(1)}, bf16[512,1024]{1,0:T(8,128)(2,1)S(1)}, u32[]{:S(2)}, u32[]{:S(2)}) collective-permute-start(bf16[512,1024]{1,0:T(8,128)(2,1)S(1)} %pad_maximum_fusion.4), channel_id=1, source_target_pairs={{0,2},{2,0},{4,6},{6,4},{8,10},{10,8},{12,14},{14,12},{16,20},{18,... | collective-permute-start | bytes 3145736 | tf_op jit(solution)/shard_map/ppermute | solution.py:779
  471.2 35.3 %collective-permute-start.81 = (bf16[1024,1024]{1,0:T(8,128)(2,1)S(1)}, bf16[1024,1024]{1,0:T(8,128)(2,1)}, u32[]{:S(2)}, u32[]{:S(2)}) collective-permute-start(bf16[1024,1024]{1,0:T(8,128)(2,1)S(1)} %pad_maximum_fusion.3.own1), channel_id=1, source_target_pairs={{0,16},{1,17},{2,18},{3,19},{4,20},{5,21},{6,22},{7,23},{8,24},{9,... | collective-permute-start | bytes 6291464 | tf_op jit(solution)/shard_map/ppermute | solution.py:779
  475.9 35.8 %collective-permute-start.70 = (bf16[1024,1024]{1,0:T(8,128)(2,1)}, bf16[1024,1024]{1,0:T(8,128)(2,1)}, u32[]{:S(2)}, u32[]{:S(2)}) collective-permute-start(bf16[1024,1024]{1,0:T(8,128)(2,1)} %pad_maximum_fusion.1.own1), channel_id=1, source_target_pairs={{0,16},{1,17},{2,18},{3,19},{4,20},{5,21},{6,22},{7,23},{8,24},{9,... | collective-permute-start | bytes 6291464 | tf_op jit(solution)/shard_map/ppermute | solution.py:779
  480.7 25.8 %collective-permute-start.77 = (bf16[1024,1024]{1,0:T(8,128)(2,1)}, bf16[1024,1024]{1,0:T(8,128)(2,1)}, u32[]{:S(2)}, u32[]{:S(2)}) collective-permute-start(bf16[1024,1024]{1,0:T(8,128)(2,1)} %pad_maximum_fusion.2.own0), channel_id=1, source_target_pairs={{16,0},{17,1},{18,2},{19,3},{20,4},{21,5},{22,6},{23,7},{24,8},{25... | collective-permute-start | bytes 6291464 | tf_op jit(solution)/shard_map/ppermute | solution.py:779
  487.1 24.7 %collective-permute-start.65 = (bf16[1024,1024]{1,0:T(8,128)(2,1)}, bf16[1024,1024]{1,0:T(8,128)(2,1)}, u32[]{:S(2)}, u32[]{:S(2)}) collective-permute-start(bf16[1024,1024]{1,0:T(8,128)(2,1)} %pad_maximum_fusion.own0), channel_id=1, source_target_pairs={{16,0},{17,1},{18,2},{19,3},{20,4},{21,5},{22,6},{23,7},{24,8},{25... | collective-permute-start | bytes 6291464 | tf_op jit(solution)/shard_map/ppermute | solution.py:779
  (83 other events, 836.3 us)

commit v3 on v2

--- a/solution.py
+++ b/solution.py
@@ -882,10 +882,15 @@
     feed_cut = lax.ppermute(cuts[1], sections, [(0, 1), (1, 0)])
     span = width // size
     came = swap_cores(jnp.concatenate([attention_cut[span:], feed_cut[span:]], axis=0))
-    first_piece = jnp.where(
-        sec == 0, jnp.concatenate([attention_cut[:span], feed_cut[:span]], axis=0), came
-    )
-    second_piece = jnp.where(sec == 1, attention_cut[:span], came[:span])
+    attention_mine = attention_cut[:span]
+    piece = jnp.concatenate(
+        [
+            jnp.where(sec == 0, attention_mine, came[:span]),
+            jnp.where(sec == 0, feed_cut[:span], came[span:]),
+            jnp.where(sec == 0, came[:span], attention_mine),
+        ],
+        axis=0,
+    )
 
     def slots_of(arrays, rows, last):
         half = span // 2
@@ -895,38 +900,36 @@
         return Pieces(sec, slot_places, *(slots_of(arrays, rows, last) for arrays in gathered))
 
     half = span // 2
-    first_gather = Flow(spread_steps(first_piece, both_cores))
-    second_gather = Flow(spread_steps(second_piece, both_cores))
-    operand = first_gather.advance()
+    gather = Flow(spread_steps(piece, both_cores))
+    operand = gather.advance()
     (u0, start), _ = lax.optimization_barrier(((u0, start), operand))
     a0 = first_call(here, own_weights[0], u0, start, gains[0][0], gains[0][2])
     whole_up = lax.ppermute(mine[2], sections, [(2, 3), (3, 2)])
     whole_down = lax.ppermute(mine[3], sections, [(2, 3), (3, 2)])
-    together([first_gather], a0["h"])
-    together([first_gather])
-    together([first_gather])
-    operands, (n1_zero, whole_up) = together([first_gather, second_gather], a0["n1"], whole_up)
+    together([gather], a0["h"])
+    together([gather])
+    together([gather])
+    operands, (n1_zero, whole_up) = together([gather], a0["n1"], whole_up)
     a0 = dict(a0, n1=n1_zero)
-    gathered = finished(first_gather)
+    gathered = finished(gather)
     far_zero = pieces_of(gathered, 0, lambda x: ((x[0], 0), (x[0], half)))
-    far_two_zero = pieces_of(gathered, span, lambda x: ((x[1], 0), (x[1], half)))
+    far_two_zero = pieces_of(gathered, span, lambda x: ((x[0], span), (x[1], 0)))
+    far_one = pieces_of(gathered, 2 * span, lambda x: ((x[1], half), (x[1], span)))
     b0 = kernel_after(
         lambda *x: second_call(here, far_zero, *x), [], None,
         a0["n1"], start, a0["h"], gains[0][1], gains[0][3],
     )
-    late, _ = lax.optimization_barrier((lax.dynamic_index_in_dim(cotangent, sec, 0, False), b0["h"]))
-    gy1 = across(late)
-    operands, (n2_zero,) = together([second_gather], b0["n2"])
+    n2_zero, whole_down = lax.optimization_barrier((b0["n2"], whole_down))
     b0 = dict(b0, n2=n2_zero)
     c0 = kernel_after(
         lambda *x: feed_call(here, own_weights[0], far_two_zero, *x), [], None, b0["n2"], b0["h"]
     )
-    operands, (u1, whole_down) = together([second_gather], c0["y"], whole_down)
+    late, _ = lax.optimization_barrier((lax.dynamic_index_in_dim(cotangent, sec, 0, False), c0["y"]))
+    gy1 = across(late)
     a1 = kernel_after(
-        lambda *x: first_call(here, own_weights[1], *x), [], None, u1, start, gains[1][0], gains[1][2]
-    )
-    together([second_gather], a1["h"])
-    far_one = pieces_of(finished(second_gather), 0, lambda x: ((x[0], 0), (x[1], 0)))
+        lambda *x: first_call(here, own_weights[1], *x), [], None, c0["y"], start, gains[1][0], gains[1][2]
+    )
+    (whole_up, whole_down), _ = lax.optimization_barrier(((whole_up, whole_down), c0["y"]))
     b1 = kernel_after(
         lambda *x: second_call(here, far_one, *x), [], None,
         a1["n1"], start, a1["h"], gains[1][1], gains[1][3],
@@ -969,7 +972,6 @@
     sums.append(Flow(sum_steps(0, e0["give"], e0["keep"])))
     f0 = heads_back(0, sums, e0["gh"], a0, e0)
     sums.append(Flow(sum_steps(0, f0["give"], f0["keep"])))
-    sums[3].advance()
     g0 = input_back(0, far_zero, sums, f0["d"], a0, b0, e0, f0, u0)
     norm_grads = [
         jnp.concatenate([g["grads"][:1], e["grads"][:1], g["grads"][1:], e["grads"][1:]])

time: 525 us -> 495 us (0.943)
  waiting for transfers between devices: 176 us -> 163 us
  local copies, waits for them, and re-layouts: 22.6 us -> 15.7 us
    ppermute x51 -> x42, waiting for transfers between devices: 103 us -> 87.6 us  [move(): return lambda value: lax.ppermute(value, axis, route)]
    ppermute x8 -> x4, starting transfers between devices: 13.2 us -> 1.81 us  [around(): lax.ppermute(pair[1], 'dp', ring_down)]
    ppermute x2, waiting for transfers between devices: 0.01 us -> 9.32 us  [across(): other = lax.ppermute(shard, 'tensor', swap)]
    ppermute x6, starting transfers between devices: 4.02 us -> 11.3 us  [swap_cores(): return lax.ppermute(value, 'section', swap)]
    ppermute x8 -> x4, waiting for transfers between devices: 11.1 us -> 3.99 us  [around(): lax.ppermute(pair[1], 'dp', ring_down)]
    ppermute x8 -> x4, starting transfers between devices: 12.8 us -> 6.72 us  [around(): lax.ppermute(pair[0], 'dp', ring_up)]
    ppermute x1, waiting for transfers between devices: 11 us -> 5.6 us  [per_device(): feed_cut = lax.ppermute(cuts[1], sections, [(0, 1), (1, 0)])]
    ppermute x8 -> x4, waiting for transfers between devices: 39.1 us -> 43.3 us  [around(): lax.ppermute(pair[0], 'dp', ring_up)]
  transfers between devices with their start and end apart: 86 -> 69, of which waited for: 31 -> 26; matrix products, arithmetic and copies ran while one was open for 12% -> 12% of each run, Pallas kernels for 32% -> 32%
where the time goes in v3:
time: 495 us; the launch traced here: 488 us
  Pallas kernels  183 us (37%)
  waiting for transfers between devices  163 us (33%)
  starting transfers between devices  78.6 us (16%)
  other arithmetic  45.9 us (9%)
  local copies, waits for them, and re-layouts  15.7 us (3%)
    pallas_call x12, Pallas kernels, room_call(): pl.pallas_call(whole, in_specs=[pl.BlockSpec(memory_space=pltpu.SMEM)] *...  170 us
    ppermute x42, waiting for transfers between devices, move(): return lambda value: lax.ppermute(value, axis, route)  87.6 us
    ppermute x4, waiting for transfers between devices, around(): lax.ppermute(pair[0], 'dp', ring_up)  43.3 us
    ppermute x42, starting transfers between devices, move(): return lambda value: lax.ppermute(value, axis, route)  41.7 us
    ppermute x6, starting transfers between devices, swap_cores(): return lax.ppermute(value, 'section', swap)  11.3 us
    ppermute x1, waiting for transfers between devices, swap_tensor(): return lax.ppermute(value, 'tensor', swap)  10.7 us
    pallas_call x2, Pallas kernels, final_call(): pl.pallas_call(kernel, in_specs=[pl.BlockSpec(memory_space=pltpu.SMEM)] +...  10.4 us
  transfers between devices with their start and end apart: 69, of which 26 were waited for; matrix products, arithmetic and copies ran while one was open for 12% of the time, Pallas kernels for 32%

profile of v3, /device:TPU:0, one launch (start us, length us, event | category | flops | bytes accessed | tf_op | source)
XLA Modules:
  0.0 488.3 jit_solution(2332824883203381968)
XLA Ops:
  1.8 2.9 cut.1
  4.7 2.6 collective-permute-start
  9.4 10.7 %collective-permute-done = bf16[256,1024]{1,0:T(8,128)(2,1)S(1)} collective-permute-done((bf16[256,1024]{1,0:T(8,128)(2,1)}, bf16[256,1024]{1,0:T(8,128)(2,1)S(1)}, u32[]{:S(2)}, u32[]{:S(2)}) %collective-permute-start) | collective-permute-done | bytes 524320 | tf_op jit(solution)/shard_map/ppermute | solution.py:776
  20.1 5.6 %collective-permute-done.1 = bf16[256,1024]{1,0:T(8,128)(2,1)S(1)} collective-permute-done((bf16[256,1024]{1,0:T(8,128)(2,1)}, bf16[256,1024]{1,0:T(8,128)(2,1)S(1)}, u32[]{:S(2)}, u32[]{:S(2)}) %collective-permute-start.1) | collective-permute-done | bytes 524320 | tf_op jit(solution)/shard_map/ppermute | solution.py:882
  32.0 9.3 %collective-permute-done.6 = bf16[256,1024]{1,0:T(8,128)(2,1)} collective-permute-done((bf16[256,1024]{1,0:T(8,128)(2,1)}, bf16[256,1024]{1,0:T(8,128)(2,1)}, u32[]{:S(2)}, u32[]{:S(2)}) %collective-permute-start.6) | collective-permute-done | bytes 524320 | tf_op jit(solution)/shard_map/ppermute | solution.py:762
  42.6 3.1 maximum_select_fusion.refs_2_.refs_7_
  48.5 10.4 %first.2 = (bf16[512,1024]{1,0:T(8,128)(2,1)}, bf16[512,1536]{1,0:T(8,128)(2,1)}, bf16[512,512]{1,0:T(8,128)(2,1)}, f32[512,1024]{1,0:T(8,128)}) custom-call(s32[1]{0:T(128)} %bitcast.refs_0_.scalar_ref, s32[2]{0:T(128)} %pad_add_fusion.refs_1_.refs_2_, bf16[512,1024]{1,0:T(8,128)(2,1)} %maximum_select_fusion.refs_2_.refs_7_, s32[512,1]{1,0:T(8,128)} %copy.29.refs_3_, ...), custom_call_target="tpu_custom_call" | custom-call | flops 2415919104 | bytes 10496000 | tf_op jit(solution)/shard_map/first/pallas_call | solution.py:254
  62.0 17.1 %collective-permute-done.10.refs_9_.refs_11_.refs_12_.refs_16_ = bf16[384,1024]{1,0:T(8,128)(2,1)S(1)} collective-permute-done((bf16[384,1024]{1,0:T(8,128)(2,1)}, bf16[384,1024]{1,0:T(8,128)(2,1)S(1)}, u32[]{:S(2)}, u32[]{:S(2)}) %collective-permute-start.10) | collective-permute-done | bytes 786464 | tf_op jit(solution)/shard_map/ppermute | solution.py:809
  79.1 2.3 collective-permute-done.11.refs_12_.refs_14_.refs_15_.refs_19_
  84.9 17.0 %collective-permute-done.14.refs_10_.refs_12_.refs_13_.refs_17_ = bf16[384,1024]{1,0:T(8,128)(2,1)S(1)} collective-permute-done((bf16[384,1024]{1,0:T(8,128)(2,1)S(1)}, bf16[384,1024]{1,0:T(8,128)(2,1)S(1)}, u32[]{:S(2)}, u32[]{:S(2)}) %collective-permute-start.14) | collective-permute-done | bytes 786464 | tf_op jit(solution)/shard_map/ppermute | solution.py:809
  107.4 9.1 %collective-permute-done.18.refs_14_.refs_16_.refs_21_.refs_17_ = bf16[192,1024]{1,0:T(8,128)(2,1)S(1)} collective-permute-done((bf16[192,1024]{1,0:T(8,128)(2,1)S(1)}, bf16[192,1024]{1,0:T(8,128)(2,1)S(1)}, u32[]{:S(2)}, u32[]{:S(2)}) %collective-permute-start.18) | collective-permute-done | bytes 393248 | tf_op jit(solution)/shard_map/ppermute | solution.py:809
  123.4 11.7 %second.2 = (bf16[512,1536]{1,0:T(8,128)(2,1)}, f32[512,1024]{1,0:T(8,128)}, bf16[512,1024]{1,0:T(8,128)(2,1)}) custom-call(s32[1]{0:T(128)} %bitcast.refs_0_.scalar_ref, s32[9]{0:T(128)} %pad_add_fusion.1.refs_1_.refs_2_, bf16[512,1024]{1,0:T(8,128)(2,1)} %get-tuple-element.265.refs_2_.refs_6_, s32[512,1]{1,0:T(8,128)} %copy.30.refs_3_, ...), custom_call_target="tpu_custom_call" | custom-call | flops 2415919104 | bytes 12068864 | tf_op jit(solution)/shard_map/second/pallas_call | solution.py:254
  135.2 12.6 %feed.2 = (bf16[512,1024]{1,0:T(8,128)(2,1)}, bf16[512,1024]{1,0:T(8,128)(2,1)}, bf16[512,1024]{1,0:T(8,128)(2,1)}, bf16[512,1024]{1,0:T(8,128)(2,1)}) custom-call(s32[1]{0:T(128)} %bitcast.refs_0_.scalar_ref, s32[2]{0:T(128)} %pad_add_fusion.refs_1_.refs_2_, s32[9]{0:T(128)} %pad_add_fusion.1.refs_1_.refs_2_, ...), custom_call_target="tpu_custom_call" | custom-call | flops 4294967296 | bytes 15728640 | tf_op jit(solution)/shard_map/feed/pallas_call | solution.py:254
  154.6 9.9 %first.3 = (bf16[512,1024]{1,0:T(8,128)(2,1)}, bf16[512,1536]{1,0:T(8,128)(2,1)}, bf16[512,512]{1,0:T(8,128)(2,1)}, f32[512,1024]{1,0:T(8,128)}) custom-call(s32[1]{0:T(128)} %bitcast.refs_0_.scalar_ref, s32[2]{0:T(128)} %pad_add_fusion.3.refs_1_.refs_2_, bf16[512,1024]{1,0:T(8,128)(2,1)} %get-tuple-element.238.refs_2_.refs_7_, s32[512,1]{1,0:T(8,128)} %copy.31.refs_3_, ...), custom_call_target="tpu_custom_call" | custom-call | flops 2415919104 | bytes 10496000 | tf_op jit(solution)/shard_map/first/pallas_call | solution.py:254
  165.3 11.7 %second.3 = (bf16[512,1536]{1,0:T(8,128)(2,1)}, f32[512,1024]{1,0:T(8,128)}, bf16[512,1024]{1,0:T(8,128)(2,1)}) custom-call(s32[1]{0:T(128)} %bitcast.refs_0_.scalar_ref, s32[9]{0:T(128)} %pad_add_fusion.1.refs_1_.refs_2_, bf16[512,1024]{1,0:T(8,128)(2,1)} %get-tuple-element.228.refs_2_.refs_6_, s32[512,1]{1,0:T(8,128)} %copy.32.refs_3_, ...), custom_call_target="tpu_custom_call" | custom-call | flops 2415919104 | bytes 12068864 | tf_op jit(solution)/shard_map/second/pallas_call | solution.py:254
  179.8 10.9 %feed.3 = (bf16[512,1024]{1,0:T(8,128)(2,1)}, bf16[512,1024]{1,0:T(8,128)(2,1)}, bf16[512,1024]{1,0:T(8,128)(2,1)}, bf16[512,1024]{1,0:T(8,128)(2,1)}) custom-call(s32[1]{0:T(128)} %bitcast.refs_0_.scalar_ref, s32[2]{0:T(128)} %pad_add_fusion.3.refs_1_.refs_2_, s32[2]{0:T(128)} %pad_add_fusion.3.refs_1_.refs_2_, ...), custom_call_target="tpu_custom_call" | custom-call | flops 4294967296 | bytes 15728640 | tf_op jit(solution)/shard_map/feed/pallas_call | solution.py:254
  192.0 4.6 collective-permute-start.30
  196.6 16.6 %feed_back.2 = (bf16[1024,1024]{1,0:T(8,128)(2,1)}, bf16[1024,1024]{1,0:T(8,128)(2,1)}, f32[512,1024]{1,0:T(8,128)}, bf16[512,1024]{1,0:T(8,128)(2,1)}, f32[2,1024]{1,0:T(2,128)}) custom-call(s32[1]{0:T(128)} %bitcast.refs_0_.scalar_ref, s32[2]{0:T(128)} %pad_add_fusion.3.refs_1_.refs_2_, s32[2]{0:T(128)} %pad_add_fusion.3.refs_1_.refs_2_, ...), custom_call_target="tpu_custom_call" | custom-call | flops 6442450944 | bytes 23080960 | tf_op jit(solution)/shard_map/feed_back/pallas_call | solution.py:254
  215.4 16.1 %heads_back.2 = (bf16[1024,1024]{1,0:T(8,128)(2,1)}, bf16[1024,1024]{1,0:T(8,128)(2,1)}, bf16[512,1536]{1,0:T(8,128)(2,1)}) custom-call(s32[1]{0:T(128)} %bitcast.refs_0_.scalar_ref, s32[2]{0:T(128)} %pad_add_fusion.3.refs_1_.refs_2_, bf16[512,1024]{1,0:T(8,128)(2,1)} %get-tuple-element.234.refs_2_.refs_3_, bf16[512,1536]{1,0:T(8,128)(2,1)} %get-tuple-element.225.refs_3_, ...), custom_call_target="tpu_custom_call" | custom-call | flops 4563402752 | bytes 11012096 | tf_op jit(solution)/shard_map/heads_back/pallas_call | solution.py:254
  235.0 18.7 %input_back.2 = (bf16[512,1024]{1,0:T(8,128)(2,1)}, f32[2,1024]{1,0:T(2,128)}) custom-call(s32[1]{0:T(128)} %bitcast.refs_0_.scalar_ref, s32[9]{0:T(128)} %pad_add_fusion.1.refs_1_.refs_2_, s32[2]{0:T(128)} %pad_add_fusion.3.refs_1_.refs_2_, bf16[512,1024]{1,0:T(8,128)(2,1)} %get-tuple-element.234.refs_2_.refs_3_, ...), custom_call_target="tpu_custom_call" | custom-call | flops 5637144576 | bytes 15742976 | tf_op jit(solution)/shard_map/input_back/pallas_call | solution.py:254
  253.7 2.8 add_convert_fusion.5
  262.0 16.9 %feed_back.3 = (bf16[1024,1024]{1,0:T(8,128)(2,1)}, bf16[1024,1024]{1,0:T(8,128)(2,1)}, f32[512,1024]{1,0:T(8,128)}, bf16[512,1024]{1,0:T(8,128)(2,1)}, f32[2,1024]{1,0:T(2,128)}) custom-call(s32[1]{0:T(128)} %bitcast.refs_0_.scalar_ref, s32[2]{0:T(128)} %pad_add_fusion.refs_1_.refs_2_, s32[9]{0:T(128)} %pad_add_fusion.1.refs_1_.refs_2_, ...), custom_call_target="tpu_custom_call" | custom-call | flops 6442450944 | bytes 23080960 | tf_op jit(solution)/shard_map/feed_back/pallas_call | solution.py:254
  283.8 2.5 collective-permute-start.37
  287.2 15.9 %heads_back.3 = (bf16[1024,1024]{1,0:T(8,128)(2,1)}, bf16[1024,1024]{1,0:T(8,128)(2,1)}, bf16[512,1536]{1,0:T(8,128)(2,1)}) custom-call(s32[1]{0:T(128)} %bitcast.refs_0_.scalar_ref, s32[2]{0:T(128)} %pad_add_fusion.refs_1_.refs_2_, bf16[512,1024]{1,0:T(8,128)(2,1)} %get-tuple-element.273.refs_2_.refs_3_, bf16[512,1536]{1,0:T(8,128)(2,1)} %get-tuple-element.262.refs_3_, ...), custom_call_target="tpu_custom_call" | custom-call | flops 4563402752 | bytes 11012096 | tf_op jit(solution)/shard_map/heads_back/pallas_call | solution.py:254
  304.1 2.5 collective-permute-start.49
  306.7 3.0 add_convert_fusion.3
  311.6 18.4 %input_back.3 = (bf16[512,1024]{1,0:T(8,128)(2,1)}, f32[2,1024]{1,0:T(2,128)}) custom-call(s32[1]{0:T(128)} %bitcast.refs_0_.scalar_ref, s32[9]{0:T(128)} %pad_add_fusion.1.refs_1_.refs_2_, s32[2]{0:T(128)} %pad_add_fusion.refs_1_.refs_2_, bf16[512,1024]{1,0:T(8,128)(2,1)} %get-tuple-element.273.refs_2_.refs_3_, ...), custom_call_target="tpu_custom_call" | custom-call | flops 5637144576 | bytes 15742976 | tf_op jit(solution)/shard_map/input_back/pallas_call | solution.py:254
  339.9 4.6 collective-permute-done.50
  345.9 10.0 %collective-permute-done.55 = bf16[256,1024]{1,0:T(8,128)(2,1)S(1)} collective-permute-done((bf16[256,1024]{1,0:T(8,128)(2,1)S(1)}, bf16[256,1024]{1,0:T(8,128)(2,1)S(1)}, u32[]{:S(2)}, u32[]{:S(2)}) %collective-permute-start.55) | collective-permute-done | bytes 524320 | tf_op jit(solution)/shard_map/ppermute | solution.py:779
  356.2 3.4 collective-permute-done.42
  361.9 9.7 %collective-permute-done.62 = bf16[256,1024]{1,0:T(8,128)(2,1)S(1)} collective-permute-done((bf16[256,1024]{1,0:T(8,128)(2,1)S(1)}, bf16[256,1024]{1,0:T(8,128)(2,1)S(1)}, u32[]{:S(2)}, u32[]{:S(2)}) %collective-permute-start.62) | collective-permute-done | bytes 524320 | tf_op jit(solution)/shard_map/ppermute | solution.py:779
  371.5 7.3 %collective-permute-done.51 = bf16[256,1024]{1,0:T(8,128)(2,1)S(1)} collective-permute-done((bf16[256,1024]{1,0:T(8,128)(2,1)S(1)}, bf16[256,1024]{1,0:T(8,128)(2,1)S(1)}, u32[]{:S(2)}, u32[]{:S(2)}) %collective-permute-start.51) | collective-permute-done | bytes 524320 | tf_op jit(solution)/shard_map/ppermute | solution.py:779
  379.8 6.1 %collective-permute-done.43 = bf16[256,1024]{1,0:T(8,128)(2,1)S(1)} collective-permute-done((bf16[256,1024]{1,0:T(8,128)(2,1)S(1)}, bf16[256,1024]{1,0:T(8,128)(2,1)S(1)}, u32[]{:S(2)}, u32[]{:S(2)}) %collective-permute-start.43) | collective-permute-done | bytes 524320 | tf_op jit(solution)/shard_map/ppermute | solution.py:779
  387.3 9.2 %collective-permute-done.57 = bf16[128,1024]{1,0:T(8,128)(2,1)S(1)} collective-permute-done((bf16[128,1024]{1,0:T(8,128)(2,1)S(1)}, bf16[128,1024]{1,0:T(8,128)(2,1)S(1)}, u32[]{:S(2)}, u32[]{:S(2)}) %collective-permute-start.57) | collective-permute-done | bytes 262176 | tf_op jit(solution)/shard_map/ppermute | solution.py:779
  396.6 3.0 collective-permute-done.44
  400.5 3.9 collective-permute-start.58
  405.7 6.5 %collective-permute-done.45 = bf16[128,1024]{1,0:T(8,128)(2,1)} collective-permute-done((bf16[128,1024]{1,0:T(8,128)(2,1)S(1)}, bf16[128,1024]{1,0:T(8,128)(2,1)}, u32[]{:S(2)}, u32[]{:S(2)}) %collective-permute-start.45) | collective-permute-done | bytes 262176 | tf_op jit(solution)/shard_map/ppermute | solution.py:779
  413.9 7.1 %collective-permute-done.58 = bf16[256,1024]{1,0:T(8,128)(2,1)S(1)} collective-permute-done((bf16[256,1024]{1,0:T(8,128)(2,1)}, bf16[256,1024]{1,0:T(8,128)(2,1)S(1)}, u32[]{:S(2)}, u32[]{:S(2)}) %collective-permute-start.58) | collective-permute-done | bytes 524320 | tf_op jit(solution)/shard_map/ppermute | solution.py:779
  421.4 2.5 collective-permute-start.59
  425.6 6.6 %collective-permute-done.46 = bf16[256,1024]{1,0:T(8,128)(2,1)S(1)} collective-permute-done((bf16[256,1024]{1,0:T(8,128)(2,1)S(1)}, bf16[256,1024]{1,0:T(8,128)(2,1)S(1)}, u32[]{:S(2)}, u32[]{:S(2)}) %collective-permute-start.46) | collective-permute-done | bytes 524320 | tf_op jit(solution)/shard_map/ppermute | solution.py:779
  432.6 2.5 collective-permute-start.47
  435.3 2.6 collective-permute-start.64
  439.9 2.6 collective-permute-start.53
  451.5 10.5 %collective-permute-start.65 = (f32[8,1024]{1,0:T(8,128)S(1)}, f32[8,1024]{1,0:T(8,128)S(1)}, u32[]{:S(2)}, u32[]{:S(2)}) collective-permute-start(f32[8,1024]{1,0:T(8,128)S(1)} %concatenate.113), channel_id=1, source_target_pairs={{0,16},{16,0},{1,17},{17,1},{2,18},{18,2},{3,19},{19,3},{4,20},{20... | collective-permute-start | bytes 98312 | tf_op jit(solution)/shard_map/ppermute | solution.py:773
  468.0 3.9 collective-permute-done.67
  473.0 3.7 collective-permute-done.68
  477.4 5.2 %final_mlp.1 = (f32[1024,1024]{1,0:T(8,128)}, f32[1024,1024]{1,0:T(8,128)}) custom-call(s32[1]{0:T(128)} %bitcast.refs_0_.scalar_ref, bf16[1024,1024]{1,0:T(8,128)(2,1)} %pad_maximum_fusion.2.own0, bf16[1024,1024]{1,0:T(8,128)(2,1)} %collective-permute-done.60.far0, bf16[1024,1024]{1,0:T(8,128)(2,1)} %copy-done.14, ...), custom_call_target="tpu_custom_call" | custom-call | bytes 12582912 | tf_op jit(solution)/shard_map/final_mlp/pallas_call | solution.py:687
  482.6 5.2 %final_attention.1 = (f32[512,1024]{1,0:T(8,128)}, f32[3,1024,512]{2,1,0:T(8,128)}) custom-call(s32[1]{0:T(128)} %bitcast.refs_0_.scalar_ref, bf16[1024,1024]{1,0:T(8,128)(2,1)} %pad_maximum_fusion.own0, bf16[1024,1024]{1,0:T(8,128)(2,1)} %collective-permute-done.48.far0, bf16[1024,1024]{1,0:T(8,128)(2,1)} %pad_maximum_fusion.1.own1, ...), custom_call_target="tpu_custom_call" | custom-call | bytes 12582912 | tf_op jit(solution)/shard_map/final_attention/pallas_call | solution.py:687
  (264 shorter events, 104.9 us)
Async XLA Ops:
  0.6 47.8 %collective-permute-start.8 = (bf16[3,1024,512]{2,1,0:T(8,128)(2,1)}, bf16[3,1024,512]{2,1,0:T(8,128)(2,1)}, u32[]{:S(2)}, u32[]{:S(2)}) collective-permute-start(bf16[3,1024,512]{2,1,0:T(8,128)(2,1)} %bitcast.33), channel_id=1, source_target_pairs={{0,16},{16,0},{1,17},{17,1},{2,18},{18,2},{3,19},{19,3},{4,20},{20... | collective-permute-start | bytes 9437192 | tf_op jit(solution)/shard_map/ppermute | solution.py:770
  7.3 18.4 %collective-permute-start.1 = (bf16[256,1024]{1,0:T(8,128)(2,1)}, bf16[256,1024]{1,0:T(8,128)(2,1)S(1)}, u32[]{:S(2)}, u32[]{:S(2)}) collective-permute-start(bf16[256,1024]{1,0:T(8,128)(2,1)} %get-tuple-element.153), channel_id=1, source_target_pairs={{0,1},{1,0},{2,3},{3,2},{4,5},{5,4},{6,7},{7,6},{8,9},{9,8},{10,11... | collective-permute-start | bytes 1572872 | tf_op jit(solution)/shard_map/ppermute | solution.py:882
  9.3 37.2 %collective-permute-start.9 = (bf16[512,1024]{1,0:T(8,128)(2,1)}, bf16[512,1024]{1,0:T(8,128)(2,1)}, u32[]{:S(2)}, u32[]{:S(2)}) collective-permute-start(bf16[512,1024]{1,0:T(8,128)(2,1)} %bitcast.4.out.refs_7_), channel_id=1, source_target_pairs={{0,16},{16,0},{1,17},{17,1},{2,18},{18,2},{3,19},{19,3},{4,20},{20... | collective-permute-start | bytes 3145736 | tf_op jit(solution)/shard_map/ppermute | solution.py:770
  29.9 29.0 %collective-permute-start.3 = (bf16[384,1024]{1,0:T(8,128)(2,1)S(1)}, bf16[384,1024]{1,0:T(8,128)(2,1)}, u32[]{:S(2)}, u32[]{:S(2)}) collective-permute-start(bf16[384,1024]{1,0:T(8,128)(2,1)S(1)} %pad_maximum_fusion.8.refs_7_.refs_9_.refs_10_.refs_14_), channel_id=1, source_target_pairs={{0,4},{4,8},{8,12},{12,14},{14,10},{10,6},{6,2},{2,0},{1,5},{5,9},... | collective-permute-start | bytes 2359304 | tf_op jit(solution)/shard_map/ppermute | solution.py:809
  31.6 27.4 %collective-permute-start.4 = (bf16[384,1024]{1,0:T(8,128)(2,1)S(1)}, bf16[384,1024]{1,0:T(8,128)(2,1)}, u32[]{:S(2)}, u32[]{:S(2)}) collective-permute-start(bf16[384,1024]{1,0:T(8,128)(2,1)S(1)} %pad_maximum_fusion.8.refs_7_.refs_9_.refs_10_.refs_14_), channel_id=1, source_target_pairs={{4,0},{8,4},{12,8},{14,12},{10,14},{6,10},{2,6},{0,2},{5,1},{9,5},... | collective-permute-start | bytes 2359304 | tf_op jit(solution)/shard_map/ppermute | solution.py:809
  46.5 60.2 %collective-permute-start.22 = (bf16[1024,1024]{1,0:T(8,128)(2,1)S(1)}, bf16[1024,1024]{1,0:T(8,128)(2,1)}, u32[]{:S(2)}, u32[]{:S(2)}) collective-permute-start(bf16[1024,1024]{1,0:T(8,128)(2,1)S(1)} %bitcast.44), channel_id=1, source_target_pairs={{16,17},{17,16},{18,19},{19,18},{20,21},{21,20},{22,23},{23,22},{2... | collective-permute-start | bytes 6291464 | tf_op jit(solution)/shard_map/ppermute | solution.py:907
  58.9 20.2 %collective-permute-start.10 = (bf16[384,1024]{1,0:T(8,128)(2,1)}, bf16[384,1024]{1,0:T(8,128)(2,1)S(1)}, u32[]{:S(2)}, u32[]{:S(2)}) collective-permute-start(bf16[384,1024]{1,0:T(8,128)(2,1)} %collective-permute-done.3.refs_8_.refs_10_.refs_11_.refs_15_), channel_id=1, source_target_pairs={{0,4},{4,8},{8,12},{12,14},{14,10},{10,6},{6,2},{2,0},{1,5},{5,9},... | collective-permute-start | bytes 2359304 | tf_op jit(solution)/shard_map/ppermute | solution.py:809
  60.8 20.6 %collective-permute-start.11 = (bf16[384,1024]{1,0:T(8,128)(2,1)}, bf16[384,1024]{1,0:T(8,128)(2,1)S(1)}, u32[]{:S(2)}, u32[]{:S(2)}) collective-permute-start(bf16[384,1024]{1,0:T(8,128)(2,1)} %collective-permute-done.4.refs_11_.refs_13_.refs_14_.refs_18_), channel_id=1, source_target_pairs={{4,0},{8,4},{12,8},{14,12},{10,14},{6,10},{2,6},{0,2},{5,1},{9,5},... | collective-permute-start | bytes 2359304 | tf_op jit(solution)/shard_map/ppermute | solution.py:809
  61.0 20.4 %collective-permute-start.12 = (bf16[384,1024]{1,0:T(8,128)(2,1)}, bf16[384,1024]{1,0:T(8,128)(2,1)S(1)}, u32[]{:S(2)}, u32[]{:S(2)}) collective-permute-start(bf16[384,1024]{1,0:T(8,128)(2,1)} %collective-permute-done.3.refs_8_.refs_10_.refs_11_.refs_15_), channel_id=1, source_target_pairs={{0,16},{16,0},{1,17},{17,1},{2,18},{18,2},{3,19},{19,3},{4,20},{20... | collective-permute-start | bytes 2359304 | tf_op jit(solution)/shard_map/ppermute | solution.py:779
  62.0 20.3 %collective-permute-start.13 = (bf16[384,1024]{1,0:T(8,128)(2,1)}, bf16[384,1024]{1,0:T(8,128)(2,1)S(1)}, u32[]{:S(2)}, u32[]{:S(2)}) collective-permute-start(bf16[384,1024]{1,0:T(8,128)(2,1)} %collective-permute-done.4.refs_11_.refs_13_.refs_14_.refs_18_), channel_id=1, source_target_pairs={{0,16},{16,0},{1,17},{17,1},{2,18},{18,2},{3,19},{19,3},{4,20},{20... | collective-permute-start | bytes 2359304 | tf_op jit(solution)/shard_map/ppermute | solution.py:779
  82.3 19.6 %collective-permute-start.14 = (bf16[384,1024]{1,0:T(8,128)(2,1)S(1)}, bf16[384,1024]{1,0:T(8,128)(2,1)S(1)}, u32[]{:S(2)}, u32[]{:S(2)}) collective-permute-start(bf16[384,1024]{1,0:T(8,128)(2,1)S(1)} %collective-permute-done.10.refs_9_.refs_11_.refs_12_.refs_16_), channel_id=1, source_target_pairs={{0,4},{4,8},{8,12},{12,14},{14,10},{10,6},{6,2},{2,0},{1,5},{5,9},... | collective-permute-start | bytes 2359304 | tf_op jit(solution)/shard_map/ppermute | solution.py:809
  83.9 20.1 %collective-permute-start.15 = (bf16[384,1024]{1,0:T(8,128)(2,1)S(1)}, bf16[384,1024]{1,0:T(8,128)(2,1)S(1)}, u32[]{:S(2)}, u32[]{:S(2)}) collective-permute-start(bf16[384,1024]{1,0:T(8,128)(2,1)S(1)} %collective-permute-done.11.refs_12_.refs_14_.refs_15_.refs_19_), channel_id=1, source_target_pairs={{4,0},{8,4},{12,8},{14,12},{10,14},{6,10},{2,6},{0,2},{5,1},{9,5},... | collective-permute-start | bytes 2359304 | tf_op jit(solution)/shard_map/ppermute | solution.py:809
  84.4 19.6 %collective-permute-start.16 = (bf16[384,1024]{1,0:T(8,128)(2,1)S(1)}, bf16[384,1024]{1,0:T(8,128)(2,1)S(1)}, u32[]{:S(2)}, u32[]{:S(2)}) collective-permute-start(bf16[384,1024]{1,0:T(8,128)(2,1)S(1)} %collective-permute-done.10.refs_9_.refs_11_.refs_12_.refs_16_), channel_id=1, source_target_pairs={{0,16},{16,0},{1,17},{17,1},{2,18},{18,2},{3,19},{19,3},{4,20},{20... | collective-permute-start | bytes 2359304 | tf_op jit(solution)/shard_map/ppermute | solution.py:779
  84.4 20.6 %collective-permute-start.17 = (bf16[384,1024]{1,0:T(8,128)(2,1)S(1)}, bf16[384,1024]{1,0:T(8,128)(2,1)}, u32[]{:S(2)}, u32[]{:S(2)}) collective-permute-start(bf16[384,1024]{1,0:T(8,128)(2,1)S(1)} %collective-permute-done.11.refs_12_.refs_14_.refs_15_.refs_19_), channel_id=1, source_target_pairs={{0,16},{16,0},{1,17},{17,1},{2,18},{18,2},{3,19},{19,3},{4,20},{20... | collective-permute-start | bytes 2359304 | tf_op jit(solution)/shard_map/ppermute | solution.py:779
  101.9 33.2 %collective-permute-start.24 = (bf16[1024,1024]{1,0:T(8,128)(2,1)}, bf16[1024,1024]{1,0:T(8,128)(2,1)}, u32[]{:S(2)}, u32[]{:S(2)}) collective-permute-start(bf16[1024,1024]{1,0:T(8,128)(2,1)} %bitcast.47), channel_id=1, source_target_pairs={{16,17},{17,16},{18,19},{19,18},{20,21},{21,20},{22,23},{23,22},{2... | collective-permute-start | bytes 6291464 | tf_op jit(solution)/shard_map/ppermute | solution.py:908
  104.0 31.2 %collective-permute-start.25 = (bf16[1024,1024]{1,0:T(8,128)(2,1)S(1)}, bf16[1024,1024]{1,0:T(8,128)(2,1)}, u32[]{:S(2)}, u32[]{:S(2)}) collective-permute-start(bf16[1024,1024]{1,0:T(8,128)(2,1)S(1)} %bitcast.45), channel_id=1, source_target_pairs={{0,16},{16,0},{1,17},{17,1},{2,18},{18,2},{3,19},{19,3},{4,20},{20... | collective-permute-start | bytes 6291464 | tf_op jit(solution)/shard_map/ppermute | solution.py:770
  104.0 31.1 %collective-permute-start.26 = (bf16[1024,1024]{1,0:T(8,128)(2,1)}, bf16[1024,1024]{1,0:T(8,128)(2,1)}, u32[]{:S(2)}, u32[]{:S(2)}) collective-permute-start(bf16[1024,1024]{1,0:T(8,128)(2,1)} %bitcast.48), channel_id=1, source_target_pairs={{0,16},{16,0},{1,17},{17,1},{2,18},{18,2},{3,19},{19,3},{4,20},{20... | collective-permute-start | bytes 6291464 | tf_op jit(solution)/shard_map/ppermute | solution.py:770
  147.8 30.7 %collective-permute-start.28 = (bf16[1024,1024]{1,0:T(8,128)(2,1)}, bf16[1024,1024]{1,0:T(8,128)(2,1)S(1)}, u32[]{:S(2)}, u32[]{:S(2)}) collective-permute-start(bf16[1024,1024]{1,0:T(8,128)(2,1)} %collective-permute-done.22.refs_9_.refs_15_), channel_id=1, source_target_pairs={{16,0},{17,1},{18,2},{19,3},{20,4},{21,5},{22,6},{23,7},{24,8},{25... | collective-permute-start | bytes 6291464 | tf_op jit(solution)/shard_map/ppermute | solution.py:779
  149.1 29.4 %collective-permute-start.29 = (bf16[1024,1024]{1,0:T(8,128)(2,1)}, bf16[1024,1024]{1,0:T(8,128)(2,1)}, u32[]{:S(2)}, u32[]{:S(2)}) collective-permute-start(bf16[1024,1024]{1,0:T(8,128)(2,1)} %collective-permute-done.24.refs_10_.refs_14_), channel_id=1, source_target_pairs={{16,0},{17,1},{18,2},{19,3},{20,4},{21,5},{22,6},{23,7},{24,8},{25... | collective-permute-start | bytes 6291464 | tf_op jit(solution)/shard_map/ppermute | solution.py:779
  152.5 24.5 %collective-permute-start.31 = (bf16[256,1024]{1,0:T(8,128)(2,1)S(1)}, bf16[256,1024]{1,0:T(8,128)(2,1)S(1)}, u32[]{:S(2)}, u32[]{:S(2)}) collective-permute-start(bf16[256,1024]{1,0:T(8,128)(2,1)S(1)} %dynamic-slice_bitcast_fusion), channel_id=1, source_target_pairs={{0,1},{1,0},{2,3},{3,2},{4,5},{5,4},{6,7},{7,6},{8,9},{9,8},{10,11... | collective-permute-start | bytes 1572872 | tf_op jit(solution)/shard_map/ppermute | solution.py:762
  192.0 21.3 %collective-permute-start.30 = (bf16[256,1024]{1,0:T(8,128)(2,1)S(1)}, bf16[256,1024]{1,0:T(8,128)(2,1)S(1)}, u32[]{:S(2)}, u32[]{:S(2)}) collective-permute-start(bf16[256,1024]{1,0:T(8,128)(2,1)S(1)} %get-tuple-element.307), channel_id=1, source_target_pairs={{0,16},{16,0},{1,17},{17,1},{2,18},{18,2},{3,19},{19,3},{4,20},{20... | collective-permute-start | bytes 1572872 | tf_op jit(solution)/shard_map/ppermute | solution.py:770
  213.3 18.7 %collective-permute-start.32 = (bf16[1024,1024]{1,0:T(8,128)(2,1)}, bf16[1024,1024]{1,0:T(8,128)(2,1)}, u32[]{:S(2)}, u32[]{:S(2)}) collective-permute-start(bf16[1024,1024]{1,0:T(8,128)(2,1)} %get-tuple-element.223), channel_id=1, source_target_pairs={{0,16},{16,0},{1,17},{17,1},{2,18},{18,2},{3,19},{19,3},{4,20},{20... | collective-permute-start | bytes 6291464 | tf_op jit(solution)/shard_map/ppermute | solution.py:773
  231.4 22.3 %collective-permute-start.34 = (bf16[1024,1024]{1,0:T(8,128)(2,1)}, bf16[1024,1024]{1,0:T(8,128)(2,1)}, u32[]{:S(2)}, u32[]{:S(2)}) collective-permute-start(bf16[1024,1024]{1,0:T(8,128)(2,1)} %get-tuple-element.233), channel_id=1, source_target_pairs={{0,16},{16,0},{1,17},{17,1},{2,18},{18,2},{3,19},{19,3},{4,20},{20... | collective-permute-start | bytes 6291464 | tf_op jit(solution)/shard_map/ppermute | solution.py:773
  233.6 24.5 %collective-permute-start.33 = (bf16[512,1024]{1,0:T(8,128)(2,1)S(1)}, bf16[512,1024]{1,0:T(8,128)(2,1)}, u32[]{:S(2)}, u32[]{:S(2)}) collective-permute-start(bf16[512,1024]{1,0:T(8,128)(2,1)S(1)} %add_convert_fusion.7), channel_id=1, source_target_pairs={{0,2},{2,0},{4,6},{6,4},{8,10},{10,8},{12,14},{14,12},{16,20},{18,... | collective-permute-start | bytes 3145736 | tf_op jit(solution)/shard_map/ppermute | solution.py:779
  256.5 22.5 %collective-permute-start.36 = (bf16[512,1024]{1,0:T(8,128)(2,1)}, bf16[512,1024]{1,0:T(8,128)(2,1)S(1)}, u32[]{:S(2)}, u32[]{:S(2)}) collective-permute-start(bf16[512,1024]{1,0:T(8,128)(2,1)} %add_convert_fusion.5), channel_id=1, source_target_pairs={{0,2},{2,0},{4,6},{6,4},{8,10},{10,8},{12,14},{14,12},{16,20},{18,... | collective-permute-start | bytes 3145736 | tf_op jit(solution)/shard_map/ppermute | solution.py:779
  260.3 18.7 %collective-permute-start.35 = (bf16[256,1024]{1,0:T(8,128)(2,1)S(1)}, bf16[256,1024]{1,0:T(8,128)(2,1)}, u32[]{:S(2)}, u32[]{:S(2)}) collective-permute-start(bf16[256,1024]{1,0:T(8,128)(2,1)S(1)} %constant_dynamic-slice_fusion.9), channel_id=1, source_target_pairs={{0,4},{2,6},{4,0},{6,2},{8,12},{10,14},{12,8},{14,10},{16,18},{18,... | collective-permute-start | bytes 1572872 | tf_op jit(solution)/shard_map/ppermute | solution.py:779
  278.9 27.8 %collective-permute-start.39 = (bf16[1024,1024]{1,0:T(8,128)(2,1)}, bf16[1024,1024]{1,0:T(8,128)(2,1)}, u32[]{:S(2)}, u32[]{:S(2)}) collective-permute-start(bf16[1024,1024]{1,0:T(8,128)(2,1)} %get-tuple-element.260), channel_id=1, source_target_pairs={{0,16},{16,0},{1,17},{17,1},{2,18},{18,2},{3,19},{19,3},{4,20},{20... | collective-permute-start | bytes 6291464 | tf_op jit(solution)/shard_map/ppermute | solution.py:773
  282.1 21.8 %collective-permute-start.38 = (bf16[256,1024]{1,0:T(8,128)(2,1)}, bf16[256,1024]{1,0:T(8,128)(2,1)S(1)}, u32[]{:S(2)}, u32[]{:S(2)}) collective-permute-start(bf16[256,1024]{1,0:T(8,128)(2,1)} %constant_dynamic-slice_fusion.7), channel_id=1, source_target_pairs={{0,4},{2,6},{4,0},{6,2},{8,12},{10,14},{12,8},{14,10},{16,18},{18,... | collective-permute-start | bytes 1572872 | tf_op jit(solution)/shard_map/ppermute | solution.py:779
  283.8 19.4 %collective-permute-start.37 = (bf16[128,1024]{1,0:T(8,128)(2,1)S(1)}, bf16[128,1024]{1,0:T(8,128)(2,1)S(1)}, u32[]{:S(2)}, u32[]{:S(2)}) collective-permute-start(bf16[128,1024]{1,0:T(8,128)(2,1)S(1)} %constant_dynamic-slice_fusion.8), channel_id=1, source_target_pairs={{0,8},{2,10},{4,12},{6,14},{8,0},{10,2},{12,4},{14,6},{16,24},{18,... | collective-permute-start | bytes 786440 | tf_op jit(solution)/shard_map/ppermute | solution.py:779
  303.2 30.6 %collective-permute-start.41 = (bf16[1024,1024]{1,0:T(8,128)(2,1)}, bf16[1024,1024]{1,0:T(8,128)(2,1)}, u32[]{:S(2)}, u32[]{:S(2)}) collective-permute-start(bf16[1024,1024]{1,0:T(8,128)(2,1)} %get-tuple-element.272), channel_id=1, source_target_pairs={{0,16},{16,0},{1,17},{17,1},{2,18},{18,2},{3,19},{19,3},{4,20},{20... | collective-permute-start | bytes 6291464 | tf_op jit(solution)/shard_map/ppermute | solution.py:773
  303.3 27.9 %collective-permute-start.61 = (bf16[128,1024]{1,0:T(8,128)(2,1)S(1)}, bf16[128,1024]{1,0:T(8,128)(2,1)}, u32[]{:S(2)}, u32[]{:S(2)}) collective-permute-start(bf16[128,1024]{1,0:T(8,128)(2,1)S(1)} %add_convert_fusion.15), channel_id=1, source_target_pairs={{0,8},{2,10},{4,12},{6,14},{8,0},{10,2},{12,4},{14,6},{16,24},{18,... | collective-permute-start | bytes 786440 | tf_op jit(solution)/shard_map/ppermute | solution.py:779
  304.1 26.0 %collective-permute-start.49 = (bf16[128,1024]{1,0:T(8,128)(2,1)S(1)}, bf16[128,1024]{1,0:T(8,128)(2,1)S(1)}, u32[]{:S(2)}, u32[]{:S(2)}) collective-permute-start(bf16[128,1024]{1,0:T(8,128)(2,1)S(1)} %constant_dynamic-slice_fusion.6), channel_id=1, source_target_pairs={{0,8},{2,10},{4,12},{6,14},{8,0},{10,2},{12,4},{14,6},{16,24},{18,... | collective-permute-start | bytes 786440 | tf_op jit(solution)/shard_map/ppermute | solution.py:779
  309.6 26.2 %collective-permute-start.54 = (bf16[512,1024]{1,0:T(8,128)(2,1)}, bf16[512,1024]{1,0:T(8,128)(2,1)S(1)}, u32[]{:S(2)}, u32[]{:S(2)}) collective-permute-start(bf16[512,1024]{1,0:T(8,128)(2,1)} %add_convert_fusion.3), channel_id=1, source_target_pairs={{0,2},{2,0},{4,6},{6,4},{8,10},{10,8},{12,14},{14,12},{16,20},{18,... | collective-permute-start | bytes 3145736 | tf_op jit(solution)/shard_map/ppermute | solution.py:779
  335.4 24.1 %collective-permute-start.42 = (bf16[512,1024]{1,0:T(8,128)(2,1)S(1)}, bf16[512,1024]{1,0:T(8,128)(2,1)S(1)}, u32[]{:S(2)}, u32[]{:S(2)}) collective-permute-start(bf16[512,1024]{1,0:T(8,128)(2,1)S(1)} %add_convert_fusion.2), channel_id=1, source_target_pairs={{0,2},{2,0},{4,6},{6,4},{8,10},{10,8},{12,14},{14,12},{16,20},{18,... | collective-permute-start | bytes 3145736 | tf_op jit(solution)/shard_map/ppermute | solution.py:779
  337.8 18.1 %collective-permute-start.55 = (bf16[256,1024]{1,0:T(8,128)(2,1)S(1)}, bf16[256,1024]{1,0:T(8,128)(2,1)S(1)}, u32[]{:S(2)}, u32[]{:S(2)}) collective-permute-start(bf16[256,1024]{1,0:T(8,128)(2,1)S(1)} %constant_dynamic-slice_fusion.2), channel_id=1, source_target_pairs={{0,4},{2,6},{4,0},{6,2},{8,12},{10,14},{12,8},{14,10},{16,18},{18,... | collective-permute-start | bytes 1572872 | tf_op jit(solution)/shard_map/ppermute | solution.py:779
  339.4 32.2 %collective-permute-start.62 = (bf16[256,1024]{1,0:T(8,128)(2,1)S(1)}, bf16[256,1024]{1,0:T(8,128)(2,1)S(1)}, u32[]{:S(2)}, u32[]{:S(2)}) collective-permute-start(bf16[256,1024]{1,0:T(8,128)(2,1)S(1)} %pad_maximum_fusion.13), channel_id=1, source_target_pairs={{0,4},{2,6},{4,0},{6,2},{8,12},{10,14},{12,8},{14,10},{16,18},{18,... | collective-permute-start | bytes 1572872 | tf_op jit(solution)/shard_map/ppermute | solution.py:779
  344.6 34.2 %collective-permute-start.51 = (bf16[256,1024]{1,0:T(8,128)(2,1)S(1)}, bf16[256,1024]{1,0:T(8,128)(2,1)S(1)}, u32[]{:S(2)}, u32[]{:S(2)}) collective-permute-start(bf16[256,1024]{1,0:T(8,128)(2,1)S(1)} %pad_maximum_fusion.11), channel_id=1, source_target_pairs={{0,4},{2,6},{4,0},{6,2},{8,12},{10,14},{12,8},{14,10},{16,18},{18,... | collective-permute-start | bytes 1572872 | tf_op jit(solution)/shard_map/ppermute | solution.py:779
  356.1 23.6 %collective-permute-start.56 = (bf16[128,1024]{1,0:T(8,128)(2,1)S(1)}, bf16[128,1024]{1,0:T(8,128)(2,1)S(1)}, u32[]{:S(2)}, u32[]{:S(2)}) collective-permute-start(bf16[128,1024]{1,0:T(8,128)(2,1)S(1)} %constant_dynamic-slice_fusion.1), channel_id=1, source_target_pairs={{0,8},{2,10},{4,12},{6,14},{8,0},{10,2},{12,4},{14,6},{16,24},{18,... | collective-permute-start | bytes 786440 | tf_op jit(solution)/shard_map/ppermute | solution.py:779
  361.4 24.5 %collective-permute-start.43 = (bf16[256,1024]{1,0:T(8,128)(2,1)S(1)}, bf16[256,1024]{1,0:T(8,128)(2,1)S(1)}, u32[]{:S(2)}, u32[]{:S(2)}) collective-permute-start(bf16[256,1024]{1,0:T(8,128)(2,1)S(1)} %constant_dynamic-slice_fusion.5), channel_id=1, source_target_pairs={{0,4},{2,6},{4,0},{6,2},{8,12},{10,14},{12,8},{14,10},{16,18},{18,... | collective-permute-start | bytes 1572872 | tf_op jit(solution)/shard_map/ppermute | solution.py:779
  387.3 36.5 %collective-permute-start.63 = (bf16[512,1024]{1,0:T(8,128)(2,1)}, bf16[512,1024]{1,0:T(8,128)(2,1)}, u32[]{:S(2)}, u32[]{:S(2)}) collective-permute-start(bf16[512,1024]{1,0:T(8,128)(2,1)} %pad_maximum_fusion.7), channel_id=1, source_target_pairs={{0,2},{2,0},{4,6},{6,4},{8,10},{10,8},{12,14},{14,12},{16,20},{18,... | collective-permute-start | bytes 3145736 | tf_op jit(solution)/shard_map/ppermute | solution.py:779
  400.5 20.5 %collective-permute-start.58 = (bf16[256,1024]{1,0:T(8,128)(2,1)}, bf16[256,1024]{1,0:T(8,128)(2,1)S(1)}, u32[]{:S(2)}, u32[]{:S(2)}) collective-permute-start(bf16[256,1024]{1,0:T(8,128)(2,1)} %pad_maximum_fusion.12), channel_id=1, source_target_pairs={{0,4},{2,6},{4,0},{6,2},{8,12},{10,14},{12,8},{14,10},{16,18},{18,... | collective-permute-start | bytes 1572872 | tf_op jit(solution)/shard_map/ppermute | solution.py:779
  404.5 33.4 %collective-permute-start.52 = (bf16[512,1024]{1,0:T(8,128)(2,1)S(1)}, bf16[512,1024]{1,0:T(8,128)(2,1)S(1)}, u32[]{:S(2)}, u32[]{:S(2)}) collective-permute-start(bf16[512,1024]{1,0:T(8,128)(2,1)S(1)} %pad_maximum_fusion.5), channel_id=1, source_target_pairs={{0,2},{2,0},{4,6},{6,4},{8,10},{10,8},{12,14},{14,12},{16,20},{18,... | collective-permute-start | bytes 3145736 | tf_op jit(solution)/shard_map/ppermute | solution.py:779
  413.2 19.1 %collective-permute-start.46 = (bf16[256,1024]{1,0:T(8,128)(2,1)S(1)}, bf16[256,1024]{1,0:T(8,128)(2,1)S(1)}, u32[]{:S(2)}, u32[]{:S(2)}) collective-permute-start(bf16[256,1024]{1,0:T(8,128)(2,1)S(1)} %pad_maximum_fusion.10), channel_id=1, source_target_pairs={{0,4},{2,6},{4,0},{6,2},{8,12},{10,14},{12,8},{14,10},{16,18},{18,... | collective-permute-start | bytes 1572872 | tf_op jit(solution)/shard_map/ppermute | solution.py:779
  421.4 21.2 %collective-permute-start.59 = (bf16[512,1024]{1,0:T(8,128)(2,1)S(1)}, bf16[512,1024]{1,0:T(8,128)(2,1)S(1)}, u32[]{:S(2)}, u32[]{:S(2)}) collective-permute-start(bf16[512,1024]{1,0:T(8,128)(2,1)S(1)} %pad_maximum_fusion.6), channel_id=1, source_target_pairs={{0,2},{2,0},{4,6},{6,4},{8,10},{10,8},{12,14},{14,12},{16,20},{18,... | collective-permute-start | bytes 3145736 | tf_op jit(solution)/shard_map/ppermute | solution.py:779
  435.3 42.1 %collective-permute-start.64 = (bf16[1024,1024]{1,0:T(8,128)(2,1)S(1)}, bf16[1024,1024]{1,0:T(8,128)(2,1)}, u32[]{:S(2)}, u32[]{:S(2)}) collective-permute-start(bf16[1024,1024]{1,0:T(8,128)(2,1)S(1)} %pad_maximum_fusion.3.own1), channel_id=1, source_target_pairs={{0,16},{1,17},{2,18},{3,19},{4,20},{5,21},{6,22},{7,23},{8,24},{9,... | collective-permute-start | bytes 6291464 | tf_op jit(solution)/shard_map/ppermute | solution.py:779
  439.9 42.7 %collective-permute-start.53 = (bf16[1024,1024]{1,0:T(8,128)(2,1)}, bf16[1024,1024]{1,0:T(8,128)(2,1)}, u32[]{:S(2)}, u32[]{:S(2)}) collective-permute-start(bf16[1024,1024]{1,0:T(8,128)(2,1)} %pad_maximum_fusion.1.own1), channel_id=1, source_target_pairs={{0,16},{1,17},{2,18},{3,19},{4,20},{5,21},{6,22},{7,23},{8,24},{9,... | collective-permute-start | bytes 6291464 | tf_op jit(solution)/shard_map/ppermute | solution.py:779
  444.6 32.7 %collective-permute-start.60 = (bf16[1024,1024]{1,0:T(8,128)(2,1)}, bf16[1024,1024]{1,0:T(8,128)(2,1)}, u32[]{:S(2)}, u32[]{:S(2)}) collective-permute-start(bf16[1024,1024]{1,0:T(8,128)(2,1)} %pad_maximum_fusion.2.own0), channel_id=1, source_target_pairs={{16,0},{17,1},{18,2},{19,3},{20,4},{21,5},{22,6},{23,7},{24,8},{25... | collective-permute-start | bytes 6291464 | tf_op jit(solution)/shard_map/ppermute | solution.py:779
  450.0 32.6 %collective-permute-start.48 = (bf16[1024,1024]{1,0:T(8,128)(2,1)}, bf16[1024,1024]{1,0:T(8,128)(2,1)}, u32[]{:S(2)}, u32[]{:S(2)}) collective-permute-start(bf16[1024,1024]{1,0:T(8,128)(2,1)} %pad_maximum_fusion.own0), channel_id=1, source_target_pairs={{16,0},{17,1},{18,2},{19,3},{20,4},{21,5},{22,6},{23,7},{24,8},{25... | collective-permute-start | bytes 6291464 | tf_op jit(solution)/shard_map/ppermute | solution.py:779
  (53 other events, 658.8 us)

commit v4 on v3

--- a/solution.py
+++ b/solution.py
@@ -985,9 +985,10 @@
     (grads_in, results), _ = lax.optimization_barrier(((grads_in, sums[3].results), g0["du"]))
     sums[3].results = results
     while any(not flow.done for flow in sums + [norm_flow]):
-        for flow in sums + [norm_flow]:
-            if not flow.done:
-                flow.advance()
+        for n in (1, 2, 3):
+            if not sums[n].done:
+                sums[n].advance()
+        together([sums[0], norm_flow])
     parts = [flow.value for flow in sums]
     grad_down, grad_up = final_mlp_call(here, [*parts[2], *parts[0]], width)
     grad_out, grad_qkv = final_attention_call(here, [*parts[3], *parts[1]], width)

time: 495 us -> 484 us (0.978)
  the two profiles are of different devices: /device:TPU:0 before, /device:TPU:5 now
where the time goes in v4:
time: 484 us; the launch traced here: 477 us
  Pallas kernels  185 us (38%)
  waiting for transfers between devices  146 us (30%)
  starting transfers between devices  78.9 us (16%)
  other arithmetic  46.5 us (10%)
  local copies, waits for them, and re-layouts  17.6 us (4%)
    pallas_call x12, Pallas kernels, room_call(): pl.pallas_call(whole, in_specs=[pl.BlockSpec(memory_space=pltpu.SMEM)] *...  172 us
    ppermute x42, waiting for transfers between devices, move(): return lambda value: lax.ppermute(value, axis, route)  83.2 us
    ppermute x4, waiting for transfers between devices, around(): lax.ppermute(pair[0], 'dp', ring_up)  43.2 us
    ppermute x42, starting transfers between devices, move(): return lambda value: lax.ppermute(value, axis, route)  41.6 us
    ppermute x6, starting transfers between devices, swap_cores(): return lax.ppermute(value, 'section', swap)  16.1 us
    convert_element_type x4, other arithmetic, sum_steps(): both(1 - bits[0]).astype(bf16)  10.5 us
    pallas_call x2, Pallas kernels, final_call(): pl.pallas_call(kernel, in_specs=[pl.BlockSpec(memory_space=pltpu.SMEM)] +...  10.4 us
  transfers between devices with their start and end apart: 69, of which 18 were waited for; matrix products, arithmetic and copies ran while one was open for 12% of the time, Pallas kernels for 33%

profile of v4, /device:TPU:5, one launch (start us, length us, event | category | flops | bytes accessed | tf_op | source)
XLA Modules:
  0.0 476.7 jit_solution(3399225678192557684)
XLA Ops:
  2.0 2.9 cut.1
  9.1 9.7 %collective-permute-done = bf16[256,1024]{1,0:T(8,128)(2,1)S(1)} collective-permute-done((bf16[256,1024]{1,0:T(8,128)(2,1)}, bf16[256,1024]{1,0:T(8,128)(2,1)S(1)}, u32[]{:S(2)}, u32[]{:S(2)}) %collective-permute-start) | collective-permute-done | bytes 524320 | tf_op jit(solution)/shard_map/ppermute | solution.py:776
  18.8 6.5 %collective-permute-start.2 = (bf16[256,1024]{1,0:T(8,128)(2,1)S(1)}, bf16[256,1024]{1,0:T(8,128)(2,1)S(1)}, u32[]{:S(2)}, u32[]{:S(2)}) collective-permute-start(bf16[256,1024]{1,0:T(8,128)(2,1)S(1)} %pad_maximum_fusion.9), channel_id=1, source_target_pairs={{0,16},{16,0},{1,17},{17,1},{2,18},{18,2},{3,19},{19,3},{4,20},{20... | collective-permute-start | bytes 1572872 | tf_op jit(solution)/shard_map/ppermute | solution.py:773
  30.4 9.6 %collective-permute-done.6 = bf16[256,1024]{1,0:T(8,128)(2,1)} collective-permute-done((bf16[256,1024]{1,0:T(8,128)(2,1)}, bf16[256,1024]{1,0:T(8,128)(2,1)}, u32[]{:S(2)}, u32[]{:S(2)}) %collective-permute-start.6) | collective-permute-done | bytes 524320 | tf_op jit(solution)/shard_map/ppermute | solution.py:762
  42.0 3.1 maximum_select_fusion.refs_2_.refs_7_
  46.0 3.1 collective-permute-start.22
  49.2 10.0 %first.2 = (bf16[512,1024]{1,0:T(8,128)(2,1)}, bf16[512,1536]{1,0:T(8,128)(2,1)}, bf16[512,512]{1,0:T(8,128)(2,1)}, f32[512,1024]{1,0:T(8,128)}) custom-call(s32[1]{0:T(128)} %bitcast.refs_0_.scalar_ref, s32[2]{0:T(128)} %pad_add_fusion.refs_1_.refs_2_, bf16[512,1024]{1,0:T(8,128)(2,1)} %maximum_select_fusion.refs_2_.refs_7_, s32[512,1]{1,0:T(8,128)} %copy.29.refs_3_, ...), custom_call_target="tpu_custom_call" | custom-call | flops 2415919104 | bytes 10496000 | tf_op jit(solution)/shard_map/first/pallas_call | solution.py:254
  61.3 17.4 %collective-permute-done.10.refs_9_.refs_11_.refs_12_.refs_16_ = bf16[384,1024]{1,0:T(8,128)(2,1)S(1)} collective-permute-done((bf16[384,1024]{1,0:T(8,128)(2,1)}, bf16[384,1024]{1,0:T(8,128)(2,1)S(1)}, u32[]{:S(2)}, u32[]{:S(2)}) %collective-permute-start.10) | collective-permute-done | bytes 786464 | tf_op jit(solution)/shard_map/ppermute | solution.py:809
  82.1 16.8 %collective-permute-done.14.refs_10_.refs_12_.refs_13_.refs_17_ = bf16[384,1024]{1,0:T(8,128)(2,1)S(1)} collective-permute-done((bf16[384,1024]{1,0:T(8,128)(2,1)S(1)}, bf16[384,1024]{1,0:T(8,128)(2,1)S(1)}, u32[]{:S(2)}, u32[]{:S(2)}) %collective-permute-start.14) | collective-permute-done | bytes 786464 | tf_op jit(solution)/shard_map/ppermute | solution.py:809
  104.9 8.9 %collective-permute-done.18.refs_14_.refs_16_.refs_21_.refs_17_ = bf16[192,1024]{1,0:T(8,128)(2,1)S(1)} collective-permute-done((bf16[192,1024]{1,0:T(8,128)(2,1)S(1)}, bf16[192,1024]{1,0:T(8,128)(2,1)S(1)}, u32[]{:S(2)}, u32[]{:S(2)}) %collective-permute-start.18) | collective-permute-done | bytes 393248 | tf_op jit(solution)/shard_map/ppermute | solution.py:809
  121.2 11.8 %second.2 = (bf16[512,1536]{1,0:T(8,128)(2,1)}, f32[512,1024]{1,0:T(8,128)}, bf16[512,1024]{1,0:T(8,128)(2,1)}) custom-call(s32[1]{0:T(128)} %bitcast.refs_0_.scalar_ref, s32[9]{0:T(128)} %pad_add_fusion.1.refs_1_.refs_2_, bf16[512,1024]{1,0:T(8,128)(2,1)} %get-tuple-element.271.refs_2_.refs_6_, s32[512,1]{1,0:T(8,128)} %copy.30.refs_3_, ...), custom_call_target="tpu_custom_call" | custom-call | flops 2415919104 | bytes 12068864 | tf_op jit(solution)/shard_map/second/pallas_call | solution.py:254
  133.1 12.1 %feed.2 = (bf16[512,1024]{1,0:T(8,128)(2,1)}, bf16[512,1024]{1,0:T(8,128)(2,1)}, bf16[512,1024]{1,0:T(8,128)(2,1)}, bf16[512,1024]{1,0:T(8,128)(2,1)}) custom-call(s32[1]{0:T(128)} %bitcast.refs_0_.scalar_ref, s32[2]{0:T(128)} %pad_add_fusion.refs_1_.refs_2_, s32[9]{0:T(128)} %pad_add_fusion.1.refs_1_.refs_2_, ...), custom_call_target="tpu_custom_call" | custom-call | flops 4294967296 | bytes 15728640 | tf_op jit(solution)/shard_map/feed/pallas_call | solution.py:254
  145.2 2.9 collective-permute-start.28
  148.1 3.0 collective-permute-start.29
  154.6 10.3 %first.3 = (bf16[512,1024]{1,0:T(8,128)(2,1)}, bf16[512,1536]{1,0:T(8,128)(2,1)}, bf16[512,512]{1,0:T(8,128)(2,1)}, f32[512,1024]{1,0:T(8,128)}) custom-call(s32[1]{0:T(128)} %bitcast.refs_0_.scalar_ref, s32[2]{0:T(128)} %pad_add_fusion.3.refs_1_.refs_2_, bf16[512,1024]{1,0:T(8,128)(2,1)} %get-tuple-element.244.refs_2_.refs_7_, s32[512,1]{1,0:T(8,128)} %copy.31.refs_3_, ...), custom_call_target="tpu_custom_call" | custom-call | flops 2415919104 | bytes 10496000 | tf_op jit(solution)/shard_map/first/pallas_call | solution.py:254
  165.7 11.7 %second.3 = (bf16[512,1536]{1,0:T(8,128)(2,1)}, f32[512,1024]{1,0:T(8,128)}, bf16[512,1024]{1,0:T(8,128)(2,1)}) custom-call(s32[1]{0:T(128)} %bitcast.refs_0_.scalar_ref, s32[9]{0:T(128)} %pad_add_fusion.1.refs_1_.refs_2_, bf16[512,1024]{1,0:T(8,128)(2,1)} %get-tuple-element.234.refs_2_.refs_6_, s32[512,1]{1,0:T(8,128)} %copy.32.refs_3_, ...), custom_call_target="tpu_custom_call" | custom-call | flops 2415919104 | bytes 12068864 | tf_op jit(solution)/shard_map/second/pallas_call | solution.py:254
  180.2 12.7 %feed.3 = (bf16[512,1024]{1,0:T(8,128)(2,1)}, bf16[512,1024]{1,0:T(8,128)(2,1)}, bf16[512,1024]{1,0:T(8,128)(2,1)}, bf16[512,1024]{1,0:T(8,128)(2,1)}) custom-call(s32[1]{0:T(128)} %bitcast.refs_0_.scalar_ref, s32[2]{0:T(128)} %pad_add_fusion.3.refs_1_.refs_2_, s32[2]{0:T(128)} %pad_add_fusion.3.refs_1_.refs_2_, ...), custom_call_target="tpu_custom_call" | custom-call | flops 4294967296 | bytes 15728640 | tf_op jit(solution)/shard_map/feed/pallas_call | solution.py:254
  194.3 16.0 %feed_back.2 = (bf16[1024,1024]{1,0:T(8,128)(2,1)}, bf16[1024,1024]{1,0:T(8,128)(2,1)}, f32[512,1024]{1,0:T(8,128)}, bf16[512,1024]{1,0:T(8,128)(2,1)}, f32[2,1024]{1,0:T(2,128)}) custom-call(s32[1]{0:T(128)} %bitcast.refs_0_.scalar_ref, s32[2]{0:T(128)} %pad_add_fusion.3.refs_1_.refs_2_, s32[2]{0:T(128)} %pad_add_fusion.3.refs_1_.refs_2_, ...), custom_call_target="tpu_custom_call" | custom-call | flops 6442450944 | bytes 23080960 | tf_op jit(solution)/shard_map/feed_back/pallas_call | solution.py:254
  213.4 16.1 %heads_back.2 = (bf16[1024,1024]{1,0:T(8,128)(2,1)}, bf16[1024,1024]{1,0:T(8,128)(2,1)}, bf16[512,1536]{1,0:T(8,128)(2,1)}) custom-call(s32[1]{0:T(128)} %bitcast.refs_0_.scalar_ref, s32[2]{0:T(128)} %pad_add_fusion.3.refs_1_.refs_2_, bf16[512,1024]{1,0:T(8,128)(2,1)} %get-tuple-element.240.refs_2_.refs_3_, bf16[512,1536]{1,0:T(8,128)(2,1)} %get-tuple-element.231.refs_3_, ...), custom_call_target="tpu_custom_call" | custom-call | flops 4563402752 | bytes 11012096 | tf_op jit(solution)/shard_map/heads_back/pallas_call | solution.py:254
  229.6 2.6 add_convert_fusion.7
  233.7 18.7 %input_back.2 = (bf16[512,1024]{1,0:T(8,128)(2,1)}, f32[2,1024]{1,0:T(2,128)}) custom-call(s32[1]{0:T(128)} %bitcast.refs_0_.scalar_ref, s32[9]{0:T(128)} %pad_add_fusion.1.refs_1_.refs_2_, s32[2]{0:T(128)} %pad_add_fusion.3.refs_1_.refs_2_, bf16[512,1024]{1,0:T(8,128)(2,1)} %get-tuple-element.240.refs_2_.refs_3_, ...), custom_call_target="tpu_custom_call" | custom-call | flops 5637144576 | bytes 15742976 | tf_op jit(solution)/shard_map/input_back/pallas_call | solution.py:254
  252.5 2.8 add_convert_fusion.5
  259.4 18.0 %feed_back.3 = (bf16[1024,1024]{1,0:T(8,128)(2,1)}, bf16[1024,1024]{1,0:T(8,128)(2,1)}, f32[512,1024]{1,0:T(8,128)}, bf16[512,1024]{1,0:T(8,128)(2,1)}, f32[2,1024]{1,0:T(2,128)}) custom-call(s32[1]{0:T(128)} %bitcast.refs_0_.scalar_ref, s32[2]{0:T(128)} %pad_add_fusion.refs_1_.refs_2_, s32[9]{0:T(128)} %pad_add_fusion.1.refs_1_.refs_2_, ...), custom_call_target="tpu_custom_call" | custom-call | flops 6442450944 | bytes 23080960 | tf_op jit(solution)/shard_map/feed_back/pallas_call | solution.py:254
  277.5 2.2 add_convert_fusion.4
  285.0 16.1 %heads_back.3 = (bf16[1024,1024]{1,0:T(8,128)(2,1)}, bf16[1024,1024]{1,0:T(8,128)(2,1)}, bf16[512,1536]{1,0:T(8,128)(2,1)}) custom-call(s32[1]{0:T(128)} %bitcast.refs_0_.scalar_ref, s32[2]{0:T(128)} %pad_add_fusion.refs_1_.refs_2_, bf16[512,1024]{1,0:T(8,128)(2,1)} %get-tuple-element.279.refs_2_.refs_3_, bf16[512,1536]{1,0:T(8,128)(2,1)} %get-tuple-element.268.refs_3_, ...), custom_call_target="tpu_custom_call" | custom-call | flops 4563402752 | bytes 11012096 | tf_op jit(solution)/shard_map/heads_back/pallas_call | solution.py:254
  305.7 2.6 add_convert_fusion.3
  309.9 18.3 %input_back.3 = (bf16[512,1024]{1,0:T(8,128)(2,1)}, f32[2,1024]{1,0:T(2,128)}) custom-call(s32[1]{0:T(128)} %bitcast.refs_0_.scalar_ref, s32[9]{0:T(128)} %pad_add_fusion.1.refs_1_.refs_2_, s32[2]{0:T(128)} %pad_add_fusion.refs_1_.refs_2_, bf16[512,1024]{1,0:T(8,128)(2,1)} %get-tuple-element.279.refs_2_.refs_3_, ...), custom_call_target="tpu_custom_call" | custom-call | flops 5637144576 | bytes 15742976 | tf_op jit(solution)/shard_map/input_back/pallas_call | solution.py:254
  333.0 2.6 add_convert_fusion.2
  341.5 7.6 %collective-permute-start.63 = (f32[8,1024]{1,0:T(8,128)S(1)}, f32[8,1024]{1,0:T(8,128)S(1)}, u32[]{:S(2)}, u32[]{:S(2)}) collective-permute-start(f32[8,1024]{1,0:T(8,128)S(1)} %concatenate.111), channel_id=1, source_target_pairs={{0,16},{16,0},{1,17},{17,1},{2,18},{18,2},{3,19},{19,3},{4,20},{20... | collective-permute-start | bytes 98312 | tf_op jit(solution)/shard_map/ppermute | solution.py:773
  351.7 2.5 maximum_select_fusion.3
  355.5 3.2 collective-permute-start.56
  358.6 10.9 %collective-permute-done.42 = bf16[512,1024]{1,0:T(8,128)(2,1)} collective-permute-done((bf16[512,1024]{1,0:T(8,128)(2,1)}, bf16[512,1024]{1,0:T(8,128)(2,1)}, u32[]{:S(2)}, u32[]{:S(2)}) %collective-permute-start.42) | collective-permute-done | bytes 1048608 | tf_op jit(solution)/shard_map/ppermute | solution.py:779
  369.6 2.2 add_convert_fusion.1
  372.6 2.8 collective-permute-start.57
  375.4 10.5 %collective-permute-done.43 = bf16[256,1024]{1,0:T(8,128)(2,1)S(1)} collective-permute-done((bf16[256,1024]{1,0:T(8,128)(2,1)S(1)}, bf16[256,1024]{1,0:T(8,128)(2,1)S(1)}, u32[]{:S(2)}, u32[]{:S(2)}) %collective-permute-start.43) | collective-permute-done | bytes 524320 | tf_op jit(solution)/shard_map/ppermute | solution.py:779
  386.2 11.4 %collective-permute-done.57 = bf16[128,1024]{1,0:T(8,128)(2,1)S(1)} collective-permute-done((bf16[128,1024]{1,0:T(8,128)(2,1)S(1)}, bf16[128,1024]{1,0:T(8,128)(2,1)S(1)}, u32[]{:S(2)}, u32[]{:S(2)}) %collective-permute-start.57) | collective-permute-done | bytes 262176 | tf_op jit(solution)/shard_map/ppermute | solution.py:779
  397.7 5.5 %collective-permute-done.44 = bf16[128,1024]{1,0:T(8,128)(2,1)S(1)} collective-permute-done((bf16[128,1024]{1,0:T(8,128)(2,1)S(1)}, bf16[128,1024]{1,0:T(8,128)(2,1)S(1)}, u32[]{:S(2)}, u32[]{:S(2)}) %collective-permute-start.44) | collective-permute-done | bytes 262176 | tf_op jit(solution)/shard_map/ppermute | solution.py:779
  403.3 2.9 collective-permute-start.45
  406.5 10.9 %collective-permute-done.45 = bf16[128,1024]{1,0:T(8,128)(2,1)S(1)} collective-permute-done((bf16[128,1024]{1,0:T(8,128)(2,1)S(1)}, bf16[128,1024]{1,0:T(8,128)(2,1)S(1)}, u32[]{:S(2)}, u32[]{:S(2)}) %collective-permute-start.45) | collective-permute-done | bytes 262176 | tf_op jit(solution)/shard_map/ppermute | solution.py:779
  418.5 11.6 %collective-permute-done.46 = bf16[256,1024]{1,0:T(8,128)(2,1)S(1)} collective-permute-done((bf16[256,1024]{1,0:T(8,128)(2,1)S(1)}, bf16[256,1024]{1,0:T(8,128)(2,1)S(1)}, u32[]{:S(2)}, u32[]{:S(2)}) %collective-permute-start.46) | collective-permute-done | bytes 524320 | tf_op jit(solution)/shard_map/ppermute | solution.py:779
  435.5 7.4 %collective-permute-done.59 = bf16[512,1024]{1,0:T(8,128)(2,1)S(1)} collective-permute-done((bf16[512,1024]{1,0:T(8,128)(2,1)S(1)}, bf16[512,1024]{1,0:T(8,128)(2,1)S(1)}, u32[]{:S(2)}, u32[]{:S(2)}) %collective-permute-start.59) | collective-permute-done | bytes 1048608 | tf_op jit(solution)/shard_map/ppermute | solution.py:779
  444.9 2.6 collective-permute-start.60
  447.5 6.2 %collective-permute-done.47 = bf16[512,1024]{1,0:T(8,128)(2,1)S(1)} collective-permute-done((bf16[512,1024]{1,0:T(8,128)(2,1)S(1)}, bf16[512,1024]{1,0:T(8,128)(2,1)S(1)}, u32[]{:S(2)}, u32[]{:S(2)}) %collective-permute-start.47) | collective-permute-done | bytes 1048608 | tf_op jit(solution)/shard_map/ppermute | solution.py:779
  455.9 2.6 collective-permute-start.48
  458.6 2.8 collective-permute-done.67
  461.4 3.7 collective-permute-done.68
  465.8 5.2 %final_mlp.1 = (f32[1024,1024]{1,0:T(8,128)}, f32[1024,1024]{1,0:T(8,128)}) custom-call(s32[1]{0:T(128)} %bitcast.refs_0_.scalar_ref, bf16[1024,1024]{1,0:T(8,128)(2,1)} %pad_maximum_fusion.2.own0, bf16[1024,1024]{1,0:T(8,128)(2,1)} %collective-permute-done.60.far0, bf16[1024,1024]{1,0:T(8,128)(2,1)} %copy-done.14, bf16[1024,1024]{1,0:T(8,128)(2,1)} %copy-done.25), custom_call_target="tpu_custom_call" | custom-call | bytes 12582912 | tf_op jit(solution)/shard_map/final_mlp/pallas_call | solution.py:687
  471.1 5.2 %final_attention.1 = (f32[512,1024]{1,0:T(8,128)}, f32[3,1024,512]{2,1,0:T(8,128)}) custom-call(s32[1]{0:T(128)} %bitcast.refs_0_.scalar_ref, bf16[1024,1024]{1,0:T(8,128)(2,1)} %pad_maximum_fusion.own0, bf16[1024,1024]{1,0:T(8,128)(2,1)} %collective-permute-done.48.far0, bf16[1024,1024]{1,0:T(8,128)(2,1)} %pad_maximum_fusion.1.own1, ...), custom_call_target="tpu_custom_call" | custom-call | bytes 12582912 | tf_op jit(solution)/shard_map/final_attention/pallas_call | solution.py:687
  (275 shorter events, 88.6 us)
Async XLA Ops:
  0.6 48.5 %collective-permute-start.8 = (bf16[3,1024,512]{2,1,0:T(8,128)(2,1)}, bf16[3,1024,512]{2,1,0:T(8,128)(2,1)}, u32[]{:S(2)}, u32[]{:S(2)}) collective-permute-start(bf16[3,1024,512]{2,1,0:T(8,128)(2,1)} %bitcast.33), channel_id=1, source_target_pairs={{0,16},{16,0},{1,17},{17,1},{2,18},{18,2},{3,19},{19,3},{4,20},{20... | collective-permute-start | bytes 9437192 | tf_op jit(solution)/shard_map/ppermute | solution.py:770
  6.9 39.1 %collective-permute-start.9 = (bf16[512,1024]{1,0:T(8,128)(2,1)}, bf16[512,1024]{1,0:T(8,128)(2,1)}, u32[]{:S(2)}, u32[]{:S(2)}) collective-permute-start(bf16[512,1024]{1,0:T(8,128)(2,1)} %bitcast.4.out.refs_7_), channel_id=1, source_target_pairs={{0,16},{16,0},{1,17},{17,1},{2,18},{18,2},{3,19},{19,3},{4,20},{20... | collective-permute-start | bytes 3145736 | tf_op jit(solution)/shard_map/ppermute | solution.py:770
  28.9 30.3 %collective-permute-start.3 = (bf16[384,1024]{1,0:T(8,128)(2,1)S(1)}, bf16[384,1024]{1,0:T(8,128)(2,1)}, u32[]{:S(2)}, u32[]{:S(2)}) collective-permute-start(bf16[384,1024]{1,0:T(8,128)(2,1)S(1)} %pad_maximum_fusion.8.refs_7_.refs_9_.refs_10_.refs_14_), channel_id=1, source_target_pairs={{0,4},{4,8},{8,12},{12,14},{14,10},{10,6},{6,2},{2,0},{1,5},{5,9},... | collective-permute-start | bytes 2359304 | tf_op jit(solution)/shard_map/ppermute | solution.py:809
  29.2 30.0 %collective-permute-start.4 = (bf16[384,1024]{1,0:T(8,128)(2,1)S(1)}, bf16[384,1024]{1,0:T(8,128)(2,1)}, u32[]{:S(2)}, u32[]{:S(2)}) collective-permute-start(bf16[384,1024]{1,0:T(8,128)(2,1)S(1)} %pad_maximum_fusion.8.refs_7_.refs_9_.refs_10_.refs_14_), channel_id=1, source_target_pairs={{4,0},{8,4},{12,8},{14,12},{10,14},{6,10},{2,6},{0,2},{5,1},{9,5},... | collective-permute-start | bytes 2359304 | tf_op jit(solution)/shard_map/ppermute | solution.py:809
  40.0 19.2 %collective-permute-start.5 = (bf16[384,1024]{1,0:T(8,128)(2,1)S(1)}, bf16[384,1024]{1,0:T(8,128)(2,1)}, u32[]{:S(2)}, u32[]{:S(2)}) collective-permute-start(bf16[384,1024]{1,0:T(8,128)(2,1)S(1)} %pad_maximum_fusion.8.refs_7_.refs_9_.refs_10_.refs_14_), channel_id=1, source_target_pairs={{0,16},{16,0},{1,17},{17,1},{2,18},{18,2},{3,19},{19,3},{4,20},{20... | collective-permute-start | bytes 2359304 | tf_op jit(solution)/shard_map/ppermute | solution.py:779
  46.0 58.6 %collective-permute-start.22 = (bf16[1024,1024]{1,0:T(8,128)(2,1)S(1)}, bf16[1024,1024]{1,0:T(8,128)(2,1)}, u32[]{:S(2)}, u32[]{:S(2)}) collective-permute-start(bf16[1024,1024]{1,0:T(8,128)(2,1)S(1)} %bitcast.44), channel_id=1, source_target_pairs={{16,17},{17,16},{18,19},{19,18},{20,21},{21,20},{22,23},{23,22},{2... | collective-permute-start | bytes 6291464 | tf_op jit(solution)/shard_map/ppermute | solution.py:907
  59.2 19.5 %collective-permute-start.10 = (bf16[384,1024]{1,0:T(8,128)(2,1)}, bf16[384,1024]{1,0:T(8,128)(2,1)S(1)}, u32[]{:S(2)}, u32[]{:S(2)}) collective-permute-start(bf16[384,1024]{1,0:T(8,128)(2,1)} %collective-permute-done.3.refs_8_.refs_10_.refs_11_.refs_15_), channel_id=1, source_target_pairs={{0,4},{4,8},{8,12},{12,14},{14,10},{10,6},{6,2},{2,0},{1,5},{5,9},... | collective-permute-start | bytes 2359304 | tf_op jit(solution)/shard_map/ppermute | solution.py:809
  59.5 19.2 %collective-permute-start.11 = (bf16[384,1024]{1,0:T(8,128)(2,1)}, bf16[384,1024]{1,0:T(8,128)(2,1)S(1)}, u32[]{:S(2)}, u32[]{:S(2)}) collective-permute-start(bf16[384,1024]{1,0:T(8,128)(2,1)} %collective-permute-done.4.refs_11_.refs_13_.refs_14_.refs_18_), channel_id=1, source_target_pairs={{4,0},{8,4},{12,8},{14,12},{10,14},{6,10},{2,6},{0,2},{5,1},{9,5},... | collective-permute-start | bytes 2359304 | tf_op jit(solution)/shard_map/ppermute | solution.py:809
  60.8 17.9 %collective-permute-start.12 = (bf16[384,1024]{1,0:T(8,128)(2,1)}, bf16[384,1024]{1,0:T(8,128)(2,1)S(1)}, u32[]{:S(2)}, u32[]{:S(2)}) collective-permute-start(bf16[384,1024]{1,0:T(8,128)(2,1)} %collective-permute-done.3.refs_8_.refs_10_.refs_11_.refs_15_), channel_id=1, source_target_pairs={{0,16},{16,0},{1,17},{17,1},{2,18},{18,2},{3,19},{19,3},{4,20},{20... | collective-permute-start | bytes 2359304 | tf_op jit(solution)/shard_map/ppermute | solution.py:779
  60.8 18.9 %collective-permute-start.13 = (bf16[384,1024]{1,0:T(8,128)(2,1)}, bf16[384,1024]{1,0:T(8,128)(2,1)S(1)}, u32[]{:S(2)}, u32[]{:S(2)}) collective-permute-start(bf16[384,1024]{1,0:T(8,128)(2,1)} %collective-permute-done.4.refs_11_.refs_13_.refs_14_.refs_18_), channel_id=1, source_target_pairs={{0,16},{16,0},{1,17},{17,1},{2,18},{18,2},{3,19},{19,3},{4,20},{20... | collective-permute-start | bytes 2359304 | tf_op jit(solution)/shard_map/ppermute | solution.py:779
  79.6 19.3 %collective-permute-start.14 = (bf16[384,1024]{1,0:T(8,128)(2,1)S(1)}, bf16[384,1024]{1,0:T(8,128)(2,1)S(1)}, u32[]{:S(2)}, u32[]{:S(2)}) collective-permute-start(bf16[384,1024]{1,0:T(8,128)(2,1)S(1)} %collective-permute-done.10.refs_9_.refs_11_.refs_12_.refs_16_), channel_id=1, source_target_pairs={{0,4},{4,8},{8,12},{12,14},{14,10},{10,6},{6,2},{2,0},{1,5},{5,9},... | collective-permute-start | bytes 2359304 | tf_op jit(solution)/shard_map/ppermute | solution.py:809
  81.5 19.4 %collective-permute-start.15 = (bf16[384,1024]{1,0:T(8,128)(2,1)S(1)}, bf16[384,1024]{1,0:T(8,128)(2,1)S(1)}, u32[]{:S(2)}, u32[]{:S(2)}) collective-permute-start(bf16[384,1024]{1,0:T(8,128)(2,1)S(1)} %collective-permute-done.11.refs_12_.refs_14_.refs_15_.refs_19_), channel_id=1, source_target_pairs={{4,0},{8,4},{12,8},{14,12},{10,14},{6,10},{2,6},{0,2},{5,1},{9,5},... | collective-permute-start | bytes 2359304 | tf_op jit(solution)/shard_map/ppermute | solution.py:809
  81.5 20.5 %collective-permute-start.16 = (bf16[384,1024]{1,0:T(8,128)(2,1)S(1)}, bf16[384,1024]{1,0:T(8,128)(2,1)S(1)}, u32[]{:S(2)}, u32[]{:S(2)}) collective-permute-start(bf16[384,1024]{1,0:T(8,128)(2,1)S(1)} %collective-permute-done.10.refs_9_.refs_11_.refs_12_.refs_16_), channel_id=1, source_target_pairs={{0,16},{16,0},{1,17},{17,1},{2,18},{18,2},{3,19},{19,3},{4,20},{20... | collective-permute-start | bytes 2359304 | tf_op jit(solution)/shard_map/ppermute | solution.py:779
  82.1 20.8 %collective-permute-start.17 = (bf16[384,1024]{1,0:T(8,128)(2,1)S(1)}, bf16[384,1024]{1,0:T(8,128)(2,1)}, u32[]{:S(2)}, u32[]{:S(2)}) collective-permute-start(bf16[384,1024]{1,0:T(8,128)(2,1)S(1)} %collective-permute-done.11.refs_12_.refs_14_.refs_15_.refs_19_), channel_id=1, source_target_pairs={{0,16},{16,0},{1,17},{17,1},{2,18},{18,2},{3,19},{19,3},{4,20},{20... | collective-permute-start | bytes 2359304 | tf_op jit(solution)/shard_map/ppermute | solution.py:779
  99.0 34.0 %collective-permute-start.24 = (bf16[1024,1024]{1,0:T(8,128)(2,1)}, bf16[1024,1024]{1,0:T(8,128)(2,1)}, u32[]{:S(2)}, u32[]{:S(2)}) collective-permute-start(bf16[1024,1024]{1,0:T(8,128)(2,1)} %bitcast.47), channel_id=1, source_target_pairs={{16,17},{17,16},{18,19},{19,18},{20,21},{21,20},{22,23},{23,22},{2... | collective-permute-start | bytes 6291464 | tf_op jit(solution)/shard_map/ppermute | solution.py:908
  100.9 32.1 %collective-permute-start.25 = (bf16[1024,1024]{1,0:T(8,128)(2,1)S(1)}, bf16[1024,1024]{1,0:T(8,128)(2,1)}, u32[]{:S(2)}, u32[]{:S(2)}) collective-permute-start(bf16[1024,1024]{1,0:T(8,128)(2,1)S(1)} %bitcast.45), channel_id=1, source_target_pairs={{0,16},{16,0},{1,17},{17,1},{2,18},{18,2},{3,19},{19,3},{4,20},{20... | collective-permute-start | bytes 6291464 | tf_op jit(solution)/shard_map/ppermute | solution.py:770
  102.0 31.1 %collective-permute-start.26 = (bf16[1024,1024]{1,0:T(8,128)(2,1)}, bf16[1024,1024]{1,0:T(8,128)(2,1)}, u32[]{:S(2)}, u32[]{:S(2)}) collective-permute-start(bf16[1024,1024]{1,0:T(8,128)(2,1)} %bitcast.48), channel_id=1, source_target_pairs={{0,16},{16,0},{1,17},{17,1},{2,18},{18,2},{3,19},{19,3},{4,20},{20... | collective-permute-start | bytes 6291464 | tf_op jit(solution)/shard_map/ppermute | solution.py:770
  145.2 33.7 %collective-permute-start.28 = (bf16[1024,1024]{1,0:T(8,128)(2,1)}, bf16[1024,1024]{1,0:T(8,128)(2,1)S(1)}, u32[]{:S(2)}, u32[]{:S(2)}) collective-permute-start(bf16[1024,1024]{1,0:T(8,128)(2,1)} %collective-permute-done.22.refs_9_.refs_15_), channel_id=1, source_target_pairs={{16,0},{17,1},{18,2},{19,3},{20,4},{21,5},{22,6},{23,7},{24,8},{25... | collective-permute-start | bytes 6291464 | tf_op jit(solution)/shard_map/ppermute | solution.py:779
  148.1 30.8 %collective-permute-start.29 = (bf16[1024,1024]{1,0:T(8,128)(2,1)}, bf16[1024,1024]{1,0:T(8,128)(2,1)}, u32[]{:S(2)}, u32[]{:S(2)}) collective-permute-start(bf16[1024,1024]{1,0:T(8,128)(2,1)} %collective-permute-done.24.refs_10_.refs_14_), channel_id=1, source_target_pairs={{16,0},{17,1},{18,2},{19,3},{20,4},{21,5},{22,6},{23,7},{24,8},{25... | collective-permute-start | bytes 6291464 | tf_op jit(solution)/shard_map/ppermute | solution.py:779
  152.8 24.6 %collective-permute-start.31 = (bf16[256,1024]{1,0:T(8,128)(2,1)S(1)}, bf16[256,1024]{1,0:T(8,128)(2,1)S(1)}, u32[]{:S(2)}, u32[]{:S(2)}) collective-permute-start(bf16[256,1024]{1,0:T(8,128)(2,1)S(1)} %dynamic-slice_bitcast_fusion), channel_id=1, source_target_pairs={{0,1},{1,0},{2,3},{3,2},{4,5},{5,4},{6,7},{7,6},{8,9},{9,8},{10,11... | collective-permute-start | bytes 1572872 | tf_op jit(solution)/shard_map/ppermute | solution.py:762
  194.2 17.2 %collective-permute-start.30 = (bf16[256,1024]{1,0:T(8,128)(2,1)S(1)}, bf16[256,1024]{1,0:T(8,128)(2,1)S(1)}, u32[]{:S(2)}, u32[]{:S(2)}) collective-permute-start(bf16[256,1024]{1,0:T(8,128)(2,1)S(1)} %get-tuple-element.319), channel_id=1, source_target_pairs={{0,16},{16,0},{1,17},{17,1},{2,18},{18,2},{3,19},{19,3},{4,20},{20... | collective-permute-start | bytes 1572872 | tf_op jit(solution)/shard_map/ppermute | solution.py:770
  210.3 19.3 %collective-permute-start.32 = (bf16[1024,1024]{1,0:T(8,128)(2,1)}, bf16[1024,1024]{1,0:T(8,128)(2,1)}, u32[]{:S(2)}, u32[]{:S(2)}) collective-permute-start(bf16[1024,1024]{1,0:T(8,128)(2,1)} %get-tuple-element.229), channel_id=1, source_target_pairs={{0,16},{16,0},{1,17},{17,1},{2,18},{18,2},{3,19},{19,3},{4,20},{20... | collective-permute-start | bytes 6291464 | tf_op jit(solution)/shard_map/ppermute | solution.py:773
  229.5 22.9 %collective-permute-start.34 = (bf16[1024,1024]{1,0:T(8,128)(2,1)}, bf16[1024,1024]{1,0:T(8,128)(2,1)}, u32[]{:S(2)}, u32[]{:S(2)}) collective-permute-start(bf16[1024,1024]{1,0:T(8,128)(2,1)} %get-tuple-element.239), channel_id=1, source_target_pairs={{0,16},{16,0},{1,17},{17,1},{2,18},{18,2},{3,19},{19,3},{4,20},{20... | collective-permute-start | bytes 6291464 | tf_op jit(solution)/shard_map/ppermute | solution.py:773
  232.2 23.8 %collective-permute-start.33 = (bf16[512,1024]{1,0:T(8,128)(2,1)}, bf16[512,1024]{1,0:T(8,128)(2,1)S(1)}, u32[]{:S(2)}, u32[]{:S(2)}) collective-permute-start(bf16[512,1024]{1,0:T(8,128)(2,1)} %add_convert_fusion.7), channel_id=1, source_target_pairs={{0,2},{2,0},{4,6},{6,4},{8,10},{10,8},{12,14},{14,12},{16,20},{18,... | collective-permute-start | bytes 3145736 | tf_op jit(solution)/shard_map/ppermute | solution.py:779
  255.2 22.3 %collective-permute-start.36 = (bf16[512,1024]{1,0:T(8,128)(2,1)}, bf16[512,1024]{1,0:T(8,128)(2,1)S(1)}, u32[]{:S(2)}, u32[]{:S(2)}) collective-permute-start(bf16[512,1024]{1,0:T(8,128)(2,1)} %add_convert_fusion.5), channel_id=1, source_target_pairs={{0,2},{2,0},{4,6},{6,4},{8,10},{10,8},{12,14},{14,12},{16,20},{18,... | collective-permute-start | bytes 3145736 | tf_op jit(solution)/shard_map/ppermute | solution.py:779
  258.0 19.5 %collective-permute-start.35 = (bf16[256,1024]{1,0:T(8,128)(2,1)S(1)}, bf16[256,1024]{1,0:T(8,128)(2,1)S(1)}, u32[]{:S(2)}, u32[]{:S(2)}) collective-permute-start(bf16[256,1024]{1,0:T(8,128)(2,1)S(1)} %constant_dynamic-slice_fusion.9), channel_id=1, source_target_pairs={{0,4},{2,6},{4,0},{6,2},{8,12},{10,14},{12,8},{14,10},{16,18},{18,... | collective-permute-start | bytes 1572872 | tf_op jit(solution)/shard_map/ppermute | solution.py:779
  277.4 28.3 %collective-permute-start.39 = (bf16[1024,1024]{1,0:T(8,128)(2,1)}, bf16[1024,1024]{1,0:T(8,128)(2,1)}, u32[]{:S(2)}, u32[]{:S(2)}) collective-permute-start(bf16[1024,1024]{1,0:T(8,128)(2,1)} %get-tuple-element.266), channel_id=1, source_target_pairs={{0,16},{16,0},{1,17},{17,1},{2,18},{18,2},{3,19},{19,3},{4,20},{20... | collective-permute-start | bytes 6291464 | tf_op jit(solution)/shard_map/ppermute | solution.py:773
  280.5 22.2 %collective-permute-start.38 = (bf16[256,1024]{1,0:T(8,128)(2,1)}, bf16[256,1024]{1,0:T(8,128)(2,1)}, u32[]{:S(2)}, u32[]{:S(2)}) collective-permute-start(bf16[256,1024]{1,0:T(8,128)(2,1)} %constant_dynamic-slice_fusion.7), channel_id=1, source_target_pairs={{0,4},{2,6},{4,0},{6,2},{8,12},{10,14},{12,8},{14,10},{16,18},{18,... | collective-permute-start | bytes 1572872 | tf_op jit(solution)/shard_map/ppermute | solution.py:779
  282.4 19.5 %collective-permute-start.37 = (bf16[128,1024]{1,0:T(8,128)(2,1)S(1)}, bf16[128,1024]{1,0:T(8,128)(2,1)S(1)}, u32[]{:S(2)}, u32[]{:S(2)}) collective-permute-start(bf16[128,1024]{1,0:T(8,128)(2,1)S(1)} %constant_dynamic-slice_fusion.8), channel_id=1, source_target_pairs={{0,8},{2,10},{4,12},{6,14},{8,0},{10,2},{12,4},{14,6},{16,24},{18,... | collective-permute-start | bytes 786440 | tf_op jit(solution)/shard_map/ppermute | solution.py:779
  301.0 32.0 %collective-permute-start.41 = (bf16[1024,1024]{1,0:T(8,128)(2,1)}, bf16[1024,1024]{1,0:T(8,128)(2,1)}, u32[]{:S(2)}, u32[]{:S(2)}) collective-permute-start(bf16[1024,1024]{1,0:T(8,128)(2,1)} %get-tuple-element.278), channel_id=1, source_target_pairs={{0,16},{16,0},{1,17},{17,1},{2,18},{18,2},{3,19},{19,3},{4,20},{20... | collective-permute-start | bytes 6291464 | tf_op jit(solution)/shard_map/ppermute | solution.py:773
  301.9 26.3 %collective-permute-start.61 = (bf16[128,1024]{1,0:T(8,128)(2,1)S(1)}, bf16[128,1024]{1,0:T(8,128)(2,1)S(1)}, u32[]{:S(2)}, u32[]{:S(2)}) collective-permute-start(bf16[128,1024]{1,0:T(8,128)(2,1)S(1)} %add_convert_fusion.15), channel_id=1, source_target_pairs={{0,8},{2,10},{4,12},{6,14},{8,0},{10,2},{12,4},{14,6},{16,24},{18,... | collective-permute-start | bytes 786440 | tf_op jit(solution)/shard_map/ppermute | solution.py:779
  304.0 25.7 %collective-permute-start.49 = (bf16[128,1024]{1,0:T(8,128)(2,1)S(1)}, bf16[128,1024]{1,0:T(8,128)(2,1)S(1)}, u32[]{:S(2)}, u32[]{:S(2)}) collective-permute-start(bf16[128,1024]{1,0:T(8,128)(2,1)S(1)} %constant_dynamic-slice_fusion.6), channel_id=1, source_target_pairs={{0,8},{2,10},{4,12},{6,14},{8,0},{10,2},{12,4},{14,6},{16,24},{18,... | collective-permute-start | bytes 786440 | tf_op jit(solution)/shard_map/ppermute | solution.py:779
  308.3 27.5 %collective-permute-start.54 = (bf16[512,1024]{1,0:T(8,128)(2,1)}, bf16[512,1024]{1,0:T(8,128)(2,1)}, u32[]{:S(2)}, u32[]{:S(2)}) collective-permute-start(bf16[512,1024]{1,0:T(8,128)(2,1)} %add_convert_fusion.3), channel_id=1, source_target_pairs={{0,2},{2,0},{4,6},{6,4},{8,10},{10,8},{12,14},{14,12},{16,20},{18,... | collective-permute-start | bytes 3145736 | tf_op jit(solution)/shard_map/ppermute | solution.py:779
  329.1 21.0 %collective-permute-start.62 = (bf16[256,1024]{1,0:T(8,128)(2,1)}, bf16[256,1024]{1,0:T(8,128)(2,1)S(1)}, u32[]{:S(2)}, u32[]{:S(2)}) collective-permute-start(bf16[256,1024]{1,0:T(8,128)(2,1)} %pad_maximum_fusion.13), channel_id=1, source_target_pairs={{0,4},{2,6},{4,0},{6,2},{8,12},{10,14},{12,8},{14,10},{16,18},{18,... | collective-permute-start | bytes 1572872 | tf_op jit(solution)/shard_map/ppermute | solution.py:779
  331.6 20.1 %collective-permute-start.40 = (bf16[256,1024]{1,0:T(8,128)(2,1)}, bf16[256,1024]{1,0:T(8,128)(2,1)}, u32[]{:S(2)}, u32[]{:S(2)}) collective-permute-start(bf16[256,1024]{1,0:T(8,128)(2,1)} %get-tuple-element.317), channel_id=1, source_target_pairs={{0,16},{16,0},{1,17},{17,1},{2,18},{18,2},{3,19},{19,3},{4,20},{20... | collective-permute-start | bytes 1572872 | tf_op jit(solution)/shard_map/ppermute | solution.py:770
  335.6 33.9 %collective-permute-start.42 = (bf16[512,1024]{1,0:T(8,128)(2,1)}, bf16[512,1024]{1,0:T(8,128)(2,1)}, u32[]{:S(2)}, u32[]{:S(2)}) collective-permute-start(bf16[512,1024]{1,0:T(8,128)(2,1)} %add_convert_fusion.2), channel_id=1, source_target_pairs={{0,2},{2,0},{4,6},{6,4},{8,10},{10,8},{12,14},{14,12},{16,20},{18,... | collective-permute-start | bytes 3145736 | tf_op jit(solution)/shard_map/ppermute | solution.py:779
  350.1 56.0 %collective-permute-start.51 = (bf16[256,1024]{1,0:T(8,128)(2,1)S(1)}, bf16[256,1024]{1,0:T(8,128)(2,1)S(1)}, u32[]{:S(2)}, u32[]{:S(2)}) collective-permute-start(bf16[256,1024]{1,0:T(8,128)(2,1)S(1)} %pad_maximum_fusion.11), channel_id=1, source_target_pairs={{0,4},{2,6},{4,0},{6,2},{8,12},{10,14},{12,8},{14,10},{16,18},{18,... | collective-permute-start | bytes 1572872 | tf_op jit(solution)/shard_map/ppermute | solution.py:779
  350.2 56.3 %collective-permute-start.65 = (f32[8,1024]{1,0:T(8,128)S(1)}, f32[8,1024]{1,0:T(8,128)S(1)}, u32[]{:S(2)}, u32[]{:S(2)}) collective-permute-start(f32[8,1024]{1,0:T(8,128)S(1)} %add.173), channel_id=1, source_target_pairs={{0,2},{2,0},{4,6},{6,4},{8,10},{10,8},{12,14},{14,12},{1,3},{3,1},... | collective-permute-start | bytes 98312 | tf_op jit(solution)/shard_map/ppermute | solution.py:779
  372.4 34.1 %collective-permute-start.64 = (bf16[512,1024]{1,0:T(8,128)(2,1)S(1)}, bf16[512,1024]{1,0:T(8,128)(2,1)S(1)}, u32[]{:S(2)}, u32[]{:S(2)}) collective-permute-start(bf16[512,1024]{1,0:T(8,128)(2,1)S(1)} %pad_maximum_fusion.7), channel_id=1, source_target_pairs={{0,2},{2,0},{4,6},{6,4},{8,10},{10,8},{12,14},{14,12},{16,20},{18,... | collective-permute-start | bytes 3145736 | tf_op jit(solution)/shard_map/ppermute | solution.py:779
  372.6 25.0 %collective-permute-start.57 = (bf16[128,1024]{1,0:T(8,128)(2,1)S(1)}, bf16[128,1024]{1,0:T(8,128)(2,1)S(1)}, u32[]{:S(2)}, u32[]{:S(2)}) collective-permute-start(bf16[128,1024]{1,0:T(8,128)(2,1)S(1)} %add_convert_fusion.12), channel_id=1, source_target_pairs={{0,8},{2,10},{4,12},{6,14},{8,0},{10,2},{12,4},{14,6},{16,24},{18,... | collective-permute-start | bytes 786440 | tf_op jit(solution)/shard_map/ppermute | solution.py:779
  386.1 17.1 %collective-permute-start.44 = (bf16[128,1024]{1,0:T(8,128)(2,1)S(1)}, bf16[128,1024]{1,0:T(8,128)(2,1)S(1)}, u32[]{:S(2)}, u32[]{:S(2)}) collective-permute-start(bf16[128,1024]{1,0:T(8,128)(2,1)S(1)} %constant_dynamic-slice_fusion.4), channel_id=1, source_target_pairs={{0,8},{2,10},{4,12},{6,14},{8,0},{10,2},{12,4},{14,6},{16,24},{18,... | collective-permute-start | bytes 786440 | tf_op jit(solution)/shard_map/ppermute | solution.py:779
  397.7 19.9 %collective-permute-start.58 = (bf16[256,1024]{1,0:T(8,128)(2,1)S(1)}, bf16[256,1024]{1,0:T(8,128)(2,1)S(1)}, u32[]{:S(2)}, u32[]{:S(2)}) collective-permute-start(bf16[256,1024]{1,0:T(8,128)(2,1)S(1)} %pad_maximum_fusion.12), channel_id=1, source_target_pairs={{0,4},{2,6},{4,0},{6,2},{8,12},{10,14},{12,8},{14,10},{16,18},{18,... | collective-permute-start | bytes 1572872 | tf_op jit(solution)/shard_map/ppermute | solution.py:779
  406.4 25.6 %collective-permute-start.52 = (bf16[512,1024]{1,0:T(8,128)(2,1)S(1)}, bf16[512,1024]{1,0:T(8,128)(2,1)S(1)}, u32[]{:S(2)}, u32[]{:S(2)}) collective-permute-start(bf16[512,1024]{1,0:T(8,128)(2,1)S(1)} %pad_maximum_fusion.5), channel_id=1, source_target_pairs={{0,2},{2,0},{4,6},{6,4},{8,10},{10,8},{12,14},{14,12},{16,20},{18,... | collective-permute-start | bytes 3145736 | tf_op jit(solution)/shard_map/ppermute | solution.py:779
  417.9 24.9 %collective-permute-start.59 = (bf16[512,1024]{1,0:T(8,128)(2,1)S(1)}, bf16[512,1024]{1,0:T(8,128)(2,1)S(1)}, u32[]{:S(2)}, u32[]{:S(2)}) collective-permute-start(bf16[512,1024]{1,0:T(8,128)(2,1)S(1)} %pad_maximum_fusion.6), channel_id=1, source_target_pairs={{0,2},{2,0},{4,6},{6,4},{8,10},{10,8},{12,14},{14,12},{16,20},{18,... | collective-permute-start | bytes 3145736 | tf_op jit(solution)/shard_map/ppermute | solution.py:779
  430.5 23.2 %collective-permute-start.47 = (bf16[512,1024]{1,0:T(8,128)(2,1)S(1)}, bf16[512,1024]{1,0:T(8,128)(2,1)S(1)}, u32[]{:S(2)}, u32[]{:S(2)}) collective-permute-start(bf16[512,1024]{1,0:T(8,128)(2,1)S(1)} %pad_maximum_fusion.4), channel_id=1, source_target_pairs={{0,2},{2,0},{4,6},{6,4},{8,10},{10,8},{12,14},{14,12},{16,20},{18,... | collective-permute-start | bytes 3145736 | tf_op jit(solution)/shard_map/ppermute | solution.py:779
  430.8 30.6 %collective-permute-start.66 = (bf16[1024,1024]{1,0:T(8,128)(2,1)S(1)}, bf16[1024,1024]{1,0:T(8,128)(2,1)S(1)}, u32[]{:S(2)}, u32[]{:S(2)}) collective-permute-start(bf16[1024,1024]{1,0:T(8,128)(2,1)S(1)} %pad_maximum_fusion.3.own1), channel_id=1, source_target_pairs={{0,16},{1,17},{2,18},{3,19},{4,20},{5,21},{6,22},{7,23},{8,24},{9,... | collective-permute-start | bytes 6291464 | tf_op jit(solution)/shard_map/ppermute | solution.py:779
  434.2 36.9 %collective-permute-start.53 = (bf16[1024,1024]{1,0:T(8,128)(2,1)}, bf16[1024,1024]{1,0:T(8,128)(2,1)}, u32[]{:S(2)}, u32[]{:S(2)}) collective-permute-start(bf16[1024,1024]{1,0:T(8,128)(2,1)} %pad_maximum_fusion.1.own1), channel_id=1, source_target_pairs={{0,16},{1,17},{2,18},{3,19},{4,20},{5,21},{6,22},{7,23},{8,24},{9,... | collective-permute-start | bytes 6291464 | tf_op jit(solution)/shard_map/ppermute | solution.py:779
  444.9 20.9 %collective-permute-start.60 = (bf16[1024,1024]{1,0:T(8,128)(2,1)}, bf16[1024,1024]{1,0:T(8,128)(2,1)}, u32[]{:S(2)}, u32[]{:S(2)}) collective-permute-start(bf16[1024,1024]{1,0:T(8,128)(2,1)} %pad_maximum_fusion.2.own0), channel_id=1, source_target_pairs={{16,0},{17,1},{18,2},{19,3},{20,4},{21,5},{22,6},{23,7},{24,8},{25... | collective-permute-start | bytes 6291464 | tf_op jit(solution)/shard_map/ppermute | solution.py:779
  (58 other events, 705.4 us)

commit v5 on v4

--- a/solution.py
+++ b/solution.py
@@ -985,10 +985,10 @@
     (grads_in, results), _ = lax.optimization_barrier(((grads_in, sums[3].results), g0["du"]))
     sums[3].results = results
     while any(not flow.done for flow in sums + [norm_flow]):
-        for n in (1, 2, 3):
+        for n in (0, 1, 3):
             if not sums[n].done:
                 sums[n].advance()
-        together([sums[0], norm_flow])
+        together([sums[2], norm_flow])
     parts = [flow.value for flow in sums]
     grad_down, grad_up = final_mlp_call(here, [*parts[2], *parts[0]], width)
     grad_out, grad_qkv = final_attention_call(here, [*parts[3], *parts[1]], width)

time: 484 us -> 489 us (1.010)
  the two profiles are of different devices: /device:TPU:5 before, /device:TPU:1 now
where the time goes in v5:
time: 489 us; the launch traced here: 481 us
  Pallas kernels  185 us (38%)
  waiting for transfers between devices  148 us (30%)
  starting transfers between devices  82.1 us (17%)
  other arithmetic  45.9 us (9%)
  local copies, waits for them, and re-layouts  18.5 us (4%)
    pallas_call x12, Pallas kernels, room_call(): pl.pallas_call(whole, in_specs=[pl.BlockSpec(memory_space=pltpu.SMEM)] *...  172 us
    ppermute x42, waiting for transfers between devices, move(): return lambda value: lax.ppermute(value, axis, route)  83.3 us
    ppermute x42, starting transfers between devices, move(): return lambda value: lax.ppermute(value, axis, route)  50.2 us
    ppermute x4, waiting for transfers between devices, around(): lax.ppermute(pair[0], 'dp', ring_up)  42.6 us
    ppermute x6, starting transfers between devices, swap_cores(): return lax.ppermute(value, 'section', swap)  11.1 us
    pallas_call x2, Pallas kernels, final_call(): pl.pallas_call(kernel, in_specs=[pl.BlockSpec(memory_space=pltpu.SMEM)] +...  10.4 us
    ppermute x1, waiting for transfers between devices, swap_tensor(): return lax.ppermute(value, 'tensor', swap)  10.1 us
  transfers between devices with their start and end apart: 69, of which 20 were waited for; matrix products, arithmetic and copies ran while one was open for 12% of the time, Pallas kernels for 32%

profile of v5, /device:TPU:1, one launch (start us, length us, event | category | flops | bytes accessed | tf_op | source)
XLA Modules:
  0.0 481.4 jit_solution(4097459888996598037)
XLA Ops:
  1.4 2.9 cut.1
  4.3 2.7 collective-permute-start
  9.4 10.1 %collective-permute-done = bf16[256,1024]{1,0:T(8,128)(2,1)S(1)} collective-permute-done((bf16[256,1024]{1,0:T(8,128)(2,1)}, bf16[256,1024]{1,0:T(8,128)(2,1)S(1)}, u32[]{:S(2)}, u32[]{:S(2)}) %collective-permute-start) | collective-permute-done | bytes 524320 | tf_op jit(solution)/shard_map/ppermute | solution.py:776
  19.6 6.3 %collective-permute-start.2 = (bf16[256,1024]{1,0:T(8,128)(2,1)S(1)}, bf16[256,1024]{1,0:T(8,128)(2,1)S(1)}, u32[]{:S(2)}, u32[]{:S(2)}) collective-permute-start(bf16[256,1024]{1,0:T(8,128)(2,1)S(1)} %pad_maximum_fusion.9), channel_id=1, source_target_pairs={{0,16},{16,0},{1,17},{17,1},{2,18},{18,2},{3,19},{19,3},{4,20},{20... | collective-permute-start | bytes 1572872 | tf_op jit(solution)/shard_map/ppermute | solution.py:773
  31.3 9.3 %collective-permute-done.6 = bf16[256,1024]{1,0:T(8,128)(2,1)} collective-permute-done((bf16[256,1024]{1,0:T(8,128)(2,1)}, bf16[256,1024]{1,0:T(8,128)(2,1)}, u32[]{:S(2)}, u32[]{:S(2)}) %collective-permute-start.6) | collective-permute-done | bytes 524320 | tf_op jit(solution)/shard_map/ppermute | solution.py:762
  42.6 3.1 maximum_select_fusion.refs_2_.refs_7_
  46.6 3.4 collective-permute-start.22
  49.9 10.0 %first.2 = (bf16[512,1024]{1,0:T(8,128)(2,1)}, bf16[512,1536]{1,0:T(8,128)(2,1)}, bf16[512,512]{1,0:T(8,128)(2,1)}, f32[512,1024]{1,0:T(8,128)}) custom-call(s32[1]{0:T(128)} %bitcast.refs_0_.scalar_ref, s32[2]{0:T(128)} %pad_add_fusion.refs_1_.refs_2_, bf16[512,1024]{1,0:T(8,128)(2,1)} %maximum_select_fusion.refs_2_.refs_7_, s32[512,1]{1,0:T(8,128)} %copy.29.refs_3_, ...), custom_call_target="tpu_custom_call" | custom-call | flops 2415919104 | bytes 10496000 | tf_op jit(solution)/shard_map/first/pallas_call | solution.py:254
  62.1 17.2 %collective-permute-done.10.refs_9_.refs_11_.refs_12_.refs_16_ = bf16[384,1024]{1,0:T(8,128)(2,1)S(1)} collective-permute-done((bf16[384,1024]{1,0:T(8,128)(2,1)}, bf16[384,1024]{1,0:T(8,128)(2,1)S(1)}, u32[]{:S(2)}, u32[]{:S(2)}) %collective-permute-start.10) | collective-permute-done | bytes 786464 | tf_op jit(solution)/shard_map/ppermute | solution.py:809
  84.4 16.3 %collective-permute-done.14.refs_10_.refs_12_.refs_13_.refs_17_ = bf16[384,1024]{1,0:T(8,128)(2,1)S(1)} collective-permute-done((bf16[384,1024]{1,0:T(8,128)(2,1)S(1)}, bf16[384,1024]{1,0:T(8,128)(2,1)S(1)}, u32[]{:S(2)}, u32[]{:S(2)}) %collective-permute-start.14) | collective-permute-done | bytes 786464 | tf_op jit(solution)/shard_map/ppermute | solution.py:809
  106.8 9.0 %collective-permute-done.18.refs_14_.refs_16_.refs_21_.refs_17_ = bf16[192,1024]{1,0:T(8,128)(2,1)S(1)} collective-permute-done((bf16[192,1024]{1,0:T(8,128)(2,1)S(1)}, bf16[192,1024]{1,0:T(8,128)(2,1)S(1)}, u32[]{:S(2)}, u32[]{:S(2)}) %collective-permute-start.18) | collective-permute-done | bytes 393248 | tf_op jit(solution)/shard_map/ppermute | solution.py:809
  123.0 11.7 %second.2 = (bf16[512,1536]{1,0:T(8,128)(2,1)}, f32[512,1024]{1,0:T(8,128)}, bf16[512,1024]{1,0:T(8,128)(2,1)}) custom-call(s32[1]{0:T(128)} %bitcast.refs_0_.scalar_ref, s32[9]{0:T(128)} %pad_add_fusion.1.refs_1_.refs_2_, bf16[512,1024]{1,0:T(8,128)(2,1)} %get-tuple-element.273.refs_2_.refs_6_, s32[512,1]{1,0:T(8,128)} %copy.30.refs_3_, ...), custom_call_target="tpu_custom_call" | custom-call | flops 2415919104 | bytes 12068864 | tf_op jit(solution)/shard_map/second/pallas_call | solution.py:254
  134.9 12.1 %feed.2 = (bf16[512,1024]{1,0:T(8,128)(2,1)}, bf16[512,1024]{1,0:T(8,128)(2,1)}, bf16[512,1024]{1,0:T(8,128)(2,1)}, bf16[512,1024]{1,0:T(8,128)(2,1)}) custom-call(s32[1]{0:T(128)} %bitcast.refs_0_.scalar_ref, s32[2]{0:T(128)} %pad_add_fusion.refs_1_.refs_2_, s32[9]{0:T(128)} %pad_add_fusion.1.refs_1_.refs_2_, ...), custom_call_target="tpu_custom_call" | custom-call | flops 4294967296 | bytes 15728640 | tf_op jit(solution)/shard_map/feed/pallas_call | solution.py:254
  147.0 2.9 collective-permute-start.28
  149.9 3.0 collective-permute-start.29
  156.4 10.3 %first.3 = (bf16[512,1024]{1,0:T(8,128)(2,1)}, bf16[512,1536]{1,0:T(8,128)(2,1)}, bf16[512,512]{1,0:T(8,128)(2,1)}, f32[512,1024]{1,0:T(8,128)}) custom-call(s32[1]{0:T(128)} %bitcast.refs_0_.scalar_ref, s32[2]{0:T(128)} %pad_add_fusion.3.refs_1_.refs_2_, bf16[512,1024]{1,0:T(8,128)(2,1)} %get-tuple-element.246.refs_2_.refs_7_, s32[512,1]{1,0:T(8,128)} %copy.31.refs_3_, ...), custom_call_target="tpu_custom_call" | custom-call | flops 2415919104 | bytes 10496000 | tf_op jit(solution)/shard_map/first/pallas_call | solution.py:254
  167.6 11.7 %second.3 = (bf16[512,1536]{1,0:T(8,128)(2,1)}, f32[512,1024]{1,0:T(8,128)}, bf16[512,1024]{1,0:T(8,128)(2,1)}) custom-call(s32[1]{0:T(128)} %bitcast.refs_0_.scalar_ref, s32[9]{0:T(128)} %pad_add_fusion.1.refs_1_.refs_2_, bf16[512,1024]{1,0:T(8,128)(2,1)} %get-tuple-element.236.refs_2_.refs_6_, s32[512,1]{1,0:T(8,128)} %copy.32.refs_3_, ...), custom_call_target="tpu_custom_call" | custom-call | flops 2415919104 | bytes 12068864 | tf_op jit(solution)/shard_map/second/pallas_call | solution.py:254
  182.1 12.7 %feed.3 = (bf16[512,1024]{1,0:T(8,128)(2,1)}, bf16[512,1024]{1,0:T(8,128)(2,1)}, bf16[512,1024]{1,0:T(8,128)(2,1)}, bf16[512,1024]{1,0:T(8,128)(2,1)}) custom-call(s32[1]{0:T(128)} %bitcast.refs_0_.scalar_ref, s32[2]{0:T(128)} %pad_add_fusion.3.refs_1_.refs_2_, s32[2]{0:T(128)} %pad_add_fusion.3.refs_1_.refs_2_, ...), custom_call_target="tpu_custom_call" | custom-call | flops 4294967296 | bytes 15728640 | tf_op jit(solution)/shard_map/feed/pallas_call | solution.py:254
  196.2 16.1 %feed_back.2 = (bf16[1024,1024]{1,0:T(8,128)(2,1)}, bf16[1024,1024]{1,0:T(8,128)(2,1)}, f32[512,1024]{1,0:T(8,128)}, bf16[512,1024]{1,0:T(8,128)(2,1)}, f32[2,1024]{1,0:T(2,128)}) custom-call(s32[1]{0:T(128)} %bitcast.refs_0_.scalar_ref, s32[2]{0:T(128)} %pad_add_fusion.3.refs_1_.refs_2_, s32[2]{0:T(128)} %pad_add_fusion.3.refs_1_.refs_2_, ...), custom_call_target="tpu_custom_call" | custom-call | flops 6442450944 | bytes 23080960 | tf_op jit(solution)/shard_map/feed_back/pallas_call | solution.py:254
  215.4 16.1 %heads_back.2 = (bf16[1024,1024]{1,0:T(8,128)(2,1)}, bf16[1024,1024]{1,0:T(8,128)(2,1)}, bf16[512,1536]{1,0:T(8,128)(2,1)}) custom-call(s32[1]{0:T(128)} %bitcast.refs_0_.scalar_ref, s32[2]{0:T(128)} %pad_add_fusion.3.refs_1_.refs_2_, bf16[512,1024]{1,0:T(8,128)(2,1)} %get-tuple-element.242.refs_2_.refs_3_, bf16[512,1536]{1,0:T(8,128)(2,1)} %get-tuple-element.233.refs_3_, ...), custom_call_target="tpu_custom_call" | custom-call | flops 4563402752 | bytes 11012096 | tf_op jit(solution)/shard_map/heads_back/pallas_call | solution.py:254
  235.4 18.7 %input_back.2 = (bf16[512,1024]{1,0:T(8,128)(2,1)}, f32[2,1024]{1,0:T(2,128)}) custom-call(s32[1]{0:T(128)} %bitcast.refs_0_.scalar_ref, s32[9]{0:T(128)} %pad_add_fusion.1.refs_1_.refs_2_, s32[2]{0:T(128)} %pad_add_fusion.3.refs_1_.refs_2_, bf16[512,1024]{1,0:T(8,128)(2,1)} %get-tuple-element.242.refs_2_.refs_3_, ...), custom_call_target="tpu_custom_call" | custom-call | flops 5637144576 | bytes 15742976 | tf_op jit(solution)/shard_map/input_back/pallas_call | solution.py:254
  254.2 2.8 add_convert_fusion.5
  257.1 2.2 add_convert_fusion.6
  259.6 18.0 %feed_back.3 = (bf16[1024,1024]{1,0:T(8,128)(2,1)}, bf16[1024,1024]{1,0:T(8,128)(2,1)}, f32[512,1024]{1,0:T(8,128)}, bf16[512,1024]{1,0:T(8,128)(2,1)}, f32[2,1024]{1,0:T(2,128)}) custom-call(s32[1]{0:T(128)} %bitcast.refs_0_.scalar_ref, s32[2]{0:T(128)} %pad_add_fusion.refs_1_.refs_2_, s32[9]{0:T(128)} %pad_add_fusion.1.refs_1_.refs_2_, ...), custom_call_target="tpu_custom_call" | custom-call | flops 6442450944 | bytes 23080960 | tf_op jit(solution)/shard_map/feed_back/pallas_call | solution.py:254
  283.2 2.2 collective-permute-start.37
  286.3 15.9 %heads_back.3 = (bf16[1024,1024]{1,0:T(8,128)(2,1)}, bf16[1024,1024]{1,0:T(8,128)(2,1)}, bf16[512,1536]{1,0:T(8,128)(2,1)}) custom-call(s32[1]{0:T(128)} %bitcast.refs_0_.scalar_ref, s32[2]{0:T(128)} %pad_add_fusion.refs_1_.refs_2_, bf16[512,1024]{1,0:T(8,128)(2,1)} %get-tuple-element.281.refs_2_.refs_3_, bf16[512,1536]{1,0:T(8,128)(2,1)} %get-tuple-element.270.refs_3_, ...), custom_call_target="tpu_custom_call" | custom-call | flops 4563402752 | bytes 11012096 | tf_op jit(solution)/shard_map/heads_back/pallas_call | solution.py:254
  304.4 2.3 collective-permute-start.49
  306.7 2.6 add_convert_fusion.3
  310.9 18.4 %input_back.3 = (bf16[512,1024]{1,0:T(8,128)(2,1)}, f32[2,1024]{1,0:T(2,128)}) custom-call(s32[1]{0:T(128)} %bitcast.refs_0_.scalar_ref, s32[9]{0:T(128)} %pad_add_fusion.1.refs_1_.refs_2_, s32[2]{0:T(128)} %pad_add_fusion.refs_1_.refs_2_, bf16[512,1024]{1,0:T(8,128)(2,1)} %get-tuple-element.281.refs_2_.refs_3_, ...), custom_call_target="tpu_custom_call" | custom-call | flops 5637144576 | bytes 15742976 | tf_op jit(solution)/shard_map/input_back/pallas_call | solution.py:254
  338.0 2.2 add_convert_fusion
  341.5 5.6 %collective-permute-done.50 = bf16[128,1024]{1,0:T(8,128)(2,1)S(1)} collective-permute-done((bf16[128,1024]{1,0:T(8,128)(2,1)S(1)}, bf16[128,1024]{1,0:T(8,128)(2,1)S(1)}, u32[]{:S(2)}, u32[]{:S(2)}) %collective-permute-start.50) | collective-permute-done | bytes 262176 | tf_op jit(solution)/shard_map/ppermute | solution.py:779
  349.8 4.5 collective-permute-done.55
  357.4 14.3 %collective-permute-done.42 = bf16[512,1024]{1,0:T(8,128)(2,1)S(1)} collective-permute-done((bf16[512,1024]{1,0:T(8,128)(2,1)S(1)}, bf16[512,1024]{1,0:T(8,128)(2,1)S(1)}, u32[]{:S(2)}, u32[]{:S(2)}) %collective-permute-start.42) | collective-permute-done | bytes 1048608 | tf_op jit(solution)/shard_map/ppermute | solution.py:779
  374.2 5.1 %collective-permute-start.59 = (bf16[128,1024]{1,0:T(8,128)(2,1)S(1)}, bf16[128,1024]{1,0:T(8,128)(2,1)S(1)}, u32[]{:S(2)}, u32[]{:S(2)}) collective-permute-start(bf16[128,1024]{1,0:T(8,128)(2,1)S(1)} %add_convert_fusion.12), channel_id=1, source_target_pairs={{0,8},{2,10},{4,12},{6,14},{8,0},{10,2},{12,4},{14,6},{16,24},{18,... | collective-permute-start | bytes 786440 | tf_op jit(solution)/shard_map/ppermute | solution.py:779
  379.8 11.4 %collective-permute-done.59 = bf16[128,1024]{1,0:T(8,128)(2,1)S(1)} collective-permute-done((bf16[128,1024]{1,0:T(8,128)(2,1)S(1)}, bf16[128,1024]{1,0:T(8,128)(2,1)S(1)}, u32[]{:S(2)}, u32[]{:S(2)}) %collective-permute-start.59) | collective-permute-done | bytes 262176 | tf_op jit(solution)/shard_map/ppermute | solution.py:779
  393.4 2.9 collective-permute-start.67
  396.3 9.8 %collective-permute-done.44 = bf16[128,1024]{1,0:T(8,128)(2,1)S(1)} collective-permute-done((bf16[128,1024]{1,0:T(8,128)(2,1)S(1)}, bf16[128,1024]{1,0:T(8,128)(2,1)S(1)}, u32[]{:S(2)}, u32[]{:S(2)}) %collective-permute-start.44) | collective-permute-done | bytes 262176 | tf_op jit(solution)/shard_map/ppermute | solution.py:779
  406.3 2.3 collective-permute-start.62
  408.8 12.1 %collective-permute-done.62 = f32[8,1024]{1,0:T(8,128)S(1)} collective-permute-done((f32[8,1024]{1,0:T(8,128)S(1)}, f32[8,1024]{1,0:T(8,128)S(1)}, u32[]{:S(2)}, u32[]{:S(2)}) %collective-permute-start.62) | collective-permute-done | bytes 32800 | tf_op jit(solution)/shard_map/ppermute | solution.py:779
  422.4 3.4 collective-permute-start.63
  428.9 6.5 %collective-permute-done.46 = bf16[256,1024]{1,0:T(8,128)(2,1)S(1)} collective-permute-done((bf16[256,1024]{1,0:T(8,128)(2,1)S(1)}, bf16[256,1024]{1,0:T(8,128)(2,1)S(1)}, u32[]{:S(2)}, u32[]{:S(2)}) %collective-permute-start.46) | collective-permute-done | bytes 524320 | tf_op jit(solution)/shard_map/ppermute | solution.py:779
  435.7 3.9 collective-permute-start.47
  446.2 7.6 %collective-permute-done.63 = bf16[512,1024]{1,0:T(8,128)(2,1)S(1)} collective-permute-done((bf16[512,1024]{1,0:T(8,128)(2,1)S(1)}, bf16[512,1024]{1,0:T(8,128)(2,1)S(1)}, u32[]{:S(2)}, u32[]{:S(2)}) %collective-permute-start.63) | collective-permute-done | bytes 1048608 | tf_op jit(solution)/shard_map/ppermute | solution.py:779
  455.9 2.6 collective-permute-start.64
  458.6 6.5 %collective-permute-done.47 = bf16[512,1024]{1,0:T(8,128)(2,1)S(1)} collective-permute-done((bf16[512,1024]{1,0:T(8,128)(2,1)S(1)}, bf16[512,1024]{1,0:T(8,128)(2,1)S(1)}, u32[]{:S(2)}, u32[]{:S(2)}) %collective-permute-start.47) | collective-permute-done | bytes 1048608 | tf_op jit(solution)/shard_map/ppermute | solution.py:779
  467.2 2.7 collective-permute-start.48
  470.5 5.2 %final_mlp.1 = (f32[1024,1024]{1,0:T(8,128)}, f32[1024,1024]{1,0:T(8,128)}) custom-call(s32[1]{0:T(128)} %bitcast.refs_0_.scalar_ref, bf16[1024,1024]{1,0:T(8,128)(2,1)} %pad_maximum_fusion.2.own0, bf16[1024,1024]{1,0:T(8,128)(2,1)} %collective-permute-done.64.far0, bf16[1024,1024]{1,0:T(8,128)(2,1)} %copy-done.14, ...), custom_call_target="tpu_custom_call" | custom-call | bytes 12582912 | tf_op jit(solution)/shard_map/final_mlp/pallas_call | solution.py:687
  475.8 5.2 %final_attention.1 = (f32[512,1024]{1,0:T(8,128)}, f32[3,1024,512]{2,1,0:T(8,128)}) custom-call(s32[1]{0:T(128)} %bitcast.refs_0_.scalar_ref, bf16[1024,1024]{1,0:T(8,128)(2,1)} %pad_maximum_fusion.own0, bf16[1024,1024]{1,0:T(8,128)(2,1)} %collective-permute-done.48.far0, bf16[1024,1024]{1,0:T(8,128)(2,1)} %pad_maximum_fusion.1.own1, ...), custom_call_target="tpu_custom_call" | custom-call | bytes 12582912 | tf_op jit(solution)/shard_map/final_attention/pallas_call | solution.py:687
  (264 shorter events, 95.5 us)
Async XLA Ops:
  0.6 49.3 %collective-permute-start.8 = (bf16[3,1024,512]{2,1,0:T(8,128)(2,1)}, bf16[3,1024,512]{2,1,0:T(8,128)(2,1)}, u32[]{:S(2)}, u32[]{:S(2)}) collective-permute-start(bf16[3,1024,512]{2,1,0:T(8,128)(2,1)} %bitcast.33), channel_id=1, source_target_pairs={{0,16},{16,0},{1,17},{17,1},{2,18},{18,2},{3,19},{19,3},{4,20},{20... | collective-permute-start | bytes 9437192 | tf_op jit(solution)/shard_map/ppermute | solution.py:770
  7.8 38.8 %collective-permute-start.9 = (bf16[512,1024]{1,0:T(8,128)(2,1)}, bf16[512,1024]{1,0:T(8,128)(2,1)}, u32[]{:S(2)}, u32[]{:S(2)}) collective-permute-start(bf16[512,1024]{1,0:T(8,128)(2,1)} %bitcast.4.out.refs_7_), channel_id=1, source_target_pairs={{0,16},{16,0},{1,17},{17,1},{2,18},{18,2},{3,19},{19,3},{4,20},{20... | collective-permute-start | bytes 3145736 | tf_op jit(solution)/shard_map/ppermute | solution.py:770
  29.8 30.2 %collective-permute-start.3 = (bf16[384,1024]{1,0:T(8,128)(2,1)S(1)}, bf16[384,1024]{1,0:T(8,128)(2,1)}, u32[]{:S(2)}, u32[]{:S(2)}) collective-permute-start(bf16[384,1024]{1,0:T(8,128)(2,1)S(1)} %pad_maximum_fusion.8.refs_7_.refs_9_.refs_10_.refs_14_), channel_id=1, source_target_pairs={{0,4},{4,8},{8,12},{12,14},{14,10},{10,6},{6,2},{2,0},{1,5},{5,9},... | collective-permute-start | bytes 2359304 | tf_op jit(solution)/shard_map/ppermute | solution.py:809
  31.1 28.9 %collective-permute-start.4 = (bf16[384,1024]{1,0:T(8,128)(2,1)S(1)}, bf16[384,1024]{1,0:T(8,128)(2,1)}, u32[]{:S(2)}, u32[]{:S(2)}) collective-permute-start(bf16[384,1024]{1,0:T(8,128)(2,1)S(1)} %pad_maximum_fusion.8.refs_7_.refs_9_.refs_10_.refs_14_), channel_id=1, source_target_pairs={{4,0},{8,4},{12,8},{14,12},{10,14},{6,10},{2,6},{0,2},{5,1},{9,5},... | collective-permute-start | bytes 2359304 | tf_op jit(solution)/shard_map/ppermute | solution.py:809
  40.6 19.4 %collective-permute-start.5 = (bf16[384,1024]{1,0:T(8,128)(2,1)S(1)}, bf16[384,1024]{1,0:T(8,128)(2,1)}, u32[]{:S(2)}, u32[]{:S(2)}) collective-permute-start(bf16[384,1024]{1,0:T(8,128)(2,1)S(1)} %pad_maximum_fusion.8.refs_7_.refs_9_.refs_10_.refs_14_), channel_id=1, source_target_pairs={{0,16},{16,0},{1,17},{17,1},{2,18},{18,2},{3,19},{19,3},{4,20},{20... | collective-permute-start | bytes 2359304 | tf_op jit(solution)/shard_map/ppermute | solution.py:779
  46.6 59.8 %collective-permute-start.22 = (bf16[1024,1024]{1,0:T(8,128)(2,1)S(1)}, bf16[1024,1024]{1,0:T(8,128)(2,1)}, u32[]{:S(2)}, u32[]{:S(2)}) collective-permute-start(bf16[1024,1024]{1,0:T(8,128)(2,1)S(1)} %bitcast.44), channel_id=1, source_target_pairs={{16,17},{17,16},{18,19},{19,18},{20,21},{21,20},{22,23},{23,22},{2... | collective-permute-start | bytes 6291464 | tf_op jit(solution)/shard_map/ppermute | solution.py:907
  60.0 19.3 %collective-permute-start.10 = (bf16[384,1024]{1,0:T(8,128)(2,1)}, bf16[384,1024]{1,0:T(8,128)(2,1)S(1)}, u32[]{:S(2)}, u32[]{:S(2)}) collective-permute-start(bf16[384,1024]{1,0:T(8,128)(2,1)} %collective-permute-done.3.refs_8_.refs_10_.refs_11_.refs_15_), channel_id=1, source_target_pairs={{0,4},{4,8},{8,12},{12,14},{14,10},{10,6},{6,2},{2,0},{1,5},{5,9},... | collective-permute-start | bytes 2359304 | tf_op jit(solution)/shard_map/ppermute | solution.py:809
  61.4 19.7 %collective-permute-start.11 = (bf16[384,1024]{1,0:T(8,128)(2,1)}, bf16[384,1024]{1,0:T(8,128)(2,1)S(1)}, u32[]{:S(2)}, u32[]{:S(2)}) collective-permute-start(bf16[384,1024]{1,0:T(8,128)(2,1)} %collective-permute-done.4.refs_11_.refs_13_.refs_14_.refs_18_), channel_id=1, source_target_pairs={{4,0},{8,4},{12,8},{14,12},{10,14},{6,10},{2,6},{0,2},{5,1},{9,5},... | collective-permute-start | bytes 2359304 | tf_op jit(solution)/shard_map/ppermute | solution.py:809
  61.5 19.5 %collective-permute-start.12 = (bf16[384,1024]{1,0:T(8,128)(2,1)}, bf16[384,1024]{1,0:T(8,128)(2,1)S(1)}, u32[]{:S(2)}, u32[]{:S(2)}) collective-permute-start(bf16[384,1024]{1,0:T(8,128)(2,1)} %collective-permute-done.3.refs_8_.refs_10_.refs_11_.refs_15_), channel_id=1, source_target_pairs={{0,16},{16,0},{1,17},{17,1},{2,18},{18,2},{3,19},{19,3},{4,20},{20... | collective-permute-start | bytes 2359304 | tf_op jit(solution)/shard_map/ppermute | solution.py:779
  61.5 20.4 %collective-permute-start.13 = (bf16[384,1024]{1,0:T(8,128)(2,1)}, bf16[384,1024]{1,0:T(8,128)(2,1)S(1)}, u32[]{:S(2)}, u32[]{:S(2)}) collective-permute-start(bf16[384,1024]{1,0:T(8,128)(2,1)} %collective-permute-done.4.refs_11_.refs_13_.refs_14_.refs_18_), channel_id=1, source_target_pairs={{0,16},{16,0},{1,17},{17,1},{2,18},{18,2},{3,19},{19,3},{4,20},{20... | collective-permute-start | bytes 2359304 | tf_op jit(solution)/shard_map/ppermute | solution.py:779
  82.0 18.7 %collective-permute-start.14 = (bf16[384,1024]{1,0:T(8,128)(2,1)S(1)}, bf16[384,1024]{1,0:T(8,128)(2,1)S(1)}, u32[]{:S(2)}, u32[]{:S(2)}) collective-permute-start(bf16[384,1024]{1,0:T(8,128)(2,1)S(1)} %collective-permute-done.10.refs_9_.refs_11_.refs_12_.refs_16_), channel_id=1, source_target_pairs={{0,4},{4,8},{8,12},{12,14},{14,10},{10,6},{6,2},{2,0},{1,5},{5,9},... | collective-permute-start | bytes 2359304 | tf_op jit(solution)/shard_map/ppermute | solution.py:809
  83.3 19.3 %collective-permute-start.15 = (bf16[384,1024]{1,0:T(8,128)(2,1)S(1)}, bf16[384,1024]{1,0:T(8,128)(2,1)S(1)}, u32[]{:S(2)}, u32[]{:S(2)}) collective-permute-start(bf16[384,1024]{1,0:T(8,128)(2,1)S(1)} %collective-permute-done.11.refs_12_.refs_14_.refs_15_.refs_19_), channel_id=1, source_target_pairs={{4,0},{8,4},{12,8},{14,12},{10,14},{6,10},{2,6},{0,2},{5,1},{9,5},... | collective-permute-start | bytes 2359304 | tf_op jit(solution)/shard_map/ppermute | solution.py:809
  83.5 20.6 %collective-permute-start.16 = (bf16[384,1024]{1,0:T(8,128)(2,1)S(1)}, bf16[384,1024]{1,0:T(8,128)(2,1)S(1)}, u32[]{:S(2)}, u32[]{:S(2)}) collective-permute-start(bf16[384,1024]{1,0:T(8,128)(2,1)S(1)} %collective-permute-done.10.refs_9_.refs_11_.refs_12_.refs_16_), channel_id=1, source_target_pairs={{0,16},{16,0},{1,17},{17,1},{2,18},{18,2},{3,19},{19,3},{4,20},{20... | collective-permute-start | bytes 2359304 | tf_op jit(solution)/shard_map/ppermute | solution.py:779
  84.4 20.5 %collective-permute-start.17 = (bf16[384,1024]{1,0:T(8,128)(2,1)S(1)}, bf16[384,1024]{1,0:T(8,128)(2,1)}, u32[]{:S(2)}, u32[]{:S(2)}) collective-permute-start(bf16[384,1024]{1,0:T(8,128)(2,1)S(1)} %collective-permute-done.11.refs_12_.refs_14_.refs_15_.refs_19_), channel_id=1, source_target_pairs={{0,16},{16,0},{1,17},{17,1},{2,18},{18,2},{3,19},{19,3},{4,20},{20... | collective-permute-start | bytes 2359304 | tf_op jit(solution)/shard_map/ppermute | solution.py:779
  100.7 34.1 %collective-permute-start.24 = (bf16[1024,1024]{1,0:T(8,128)(2,1)}, bf16[1024,1024]{1,0:T(8,128)(2,1)}, u32[]{:S(2)}, u32[]{:S(2)}) collective-permute-start(bf16[1024,1024]{1,0:T(8,128)(2,1)} %bitcast.47), channel_id=1, source_target_pairs={{16,17},{17,16},{18,19},{19,18},{20,21},{21,20},{22,23},{23,22},{2... | collective-permute-start | bytes 6291464 | tf_op jit(solution)/shard_map/ppermute | solution.py:908
  102.7 32.2 %collective-permute-start.25 = (bf16[1024,1024]{1,0:T(8,128)(2,1)S(1)}, bf16[1024,1024]{1,0:T(8,128)(2,1)}, u32[]{:S(2)}, u32[]{:S(2)}) collective-permute-start(bf16[1024,1024]{1,0:T(8,128)(2,1)S(1)} %bitcast.45), channel_id=1, source_target_pairs={{0,16},{16,0},{1,17},{17,1},{2,18},{18,2},{3,19},{19,3},{4,20},{20... | collective-permute-start | bytes 6291464 | tf_op jit(solution)/shard_map/ppermute | solution.py:770
  104.0 30.8 %collective-permute-start.26 = (bf16[1024,1024]{1,0:T(8,128)(2,1)}, bf16[1024,1024]{1,0:T(8,128)(2,1)}, u32[]{:S(2)}, u32[]{:S(2)}) collective-permute-start(bf16[1024,1024]{1,0:T(8,128)(2,1)} %bitcast.48), channel_id=1, source_target_pairs={{0,16},{16,0},{1,17},{17,1},{2,18},{18,2},{3,19},{19,3},{4,20},{20... | collective-permute-start | bytes 6291464 | tf_op jit(solution)/shard_map/ppermute | solution.py:770
  147.0 33.8 %collective-permute-start.28 = (bf16[1024,1024]{1,0:T(8,128)(2,1)}, bf16[1024,1024]{1,0:T(8,128)(2,1)S(1)}, u32[]{:S(2)}, u32[]{:S(2)}) collective-permute-start(bf16[1024,1024]{1,0:T(8,128)(2,1)} %collective-permute-done.22.refs_9_.refs_15_), channel_id=1, source_target_pairs={{16,0},{17,1},{18,2},{19,3},{20,4},{21,5},{22,6},{23,7},{24,8},{25... | collective-permute-start | bytes 6291464 | tf_op jit(solution)/shard_map/ppermute | solution.py:779
  149.9 30.8 %collective-permute-start.29 = (bf16[1024,1024]{1,0:T(8,128)(2,1)}, bf16[1024,1024]{1,0:T(8,128)(2,1)}, u32[]{:S(2)}, u32[]{:S(2)}) collective-permute-start(bf16[1024,1024]{1,0:T(8,128)(2,1)} %collective-permute-done.24.refs_10_.refs_14_), channel_id=1, source_target_pairs={{16,0},{17,1},{18,2},{19,3},{20,4},{21,5},{22,6},{23,7},{24,8},{25... | collective-permute-start | bytes 6291464 | tf_op jit(solution)/shard_map/ppermute | solution.py:779
  154.6 24.7 %collective-permute-start.31 = (bf16[256,1024]{1,0:T(8,128)(2,1)S(1)}, bf16[256,1024]{1,0:T(8,128)(2,1)S(1)}, u32[]{:S(2)}, u32[]{:S(2)}) collective-permute-start(bf16[256,1024]{1,0:T(8,128)(2,1)S(1)} %dynamic-slice_bitcast_fusion), channel_id=1, source_target_pairs={{0,1},{1,0},{2,3},{3,2},{4,5},{5,4},{6,7},{7,6},{8,9},{9,8},{10,11... | collective-permute-start | bytes 1572872 | tf_op jit(solution)/shard_map/ppermute | solution.py:762
  196.1 17.3 %collective-permute-start.30 = (bf16[256,1024]{1,0:T(8,128)(2,1)S(1)}, bf16[256,1024]{1,0:T(8,128)(2,1)S(1)}, u32[]{:S(2)}, u32[]{:S(2)}) collective-permute-start(bf16[256,1024]{1,0:T(8,128)(2,1)S(1)} %get-tuple-element.323), channel_id=1, source_target_pairs={{0,16},{16,0},{1,17},{17,1},{2,18},{18,2},{3,19},{19,3},{4,20},{20... | collective-permute-start | bytes 1572872 | tf_op jit(solution)/shard_map/ppermute | solution.py:770
  212.2 19.3 %collective-permute-start.32 = (bf16[1024,1024]{1,0:T(8,128)(2,1)}, bf16[1024,1024]{1,0:T(8,128)(2,1)}, u32[]{:S(2)}, u32[]{:S(2)}) collective-permute-start(bf16[1024,1024]{1,0:T(8,128)(2,1)} %get-tuple-element.231), channel_id=1, source_target_pairs={{0,16},{16,0},{1,17},{17,1},{2,18},{18,2},{3,19},{19,3},{4,20},{20... | collective-permute-start | bytes 6291464 | tf_op jit(solution)/shard_map/ppermute | solution.py:773
  231.5 22.7 %collective-permute-start.34 = (bf16[1024,1024]{1,0:T(8,128)(2,1)}, bf16[1024,1024]{1,0:T(8,128)(2,1)}, u32[]{:S(2)}, u32[]{:S(2)}) collective-permute-start(bf16[1024,1024]{1,0:T(8,128)(2,1)} %get-tuple-element.241), channel_id=1, source_target_pairs={{0,16},{16,0},{1,17},{17,1},{2,18},{18,2},{3,19},{19,3},{4,20},{20... | collective-permute-start | bytes 6291464 | tf_op jit(solution)/shard_map/ppermute | solution.py:773
  233.2 23.9 %collective-permute-start.33 = (bf16[512,1024]{1,0:T(8,128)(2,1)S(1)}, bf16[512,1024]{1,0:T(8,128)(2,1)}, u32[]{:S(2)}, u32[]{:S(2)}) collective-permute-start(bf16[512,1024]{1,0:T(8,128)(2,1)S(1)} %add_convert_fusion.7), channel_id=1, source_target_pairs={{0,2},{2,0},{4,6},{6,4},{8,10},{10,8},{12,14},{14,12},{16,20},{18,... | collective-permute-start | bytes 3145736 | tf_op jit(solution)/shard_map/ppermute | solution.py:779
  257.0 23.0 %collective-permute-start.36 = (bf16[512,1024]{1,0:T(8,128)(2,1)}, bf16[512,1024]{1,0:T(8,128)(2,1)S(1)}, u32[]{:S(2)}, u32[]{:S(2)}) collective-permute-start(bf16[512,1024]{1,0:T(8,128)(2,1)} %add_convert_fusion.5), channel_id=1, source_target_pairs={{0,2},{2,0},{4,6},{6,4},{8,10},{10,8},{12,14},{14,12},{16,20},{18,... | collective-permute-start | bytes 3145736 | tf_op jit(solution)/shard_map/ppermute | solution.py:779
  259.3 20.6 %collective-permute-start.35 = (bf16[256,1024]{1,0:T(8,128)(2,1)S(1)}, bf16[256,1024]{1,0:T(8,128)(2,1)S(1)}, u32[]{:S(2)}, u32[]{:S(2)}) collective-permute-start(bf16[256,1024]{1,0:T(8,128)(2,1)S(1)} %constant_dynamic-slice_fusion.9), channel_id=1, source_target_pairs={{0,4},{2,6},{4,0},{6,2},{8,12},{10,14},{12,8},{14,10},{16,18},{18,... | collective-permute-start | bytes 1572872 | tf_op jit(solution)/shard_map/ppermute | solution.py:779
  277.6 29.1 %collective-permute-start.39 = (bf16[1024,1024]{1,0:T(8,128)(2,1)}, bf16[1024,1024]{1,0:T(8,128)(2,1)}, u32[]{:S(2)}, u32[]{:S(2)}) collective-permute-start(bf16[1024,1024]{1,0:T(8,128)(2,1)} %get-tuple-element.268), channel_id=1, source_target_pairs={{0,16},{16,0},{1,17},{17,1},{2,18},{18,2},{3,19},{19,3},{4,20},{20... | collective-permute-start | bytes 6291464 | tf_op jit(solution)/shard_map/ppermute | solution.py:773
  283.0 20.5 %collective-permute-start.38 = (bf16[256,1024]{1,0:T(8,128)(2,1)}, bf16[256,1024]{1,0:T(8,128)(2,1)S(1)}, u32[]{:S(2)}, u32[]{:S(2)}) collective-permute-start(bf16[256,1024]{1,0:T(8,128)(2,1)} %constant_dynamic-slice_fusion.7), channel_id=1, source_target_pairs={{0,4},{2,6},{4,0},{6,2},{8,12},{10,14},{12,8},{14,10},{16,18},{18,... | collective-permute-start | bytes 1572872 | tf_op jit(solution)/shard_map/ppermute | solution.py:779
  283.2 20.0 %collective-permute-start.37 = (bf16[128,1024]{1,0:T(8,128)(2,1)S(1)}, bf16[128,1024]{1,0:T(8,128)(2,1)S(1)}, u32[]{:S(2)}, u32[]{:S(2)}) collective-permute-start(bf16[128,1024]{1,0:T(8,128)(2,1)S(1)} %constant_dynamic-slice_fusion.8), channel_id=1, source_target_pairs={{0,8},{2,10},{4,12},{6,14},{8,0},{10,2},{12,4},{14,6},{16,24},{18,... | collective-permute-start | bytes 786440 | tf_op jit(solution)/shard_map/ppermute | solution.py:779
  302.2 33.9 %collective-permute-start.41 = (bf16[1024,1024]{1,0:T(8,128)(2,1)}, bf16[1024,1024]{1,0:T(8,128)(2,1)}, u32[]{:S(2)}, u32[]{:S(2)}) collective-permute-start(bf16[1024,1024]{1,0:T(8,128)(2,1)} %get-tuple-element.280), channel_id=1, source_target_pairs={{0,16},{16,0},{1,17},{17,1},{2,18},{18,2},{3,19},{19,3},{4,20},{20... | collective-permute-start | bytes 6291464 | tf_op jit(solution)/shard_map/ppermute | solution.py:773
  303.2 30.0 %collective-permute-start.65 = (bf16[128,1024]{1,0:T(8,128)(2,1)S(1)}, bf16[128,1024]{1,0:T(8,128)(2,1)}, u32[]{:S(2)}, u32[]{:S(2)}) collective-permute-start(bf16[128,1024]{1,0:T(8,128)(2,1)S(1)} %add_convert_fusion.15), channel_id=1, source_target_pairs={{0,8},{2,10},{4,12},{6,14},{8,0},{10,2},{12,4},{14,6},{16,24},{18,... | collective-permute-start | bytes 786440 | tf_op jit(solution)/shard_map/ppermute | solution.py:779
  304.4 27.0 %collective-permute-start.49 = (bf16[128,1024]{1,0:T(8,128)(2,1)}, bf16[128,1024]{1,0:T(8,128)(2,1)}, u32[]{:S(2)}, u32[]{:S(2)}) collective-permute-start(bf16[128,1024]{1,0:T(8,128)(2,1)} %constant_dynamic-slice_fusion.6), channel_id=1, source_target_pairs={{0,8},{2,10},{4,12},{6,14},{8,0},{10,2},{12,4},{14,6},{16,24},{18,... | collective-permute-start | bytes 786440 | tf_op jit(solution)/shard_map/ppermute | solution.py:779
  309.3 28.7 %collective-permute-start.54 = (bf16[512,1024]{1,0:T(8,128)(2,1)}, bf16[512,1024]{1,0:T(8,128)(2,1)}, u32[]{:S(2)}, u32[]{:S(2)}) collective-permute-start(bf16[512,1024]{1,0:T(8,128)(2,1)} %add_convert_fusion.3), channel_id=1, source_target_pairs={{0,2},{2,0},{4,6},{6,4},{8,10},{10,8},{12,14},{14,12},{16,20},{18,... | collective-permute-start | bytes 3145736 | tf_op jit(solution)/shard_map/ppermute | solution.py:779
  330.3 19.5 %collective-permute-start.56 = (f32[8,1024]{1,0:T(8,128)S(1)}, f32[8,1024]{1,0:T(8,128)S(1)}, u32[]{:S(2)}, u32[]{:S(2)}) collective-permute-start(f32[8,1024]{1,0:T(8,128)S(1)} %concatenate.107), channel_id=1, source_target_pairs={{0,16},{16,0},{1,17},{17,1},{2,18},{18,2},{3,19},{19,3},{4,20},{20... | collective-permute-start | bytes 98312 | tf_op jit(solution)/shard_map/ppermute | solution.py:773
  337.8 33.9 %collective-permute-start.42 = (bf16[512,1024]{1,0:T(8,128)(2,1)S(1)}, bf16[512,1024]{1,0:T(8,128)(2,1)S(1)}, u32[]{:S(2)}, u32[]{:S(2)}) collective-permute-start(bf16[512,1024]{1,0:T(8,128)(2,1)S(1)} %add_convert_fusion.2), channel_id=1, source_target_pairs={{0,2},{2,0},{4,6},{6,4},{8,10},{10,8},{12,14},{14,12},{16,20},{18,... | collective-permute-start | bytes 3145736 | tf_op jit(solution)/shard_map/ppermute | solution.py:779
  347.1 32.2 %collective-permute-start.66 = (bf16[256,1024]{1,0:T(8,128)(2,1)S(1)}, bf16[256,1024]{1,0:T(8,128)(2,1)S(1)}, u32[]{:S(2)}, u32[]{:S(2)}) collective-permute-start(bf16[256,1024]{1,0:T(8,128)(2,1)S(1)} %pad_maximum_fusion.13), channel_id=1, source_target_pairs={{0,4},{2,6},{4,0},{6,2},{8,12},{10,14},{12,8},{14,10},{16,18},{18,... | collective-permute-start | bytes 1572872 | tf_op jit(solution)/shard_map/ppermute | solution.py:779
  347.7 31.5 %collective-permute-start.51 = (bf16[256,1024]{1,0:T(8,128)(2,1)S(1)}, bf16[256,1024]{1,0:T(8,128)(2,1)S(1)}, u32[]{:S(2)}, u32[]{:S(2)}) collective-permute-start(bf16[256,1024]{1,0:T(8,128)(2,1)S(1)} %pad_maximum_fusion.11), channel_id=1, source_target_pairs={{0,4},{2,6},{4,0},{6,2},{8,12},{10,14},{12,8},{14,10},{16,18},{18,... | collective-permute-start | bytes 1572872 | tf_op jit(solution)/shard_map/ppermute | solution.py:779
  354.3 19.4 %collective-permute-start.58 = (f32[8,1024]{1,0:T(8,128)S(1)}, f32[8,1024]{1,0:T(8,128)S(1)}, u32[]{:S(2)}, u32[]{:S(2)}) collective-permute-start(f32[8,1024]{1,0:T(8,128)S(1)} %add.172), channel_id=1, source_target_pairs={{0,2},{2,0},{4,6},{6,4},{8,10},{10,8},{12,14},{14,12},{1,3},{3,1},... | collective-permute-start | bytes 98312 | tf_op jit(solution)/shard_map/ppermute | solution.py:779
  355.7 18.0 %collective-permute-start.57 = (bf16[128,1024]{1,0:T(8,128)(2,1)S(1)}, bf16[128,1024]{1,0:T(8,128)(2,1)S(1)}, u32[]{:S(2)}, u32[]{:S(2)}) collective-permute-start(bf16[128,1024]{1,0:T(8,128)(2,1)S(1)} %constant_dynamic-slice_fusion.1), channel_id=1, source_target_pairs={{0,8},{2,10},{4,12},{6,14},{8,0},{10,2},{12,4},{14,6},{16,24},{18,... | collective-permute-start | bytes 786440 | tf_op jit(solution)/shard_map/ppermute | solution.py:779
  373.6 17.6 %collective-permute-start.43 = (bf16[256,1024]{1,0:T(8,128)(2,1)S(1)}, bf16[256,1024]{1,0:T(8,128)(2,1)S(1)}, u32[]{:S(2)}, u32[]{:S(2)}) collective-permute-start(bf16[256,1024]{1,0:T(8,128)(2,1)S(1)} %constant_dynamic-slice_fusion.5), channel_id=1, source_target_pairs={{0,4},{2,6},{4,0},{6,2},{8,12},{10,14},{12,8},{14,10},{16,18},{18,... | collective-permute-start | bytes 1572872 | tf_op jit(solution)/shard_map/ppermute | solution.py:779
  374.2 17.0 %collective-permute-start.59 = (bf16[128,1024]{1,0:T(8,128)(2,1)S(1)}, bf16[128,1024]{1,0:T(8,128)(2,1)S(1)}, u32[]{:S(2)}, u32[]{:S(2)}) collective-permute-start(bf16[128,1024]{1,0:T(8,128)(2,1)S(1)} %add_convert_fusion.12), channel_id=1, source_target_pairs={{0,8},{2,10},{4,12},{6,14},{8,0},{10,2},{12,4},{14,6},{16,24},{18,... | collective-permute-start | bytes 786440 | tf_op jit(solution)/shard_map/ppermute | solution.py:779
  392.4 28.5 %collective-permute-start.61 = (bf16[256,1024]{1,0:T(8,128)(2,1)}, bf16[256,1024]{1,0:T(8,128)(2,1)S(1)}, u32[]{:S(2)}, u32[]{:S(2)}) collective-permute-start(bf16[256,1024]{1,0:T(8,128)(2,1)} %pad_maximum_fusion.12), channel_id=1, source_target_pairs={{0,4},{2,6},{4,0},{6,2},{8,12},{10,14},{12,8},{14,10},{16,18},{18,... | collective-permute-start | bytes 1572872 | tf_op jit(solution)/shard_map/ppermute | solution.py:779
  393.4 33.7 %collective-permute-start.67 = (bf16[512,1024]{1,0:T(8,128)(2,1)}, bf16[512,1024]{1,0:T(8,128)(2,1)}, u32[]{:S(2)}, u32[]{:S(2)}) collective-permute-start(bf16[512,1024]{1,0:T(8,128)(2,1)} %pad_maximum_fusion.7), channel_id=1, source_target_pairs={{0,2},{2,0},{4,6},{6,4},{8,10},{10,8},{12,14},{14,12},{16,20},{18,... | collective-permute-start | bytes 3145736 | tf_op jit(solution)/shard_map/ppermute | solution.py:779
  408.7 34.2 %collective-permute-start.52 = (bf16[512,1024]{1,0:T(8,128)(2,1)S(1)}, bf16[512,1024]{1,0:T(8,128)(2,1)S(1)}, u32[]{:S(2)}, u32[]{:S(2)}) collective-permute-start(bf16[512,1024]{1,0:T(8,128)(2,1)S(1)} %pad_maximum_fusion.5), channel_id=1, source_target_pairs={{0,2},{2,0},{4,6},{6,4},{8,10},{10,8},{12,14},{14,12},{16,20},{18,... | collective-permute-start | bytes 3145736 | tf_op jit(solution)/shard_map/ppermute | solution.py:779
  422.4 31.4 %collective-permute-start.63 = (bf16[512,1024]{1,0:T(8,128)(2,1)S(1)}, bf16[512,1024]{1,0:T(8,128)(2,1)S(1)}, u32[]{:S(2)}, u32[]{:S(2)}) collective-permute-start(bf16[512,1024]{1,0:T(8,128)(2,1)S(1)} %pad_maximum_fusion.6), channel_id=1, source_target_pairs={{0,2},{2,0},{4,6},{6,4},{8,10},{10,8},{12,14},{14,12},{16,20},{18,... | collective-permute-start | bytes 3145736 | tf_op jit(solution)/shard_map/ppermute | solution.py:779
  435.7 29.3 %collective-permute-start.47 = (bf16[512,1024]{1,0:T(8,128)(2,1)S(1)}, bf16[512,1024]{1,0:T(8,128)(2,1)S(1)}, u32[]{:S(2)}, u32[]{:S(2)}) collective-permute-start(bf16[512,1024]{1,0:T(8,128)(2,1)S(1)} %pad_maximum_fusion.4), channel_id=1, source_target_pairs={{0,2},{2,0},{4,6},{6,4},{8,10},{10,8},{12,14},{14,12},{16,20},{18,... | collective-permute-start | bytes 3145736 | tf_op jit(solution)/shard_map/ppermute | solution.py:779
  439.9 30.6 %collective-permute-start.68 = (bf16[1024,1024]{1,0:T(8,128)(2,1)S(1)}, bf16[1024,1024]{1,0:T(8,128)(2,1)}, u32[]{:S(2)}, u32[]{:S(2)}) collective-permute-start(bf16[1024,1024]{1,0:T(8,128)(2,1)S(1)} %pad_maximum_fusion.3.own1), channel_id=1, source_target_pairs={{0,16},{1,17},{2,18},{3,19},{4,20},{5,21},{6,22},{7,23},{8,24},{9,... | collective-permute-start | bytes 6291464 | tf_op jit(solution)/shard_map/ppermute | solution.py:779
  444.9 30.8 %collective-permute-start.53 = (bf16[1024,1024]{1,0:T(8,128)(2,1)}, bf16[1024,1024]{1,0:T(8,128)(2,1)}, u32[]{:S(2)}, u32[]{:S(2)}) collective-permute-start(bf16[1024,1024]{1,0:T(8,128)(2,1)} %pad_maximum_fusion.1.own1), channel_id=1, source_target_pairs={{0,16},{1,17},{2,18},{3,19},{4,20},{5,21},{6,22},{7,23},{8,24},{9,... | collective-permute-start | bytes 6291464 | tf_op jit(solution)/shard_map/ppermute | solution.py:779
  (53 other events, 724.8 us)
